TPU v7x, 512 devices: a whole 4x8x8 slice. The times are simulated.
512 devices in a mesh: gx: 32 (over y, z_lo), gy: 4 (over x), gz: 4 (over z_hi, core).
Axes of the slice: x: 4, y: 8, z: 8 (z_hi: 2, z_lo: 4; z = z_hi * 4 + z_lo), core: 2. Of those that a mesh axis runs over, the one named last changes fastest.
Arguments:
- node_feat: float32 [262144, 128], P(('gx', 'gy', 'gz')), may hold values from -6 to 6
- edge_feat: float32 [1048576, 128], P(('gx', 'gy', 'gz')), may hold values from -6 to 6
- node_cot: float32 [262144, 128], P(('gx', 'gy', 'gz')), may hold values from -6 to 6
- edge_cot: float32 [1048576, 128], P(('gx', 'gy', 'gz')), may hold values from -6 to 6
- sender: int32 [1048576], P(('gx', 'gy', 'gz')), may hold values from 0 to 1375, as said below
- receiver: int32 [1048576], P(('gx', 'gy', 'gz')), may hold values from 0 to 511, as said below
- block_count: int32 [8192], P(('gx', 'gy', 'gz')), may hold values from 0 to 128, as said below
- send_rows: int32 [96, 12, 12, 32], P('gx', 'gy', 'gz'), may hold values from 0 to 511, as said below
- edge_in_weight: float32 [384, 128], replicated, may hold values from -0.3125 to 0.3125
- edge_bias: float32 [128], replicated, may hold values from -3 to 3
- edge_out_weight: float32 [128, 128], replicated, may hold values from -0.5 to 0.5
- edge_gain: float32 [128], replicated, may hold values from 0.1 to 1.9
- node_in_weight: float32 [256, 128], replicated, may hold values from -0.375 to 0.375
- node_bias: float32 [128], replicated, may hold values from -3 to 3
- node_out_weight: float32 [128, 128], replicated, may hold values from -0.5 to 0.5
- node_gain: float32 [128], replicated, may hold values from 0.1 to 1.9
Outputs:
- node_grad: float32 [262144, 128], P(('gx', 'gy', 'gz'))
- edge_grad: float32 [1048576, 128], P(('gx', 'gy', 'gz'))
- edge_in_grad: float32 [384, 128], replicated
- edge_bias_grad: float32 [128], replicated
- edge_out_grad: float32 [128, 128], replicated
- edge_gain_grad: float32 [128], replicated
- node_in_grad: float32 [256, 128], replicated
- node_bias_grad: float32 [128], replicated
- node_out_grad: float32 [128, 128], replicated
- node_gain_grad: float32 [128], replicated
Inputs may be any that keep to these rules, and one draw needn't show every extreme that they name: `sender`: A value below 512 is an owned cell; otherwise it is 512 + 32 index(d) + s with s below 32, a halo slot of direction d. It never names direction 13 nor a direction whose neighbour lies outside the device grid. `receiver`: nondecreasing over the edge rows of one device. `block_count`: the nonzero blocks of a device come first; some device has no empty block. `send_rows`: the 32 cells of one list are distinct.
All inputs are finite; a program needn't handle non-finite values.
Results may differ from a plain program's by a relative error of at most 0.000088.
Values sent between devices are 32-bit elements; how exact they have to be, the bound alone decides.
No kernel may reach another device: no remote copies, remote signals or barrier semaphores. Data moves between devices by JAX's collectives and lax.ppermute only.
A program may use at most 64 MiB of HBM per device.

v0:
```python
import math

import jax
import jax.numpy as jnp
from jax import lax
from jax.sharding import PartitionSpec as P

NORM_EPS = 1e-05
HIGHEST = lax.Precision.HIGHEST


def with_halo(value, sides, width):
    for axis, dim in sides:
        peers, length = (lax.axis_size(axis), value.shape[dim])
        up = [(i, (i + 1) % peers) for i in range(peers - 1)]
        down = [(j, i) for i, j in up]
        last = lax.slice_in_dim(value, length - width, length, axis=dim)
        initial = lax.slice_in_dim(value, 0, width, axis=dim)
        before = lax.ppermute(last, axis, up)
        after = lax.ppermute(initial, axis, down)
        value = jnp.concatenate([before, value, after], axis=dim)
    return value


def layer_norm(values, gain):
    average = jnp.mean(values, axis=-1, keepdims=True)
    centred = values - average
    spread_sq = jnp.mean(centred * centred, axis=-1, keepdims=True)
    return centred * lax.rsqrt(spread_sq + NORM_EPS) * gain


def edge_section(
    node_table,
    edge_feat,
    sender,
    receiver,
    valid_mask,
    edge_in_weight,
    edge_bias,
    edge_out_weight,
    edge_gain,
):
    width = edge_feat.shape[1]
    preact = jnp.dot(edge_feat, edge_in_weight[:width], precision=HIGHEST)
    preact = preact + jnp.dot(
        node_table[sender], edge_in_weight[width : 2 * width], precision=HIGHEST
    )
    preact = preact + jnp.dot(node_table[receiver], edge_in_weight[2 * width :], precision=HIGHEST)
    hidden = jax.nn.silu(preact + edge_bias)
    return (
        layer_norm(jnp.dot(hidden, edge_out_weight, precision=HIGHEST), edge_gain)
        * valid_mask[:, None]
    )


def node_section(node_feat, summed, node_in_weight, node_bias, node_out_weight, node_gain):
    width = node_feat.shape[1]
    preact = jnp.dot(node_feat, node_in_weight[:width], precision=HIGHEST) + jnp.dot(
        summed, node_in_weight[width:], precision=HIGHEST
    )
    hidden = jax.nn.silu(preact + node_bias)
    return node_feat + layer_norm(jnp.dot(hidden, node_out_weight, precision=HIGHEST), node_gain)


def outer_directions():
    index = lax.broadcasted_iota(jnp.int32, (27,), 0)
    return (index != 13).astype(jnp.float32).reshape(3, 3, 3, 1, 1)


def share_rows(packets):
    spread = with_halo(packets, (("gx", 0), ("gy", 1), ("gz", 2)), 1)
    return spread[::2, ::2, ::2]


def return_grads(slot_grads):
    spread = with_halo(slot_grads, (("gx", 0), ("gy", 1), ("gz", 2)), 1)
    return spread[::2, ::2, ::2]


def on_device(
    node_feat,
    edge_feat,
    node_cot,
    edge_cot,
    sender,
    receiver,
    block_count,
    send_rows,
    edge_in_weight,
    edge_bias,
    edge_out_weight,
    edge_gain,
    node_in_weight,
    node_bias,
    node_out_weight,
    node_gain,
):
    num_cells, width = node_feat.shape
    edge_rows = edge_feat.shape[0]
    slot_count = send_rows.shape[3]
    total_rows = lax.axis_size("gx") * lax.axis_size("gy") * lax.axis_size("gz") * edge_rows
    grad_scale = 1.0 / math.sqrt(total_rows)
    outer_mask = outer_directions()
    packets = node_feat[send_rows] * outer_mask
    received = share_rows(packets)
    node_table = jnp.concatenate([node_feat, received.reshape(27 * slot_count, width)], axis=0)
    valid_mask = (
        (lax.broadcasted_iota(jnp.int32, (block_count.shape[0], 128), 1) < block_count[:, None])
        .astype(jnp.float32)
        .reshape(edge_rows)
    )

    def edge_part(table_in, feat_in, weight_in, bias_in, weight_out, gain_in):
        return edge_section(
            table_in, feat_in, sender, receiver, valid_mask, weight_in, bias_in, weight_out, gain_in
        )

    message, edge_pull = jax.vjp(
        edge_part, node_table, edge_feat, edge_in_weight, edge_bias, edge_out_weight, edge_gain
    )
    summed = jax.ops.segment_sum(message, receiver, num_segments=num_cells, indices_are_sorted=True)
    _, node_pull = jax.vjp(
        node_section, node_feat, summed, node_in_weight, node_bias, node_out_weight, node_gain
    )
    node_grads = node_pull(node_cot)
    node_weights = (node_grads[2], node_grads[3], node_grads[4], node_grads[5])
    edge_grads = edge_pull(edge_cot + node_grads[1][receiver])
    combined = lax.psum(
        (
            edge_grads[2],
            edge_grads[3],
            edge_grads[4],
            edge_grads[5],
            node_weights[0],
            node_weights[1],
            node_weights[2],
            node_weights[3],
        ),
        ("gx", "gy", "gz"),
    )
    edge_weights = combined[:4]
    node_weights = combined[4:]
    table_grad = edge_grads[0]
    slot_grads = table_grad[num_cells:].reshape(3, 3, 3, slot_count, width) * outer_mask
    returned = return_grads(slot_grads) * outer_mask
    halo_sum = jax.ops.segment_sum(
        returned.reshape(27 * slot_count, width),
        send_rows.reshape(27 * slot_count),
        num_segments=num_cells,
    )
    node_grad = node_grads[0] + table_grad[:num_cells] + halo_sum
    edge_grad = edge_cot + edge_grads[1]
    return (
        node_grad,
        edge_grad,
        edge_weights[0] * grad_scale,
        edge_weights[1] * grad_scale,
        edge_weights[2] * grad_scale,
        edge_weights[3] * grad_scale,
        node_weights[0] * grad_scale,
        node_weights[1] * grad_scale,
        node_weights[2] * grad_scale,
        node_weights[3] * grad_scale,
    )


def solution(mesh):
    return jax.shard_map(
        on_device,
        mesh=mesh,
        in_specs=(
            P(("gx", "gy", "gz"), None),
            P(("gx", "gy", "gz"), None),
            P(("gx", "gy", "gz"), None),
            P(("gx", "gy", "gz"), None),
            P(("gx", "gy", "gz")),
            P(("gx", "gy", "gz")),
            P(("gx", "gy", "gz")),
            P("gx", "gy", "gz", None),
            P(),
            P(),
            P(),
            P(),
            P(),
            P(),
            P(),
            P(),
        ),
        out_specs=(
            P(("gx", "gy", "gz"), None),
            P(("gx", "gy", "gz"), None),
            P(),
            P(),
            P(),
            P(),
            P(),
            P(),
            P(),
            P(),
        ),
        check_vma=False,
    )
```

profile of v0, /device:TPU:1, one launch (start us, length us, event | category | flops | bytes accessed | tf_op | source)
XLA Modules:
  0.0 579.8 jit_solution(10663843925532535357)
XLA Ops:
  8.2 2.8 gather_fusion
  11.2 5.0 collective-permute-start
  16.2 1.3 collective-permute-start.1
  18.3 4.4 collective-permute-done.1
  23.5 4.5 collective-permute-start.2
  28.1 1.3 collective-permute-start.3
  31.5 1.3 copy.34
  32.8 1.9 fusion.47
  37.0 11.4 %collective-permute-start.4 = (f32[5,5,1,32,128]{4,3,2,1,0:T(8,128)S(1)}, f32[5,5,1,32,128]{4,3,2,1,0:T(8,128)S(1)}, u32[]{:S(2)}, u32[]{:S(2)}) collective-permute-start(f32[5,5,1,32,128]{4,3,2,1,0:T(8,128)S(1)} %get-tuple-element.29), channel_id=1, source_target_pairs={{0,1},{1,2},{2,3},{4,5},{5,6},{6,7},{8,9},{9,10},{10,11},{12,13},{... | collective-permute-start | bytes 1228808 | tf_op jit(solution)/shard_map/ppermute | solution.py:19
  48.4 1.9 collective-permute-start.5
  51.0 1.9 fusion.44
  53.3 12.7 %collective-permute-done.5 = f32[5,5,1,32,128]{4,3,2,1,0:T(8,128)S(1)} collective-permute-done((f32[5,5,1,32,128]{4,3,2,1,0:T(8,128)S(1)}, f32[5,5,1,32,128]{4,3,2,1,0:T(8,128)S(1)}, u32[]{:S(2)}, u32[]{:S(2)}) %collective-permute-start.5) | collective-permute-done | bytes 409632 | tf_op jit(solution)/shard_map/ppermute | solution.py:20
  66.0 1.2 pad_maximum_fusion
  67.3 5.5 gather_fusion.1
  72.8 7.6 %gather_fusion.2 = f32[2048,128]{1,0:T(8,128)} fusion(f32[1376,128]{1,0:T(8,128)S(1)} %pad_maximum_fusion.2, s32[2048]{0:T(1024)S(1)} %get-tuple-element.42), kind=kCustom, calls=%fused_computation.2 | custom fusion | bytes 2105344 | tf_op jit(solution)/shard_map/jvp()/gather | solution.py:48
  80.4 2.3 convolution_add_fusion.2
  83.7 1.3 fusion.64
  86.0 1.3 copy.33
  87.3 13.0 %scatter_custom_fusion = f32[512,128]{1,0:T(8,128)S(1)} fusion(s32[2048]{0:T(1024)} %param.21, f32[2048,128]{1,0:T(8,128)} %copy.33, f32[]{:T(128)} %constant.12.clone.1), kind=kCustom, calls=%fused_computation.79 | custom fusion | flops 262144 | bytes 262656 | tf_op jit(solution)/shard_map/scatter-add | solution.py:121
  100.4 1.4 fusion.2
  101.7 1.3 fusion.65
  109.1 8.4 %gather_fusion.3 = f32[2048,128]{1,0:T(8,128)} fusion(f32[512,128]{1,0:T(8,128)S(1)} %fusion.34, s32[2048]{0:T(1024)} %get-tuple-element.41), kind=kCustom, calls=%fused_computation.3 | custom fusion | bytes 2105344 | tf_op jit(solution)/shard_map/gather | solution.py:127
  117.5 2.7 copy.35
  120.2 1.6 multiply_reduce_fusion
  123.1 1.9 fusion.66
  125.0 2.6 fusion.6
  127.6 2.4 fusion.68
  130.1 2.4 fusion.69
  132.5 2.5 convolution_bitcast_fusion
  135.0 2.0 fusion.40
  136.9 2.2 fusion.37
  139.1 12.0 %scatter_custom_fusion.2 = f32[1376,128]{1,0:T(8,128)S(1)} fusion(s32[2048]{0:T(1024)} %get-tuple-element.39, f32[2048,128]{1,0:T(8,128)} %fusion.40, f32[]{:T(128)} %constant.12.clone.1), kind=kCustom, calls=%fused_computation.51 | custom fusion | flops 262144 | bytes 705024 | tf_op jit(solution)/shard_map/transpose(jvp())/scatter-add | solution.py:46
  151.1 13.6 %scatter_custom_fusion.1 = f32[1376,128]{1,0:T(8,128)} fusion(s32[2048]{0:T(1024)} %get-tuple-element.43, f32[2048,128]{1,0:T(8,128)} %fusion.37, f32[]{:T(128)} %constant.12.clone.1), kind=kCustom, calls=%fused_computation.53 | custom fusion | flops 262144 | bytes 705024 | tf_op jit(solution)/shard_map/transpose(jvp())/scatter-add | solution.py:48
  164.7 1.3 add_any.50
  166.1 1.4 fusion.1
  167.5 2.0 convolution_add_fusion
  169.6 1.3 collective-permute-start.6
  170.9 1.3 collective-permute-start.7
  173.6 105.5 %all-reduce.5 = (f32[128]{0:T(128)S(1)}, f32[128]{0:T(128)S(1)}, f32[128]{0:T(128)S(1)}, f32[128]{0:T(128)S(1)}) all-reduce(f32[128]{0:T(128)S(1)} %get-tuple-element.48, f32[128]{0:T(128)S(1)} %get-tuple-element.10, f32[128]{0:T(128)S(1)} %copy-done.43, f32[128]{0:T(128)S(1)} %copy-done.39), channel_id=1, replica_groups=mesh['gx'=32,'gy'=4,'gz'=4] {'gx','gy','gz'}, use_global_device_ids=true, to_apply=%region_14.15 | all-reduce | flops 512 | bytes 4096 | tf_op jit(solution)/shard_map/psum | solution.py:128
  279.7 3.7 collective-permute-start.8
  283.4 1.3 collective-permute-start.9
  285.2 259.1 %all-reduce.9.cloned.1.call-done = (f32[384,128]{1,0:T(8,128)}, f32[128,128]{1,0:T(8,128)}, f32[256,128]{1,0:T(8,128)}, f32[128,128]{1,0:T(8,128)}) async-done(((f32[384,128]{1,0:T(8,128)}, f32[128,128]{1,0:T(8,128)}, f32[256,128]{1,0:T(8,128)}, f32[128,128]{1,0:T(8,128)}), (f32[384,128]{1,0:T(8,128)}, f32[128,128]{1,0:T(8,128)}, f32[256,128]{1,0:T(8,128)}, ...) | async-done | bytes 458768 | tf_op jit(solution)/shard_map/psum | solution.py:128
  544.3 1.6 broadcast_multiply_fusion.3
  546.0 5.2 collective-permute-start.10
  551.2 1.9 collective-permute-start.11
  554.5 1.6 collective-permute-done.10
  556.1 9.7 %collective-permute-done.11 = f32[5,5,1,32,128]{4,3,2,1,0:T(8,128)S(1)} collective-permute-done((f32[5,5,1,32,128]{4,3,2,1,0:T(8,128)S(1)}, f32[5,5,1,32,128]{4,3,2,1,0:T(8,128)S(1)}, u32[]{:S(2)}, u32[]{:S(2)}) %collective-permute-start.11) | collective-permute-done | bytes 409632 | tf_op jit(solution)/shard_map/ppermute | solution.py:20
  566.1 6.2 %scatter_fusion = f32[512,128]{1,0:T(8,128)S(1)} fusion(f32[512,128]{1,0:T(8,128)S(1)} %fusion.1, s32[864]{0:T(1024)S(1)} %copy-done.34, f32[864,128]{1,0:T(8,128)S(1)} %bitcast.37), kind=kCustom, calls=%fused_computation.7 | custom fusion | flops 110592 | bytes 1330560 | tf_op jit(solution)/shard_map/scatter-add | solution.py:146
  (154 shorter events, 22.4 us)
Async XLA Ops:
  7.2 43.8 %copy-start = (f32[2048,128]{1,0:T(8,128)S(1)}, f32[2048,128]{1,0:T(8,128)}, u32[]{:S(2)}) copy-start(f32[2048,128]{1,0:T(8,128)} %param.17) | copy-start | bytes 3145732
  7.2 537.1 %all-reduce.9.cloned.1.call-start = ((), (), s32[]{:S(2)}) async-start(), calls=%async_computation | async-start | bytes 917504 | tf_op jit(solution)/shard_map/psum | solution.py:128
  7.2 3.9 copy-start.25
  8.2 9.3 %copy-start.36 = (s32[2048]{0:T(1024)S(1)}, s32[2048]{0:T(1024)}, u32[]{:S(2)}) copy-start(s32[2048]{0:T(1024)} %param.21) | copy-start | bytes 24580
  11.0 18.4 %copy-start.35 = (s32[2048]{0:T(1024)S(1)}, s32[2048]{0:T(1024)}, u32[]{:S(2)}) copy-start(s32[2048]{0:T(1024)} %param.20) | copy-start | bytes 24580
  11.0 18.9 %copy-start.31 = (s32[3,3,3,32]{3,2,1,0:T(4,128)S(1)}, s32[3,3,3,32]{3,2,1,0:T(4,128)}, u32[]{:S(2)}) copy-start(s32[3,3,3,32]{3,2,1,0:T(4,128)} %param.23) | copy-start | bytes 10372
  11.0 19.6 %copy-start.13 = (f32[512,128]{1,0:T(8,128)S(1)}, f32[512,128]{1,0:T(8,128)}, u32[]{:S(2)}) copy-start(f32[512,128]{1,0:T(8,128)} %param.18) | copy-start | bytes 786436
  11.0 20.4 %copy-start.7 = (f32[2048,128]{1,0:T(8,128)S(1)}, f32[2048,128]{1,0:T(8,128)}, u32[]{:S(2)}) copy-start(f32[2048,128]{1,0:T(8,128)} %param.19) | copy-start | bytes 3145732
  11.2 21.6 %copy-start.1 = (f32[512,128]{1,0:T(8,128)S(1)}, f32[512,128]{1,0:T(8,128)}, u32[]{:S(2)}) copy-start(f32[512,128]{1,0:T(8,128)} %param.16) | copy-start | bytes 786436
  11.2 7.0 %collective-permute-start = (f32[1,3,3,32,128]{4,3,2,1,0:T(8,128)S(1)}, f32[1,3,3,32,128]{4,3,2,1,0:T(8,128)S(1)}, u32[]{:S(2)}, u32[]{:S(2)}) collective-permute-start(f32[1,3,3,32,128]{4,3,2,1,0:T(8,128)S(1)} %get-tuple-element.37), channel_id=1, source_target_pairs={{0,16},{16,32},{32,48},{48,64},{64,80},{80,96},{96,112},{112,128},... | collective-permute-start | bytes 442376 | tf_op jit(solution)/shard_map/ppermute | solution.py:19
  16.2 6.5 %collective-permute-start.1 = (f32[1,3,3,32,128]{4,3,2,1,0:T(8,128)S(1)}, f32[1,3,3,32,128]{4,3,2,1,0:T(8,128)S(1)}, u32[]{:S(2)}, u32[]{:S(2)}) collective-permute-start(f32[1,3,3,32,128]{4,3,2,1,0:T(8,128)S(1)} %get-tuple-element.38), channel_id=1, source_target_pairs={{16,0},{32,16},{48,32},{64,48},{80,64},{96,80},{112,96},{128,112},... | collective-permute-start | bytes 442376 | tf_op jit(solution)/shard_map/ppermute | solution.py:20
  23.5 11.2 %collective-permute-start.2 = (f32[5,1,3,32,128]{4,3,2,1,0:T(8,128)}, f32[5,1,3,32,128]{4,3,2,1,0:T(8,128)}, u32[]{:S(2)}, u32[]{:S(2)}) collective-permute-start(f32[5,1,3,32,128]{4,3,2,1,0:T(8,128)} %get-tuple-element.33), channel_id=1, source_target_pairs={{0,4},{4,8},{8,12},{1,5},{5,9},{9,13},{2,6},{6,10},{10,14},{3,7},{... | collective-permute-start | bytes 737288 | tf_op jit(solution)/shard_map/ppermute | solution.py:19
  28.1 7.8 %collective-permute-start.3 = (f32[5,1,3,32,128]{4,3,2,1,0:T(8,128)}, f32[5,1,3,32,128]{4,3,2,1,0:T(8,128)}, u32[]{:S(2)}, u32[]{:S(2)}) collective-permute-start(f32[5,1,3,32,128]{4,3,2,1,0:T(8,128)} %get-tuple-element.34), channel_id=1, source_target_pairs={{4,0},{8,4},{12,8},{5,1},{9,5},{13,9},{6,2},{10,6},{14,10},{7,3},{... | collective-permute-start | bytes 737288 | tf_op jit(solution)/shard_map/ppermute | solution.py:20
  31.5 18.8 %copy-start.42 = (s32[16]{0:T(128)S(1)}, s32[16]{0:T(128)}, u32[]{:S(2)}) copy-start(s32[16]{0:T(128)} %param.22) | copy-start | bytes 196
  31.5 19.5 %copy-start.16 = (f32[384,128]{1,0:T(8,128)S(1)}, f32[384,128]{1,0:T(8,128)}, u32[]{:S(2)}) copy-start(f32[384,128]{1,0:T(8,128)} %param.24) | copy-start | bytes 589828
  37.0 16.3 %collective-permute-start.4 = (f32[5,5,1,32,128]{4,3,2,1,0:T(8,128)S(1)}, f32[5,5,1,32,128]{4,3,2,1,0:T(8,128)S(1)}, u32[]{:S(2)}, u32[]{:S(2)}) collective-permute-start(f32[5,5,1,32,128]{4,3,2,1,0:T(8,128)S(1)} %get-tuple-element.29), channel_id=1, source_target_pairs={{0,1},{1,2},{2,3},{4,5},{5,6},{6,7},{8,9},{9,10},{10,11},{12,13},{... | collective-permute-start | bytes 1228808 | tf_op jit(solution)/shard_map/ppermute | solution.py:19
  48.4 17.6 %collective-permute-start.5 = (f32[5,5,1,32,128]{4,3,2,1,0:T(8,128)S(1)}, f32[5,5,1,32,128]{4,3,2,1,0:T(8,128)S(1)}, u32[]{:S(2)}, u32[]{:S(2)}) collective-permute-start(f32[5,5,1,32,128]{4,3,2,1,0:T(8,128)S(1)} %get-tuple-element.30), channel_id=1, source_target_pairs={{1,0},{2,1},{3,2},{5,4},{6,5},{7,6},{9,8},{10,9},{11,10},{13,12},{... | collective-permute-start | bytes 1228808 | tf_op jit(solution)/shard_map/ppermute | solution.py:20
  72.8 7.6 %copy-start.3 = (f32[2048,128]{1,0:T(8,128)}, f32[2048,128]{1,0:T(8,128)S(1)}, u32[]{:S(2)}) copy-start(f32[2048,128]{1,0:T(8,128)S(1)} %gather_fusion.1) | copy-start | bytes 3145732
  85.8 14.5 %copy-start.18 = (f32[256,128]{1,0:T(8,128)S(1)}, f32[256,128]{1,0:T(8,128)}, u32[]{:S(2)}) copy-start(f32[256,128]{1,0:T(8,128)} %param.28) | copy-start | bytes 393220
  87.3 15.8 %copy-start.12 = (f32[512,128]{0,1:T(8,128)S(1)}, f32[512,128]{0,1:T(8,128)}, u32[]{:S(2)}) copy-start(f32[512,128]{0,1:T(8,128)} %copy.32) | copy-start | bytes 786436
  87.3 15.8 %copy-start.40 = (f32[128]{0:T(128)S(1)}, f32[128]{0:T(128)}, u32[]{:S(2)}) copy-start(f32[128]{0:T(128)} %param.31) | copy-start | bytes 1540
  100.3 3.5 copy-start.41
  100.4 3.6 copy-start.45
  105.1 4.1 copy-start.10
  117.5 2.7 copy-start.9
  117.5 2.7 copy-start.28
  117.5 2.7 copy-start.38
  130.1 4.9 copy-start.17
  139.1 26.9 %copy-start.11 = (f32[512,128]{1,0:T(8,128)S(1)}, f32[512,128]{1,0:T(8,128)}, u32[]{:S(2)}) copy-start(f32[512,128]{1,0:T(8,128)} %copy-done.10) | copy-start | bytes 786436
  164.7 2.7 copy-start.8
  166.0 3.4 copy-start.26
  167.4 4.8 copy-start.19
  167.5 4.8 copy-start.20
  167.5 5.4 copy-start.21
  167.5 5.4 copy-start.22
  167.5 5.4 copy-start.23
  167.5 6.1 %copy-start.39 = (f32[128]{0:T(128)S(1)}, f32[128]{0:T(128)}, u32[]{:S(2)}) copy-start(f32[128]{0:T(128)} %get-tuple-element.12) | copy-start | bytes 1540
  167.5 6.1 %copy-start.43 = (f32[128]{0:T(128)S(1)}, f32[128]{0:T(128)}, u32[]{:S(2)}) copy-start(f32[128]{0:T(128)} %get-tuple-element.50) | copy-start | bytes 1540
  169.6 110.0 %collective-permute-start.6 = (f32[1,3,3,32,128]{4,3,2,1,0:T(8,128)S(1)}, f32[1,3,3,32,128]{4,3,2,1,0:T(8,128)S(1)}, u32[]{:S(2)}, u32[]{:S(2)}) collective-permute-start(f32[1,3,3,32,128]{4,3,2,1,0:T(8,128)S(1)} %get-tuple-element.35), channel_id=1, source_target_pairs={{0,16},{16,32},{32,48},{48,64},{64,80},{80,96},{96,112},{112,128},... | collective-permute-start | bytes 442376 | tf_op jit(solution)/shard_map/ppermute | solution.py:19
  170.9 108.7 %collective-permute-start.7 = (f32[1,3,3,32,128]{4,3,2,1,0:T(8,128)S(1)}, f32[1,3,3,32,128]{4,3,2,1,0:T(8,128)S(1)}, u32[]{:S(2)}, u32[]{:S(2)}) collective-permute-start(f32[1,3,3,32,128]{4,3,2,1,0:T(8,128)S(1)} %get-tuple-element.36), channel_id=1, source_target_pairs={{16,0},{32,16},{48,32},{64,48},{80,64},{96,80},{112,96},{128,112},... | collective-permute-start | bytes 442376 | tf_op jit(solution)/shard_map/ppermute | solution.py:20
  279.7 266.2 %collective-permute-start.8 = (f32[5,1,3,32,128]{4,3,2,1,0:T(8,128)S(1)}, f32[5,1,3,32,128]{4,3,2,1,0:T(8,128)S(1)}, u32[]{:S(2)}, u32[]{:S(2)}) collective-permute-start(f32[5,1,3,32,128]{4,3,2,1,0:T(8,128)S(1)} %get-tuple-element.31), channel_id=1, source_target_pairs={{0,4},{4,8},{8,12},{1,5},{5,9},{9,13},{2,6},{6,10},{10,14},{3,7},{... | collective-permute-start | bytes 737288 | tf_op jit(solution)/shard_map/ppermute | solution.py:19
  283.4 262.5 %collective-permute-start.9 = (f32[5,1,3,32,128]{4,3,2,1,0:T(8,128)S(1)}, f32[5,1,3,32,128]{4,3,2,1,0:T(8,128)S(1)}, u32[]{:S(2)}, u32[]{:S(2)}) collective-permute-start(f32[5,1,3,32,128]{4,3,2,1,0:T(8,128)S(1)} %get-tuple-element.32), channel_id=1, source_target_pairs={{4,0},{8,4},{12,8},{5,1},{9,5},{13,9},{6,2},{10,6},{14,10},{7,3},{... | collective-permute-start | bytes 737288 | tf_op jit(solution)/shard_map/ppermute | solution.py:20
  544.3 8.8 %copy-start.32 = (f32[128,128]{1,0:T(8,128)S(1)}, f32[128,128]{1,0:T(8,128)}, u32[]{:S(2)}) copy-start(f32[128,128]{1,0:T(8,128)} %get-tuple-element.19) | copy-start | bytes 196612
  544.3 8.8 %copy-start.33 = (f32[128,128]{1,0:T(8,128)S(1)}, f32[128,128]{1,0:T(8,128)}, u32[]{:S(2)}) copy-start(f32[128,128]{1,0:T(8,128)} %get-tuple-element.21) | copy-start | bytes 196612
  544.3 9.5 %copy-start.24 = (f32[384,128]{1,0:T(8,128)S(1)}, f32[384,128]{1,0:T(8,128)}, u32[]{:S(2)}) copy-start(f32[384,128]{1,0:T(8,128)} %get-tuple-element.18) | copy-start | bytes 589828
  546.0 10.1 %collective-permute-start.10 = (f32[5,5,1,32,128]{4,3,2,1,0:T(8,128)S(1)}, f32[5,5,1,32,128]{4,3,2,1,0:T(8,128)S(1)}, u32[]{:S(2)}, u32[]{:S(2)}) collective-permute-start(f32[5,5,1,32,128]{4,3,2,1,0:T(8,128)S(1)} %get-tuple-element.27), channel_id=1, source_target_pairs={{0,1},{1,2},{2,3},{4,5},{5,6},{6,7},{8,9},{9,10},{10,11},{12,13},{... | collective-permute-start | bytes 1228808 | tf_op jit(solution)/shard_map/ppermute | solution.py:19
  551.2 14.6 %collective-permute-start.11 = (f32[5,5,1,32,128]{4,3,2,1,0:T(8,128)S(1)}, f32[5,5,1,32,128]{4,3,2,1,0:T(8,128)S(1)}, u32[]{:S(2)}, u32[]{:S(2)}) collective-permute-start(f32[5,5,1,32,128]{4,3,2,1,0:T(8,128)S(1)} %get-tuple-element.28), channel_id=1, source_target_pairs={{1,0},{2,1},{3,2},{5,4},{6,5},{7,6},{9,8},{10,9},{11,10},{13,12},{... | collective-permute-start | bytes 1228808 | tf_op jit(solution)/shard_map/ppermute | solution.py:20
  554.5 11.6 %copy-start.34 = (s32[864]{0:T(1024)S(1)}, s32[864]{0:T(1024)}, u32[]{:S(2)}) copy-start(s32[864]{0:T(1024)} %reshape.187) | copy-start | bytes 10372
  (13 other events, 21.7 us)
Sparse Core Ops, SparseCore 0:
  279.3 265.0 all-reduce.8
where the time goes:
time: 581 us; the launch traced here: 580 us
  waiting for transfers between devices  289 us (50%)
  blocking collectives  106 us (18%)
  other arithmetic  60.9 us (10%)
  starting transfers between devices  40.2 us (7%)
  matrix products  35.6 us (6%)
  local copies, waits for them, and re-layouts  33.6 us (6%)
  between operations  14.8 us (3%)
    psum x1, waiting for transfers between devices, on_device(): lax.psum((edge_grads[2], edge_grads[3], edge_grads[4], edge_grads[5], nod...  259 us
    psum x1, blocking collectives, on_device(): lax.psum((edge_grads[2], edge_grads[3], edge_grads[4], edge_grads[5], nod...  106 us
    ppermute x6, starting transfers between devices, with_halo(): before = lax.ppermute(last, axis, up)  31.1 us
    ppermute x6, waiting for transfers between devices, with_halo(): after = lax.ppermute(initial, axis, down)  28.1 us
    scatter-add x1, other arithmetic, edge_section(): node_table[receiver]  13.6 us
    scatter-add x1, other arithmetic, on_device(): jax.ops.segment_sum(message, receiver, num_segments=num_cells, indices_ar...  13 us
    scatter-add x1, other arithmetic, edge_section(): node_table[sender]  12 us
  transfers between devices with their start and end apart: 13, of which 8 were waited for; matrix products, arithmetic and copies ran while one was open for 2% of the time, Pallas kernels for 0%

commit v1 on v0

--- a/solution.py
+++ b/solution.py
@@ -9,17 +9,38 @@
 HIGHEST = lax.Precision.HIGHEST
 
 
-def with_halo(value, sides, width):
-    for axis, dim in sides:
-        peers, length = (lax.axis_size(axis), value.shape[dim])
-        up = [(i, (i + 1) % peers) for i in range(peers - 1)]
+AXES = ("y", "zl", "x", "zh", "c")
+SPLIT = (8, 4, 4, 2, 2)
+GX, GY, GZ = (("y", "zl"), ("x",), ("zh", "c"))
+
+
+def exchange(value):
+    for dim, axis in enumerate((GX, GY, GZ)):
+        peers = lax.axis_size(axis)
+        up = [(i, i + 1) for i in range(peers - 1)]
         down = [(j, i) for i, j in up]
-        last = lax.slice_in_dim(value, length - width, length, axis=dim)
-        initial = lax.slice_in_dim(value, 0, width, axis=dim)
-        before = lax.ppermute(last, axis, up)
-        after = lax.ppermute(initial, axis, down)
-        value = jnp.concatenate([before, value, after], axis=dim)
+        low, mid, high = (lax.index_in_dim(value, k, axis=dim) for k in range(3))
+        before = lax.ppermute(high, axis, up)
+        after = lax.ppermute(low, axis, down)
+        value = jnp.concatenate([before, mid, after], axis=dim)
     return value
+
+
+def sum_all(rows):
+    side = lax.axis_index("c")
+    halves = rows.reshape(2, 512, 128)
+    keep = lax.dynamic_index_in_dim(halves, side, 0, keepdims=False)
+    give = lax.dynamic_index_in_dim(halves, 1 - side, 0, keepdims=False)
+    swap = [(0, 1), (1, 0)]
+    part = keep + lax.ppermute(give, "c", swap)
+    part = lax.all_to_all(part.reshape(16, 32, 128), ("x", "zl"), 0, 0).sum(0)
+    part = lax.all_to_all(jnp.broadcast_to(part, (16, 32, 128)), ("y", "zh"), 0, 0).sum(0)
+    part = lax.all_to_all(jnp.broadcast_to(part, (16, 32, 128)), ("x", "zl"), 0, 0)
+    part = part.reshape(512, 128)
+    other = lax.ppermute(part, "c", swap)
+    low = jnp.where(side == 0, part, other)
+    high = jnp.where(side == 0, other, part)
+    return jnp.concatenate([low, high], axis=0)
 
 
 def layer_norm(values, gain):
@@ -65,16 +86,6 @@
 def outer_directions():
     index = lax.broadcasted_iota(jnp.int32, (27,), 0)
     return (index != 13).astype(jnp.float32).reshape(3, 3, 3, 1, 1)
-
-
-def share_rows(packets):
-    spread = with_halo(packets, (("gx", 0), ("gy", 1), ("gz", 2)), 1)
-    return spread[::2, ::2, ::2]
-
-
-def return_grads(slot_grads):
-    spread = with_halo(slot_grads, (("gx", 0), ("gy", 1), ("gz", 2)), 1)
-    return spread[::2, ::2, ::2]
 
 
 def on_device(
@@ -98,11 +109,11 @@
     num_cells, width = node_feat.shape
     edge_rows = edge_feat.shape[0]
     slot_count = send_rows.shape[3]
-    total_rows = lax.axis_size("gx") * lax.axis_size("gy") * lax.axis_size("gz") * edge_rows
+    total_rows = lax.axis_size(AXES) * edge_rows
     grad_scale = 1.0 / math.sqrt(total_rows)
     outer_mask = outer_directions()
     packets = node_feat[send_rows] * outer_mask
-    received = share_rows(packets)
+    received = exchange(packets)
     node_table = jnp.concatenate([node_feat, received.reshape(27 * slot_count, width)], axis=0)
     valid_mask = (
         (lax.broadcasted_iota(jnp.int32, (block_count.shape[0], 128), 1) < block_count[:, None])
@@ -125,24 +136,19 @@
     node_grads = node_pull(node_cot)
     node_weights = (node_grads[2], node_grads[3], node_grads[4], node_grads[5])
     edge_grads = edge_pull(edge_cot + node_grads[1][receiver])
-    combined = lax.psum(
-        (
-            edge_grads[2],
-            edge_grads[3],
-            edge_grads[4],
-            edge_grads[5],
-            node_weights[0],
-            node_weights[1],
-            node_weights[2],
-            node_weights[3],
-        ),
-        ("gx", "gy", "gz"),
-    )
+    parts = (edge_grads[2], edge_grads[3], edge_grads[4], edge_grads[5]) + node_weights
+    rows = jnp.concatenate([part.reshape(-1, 128) for part in parts])
+    rows = sum_all(jnp.pad(rows, ((0, 1024 - rows.shape[0]), (0, 0))))
+    combined, start = [], 0
+    for part in parts:
+        size = part.size // 128
+        combined.append(rows[start : start + size].reshape(part.shape))
+        start += size
     edge_weights = combined[:4]
     node_weights = combined[4:]
     table_grad = edge_grads[0]
     slot_grads = table_grad[num_cells:].reshape(3, 3, 3, slot_count, width) * outer_mask
-    returned = return_grads(slot_grads) * outer_mask
+    returned = exchange(slot_grads) * outer_mask
     halo_sum = jax.ops.segment_sum(
         returned.reshape(27 * slot_count, width),
         send_rows.reshape(27 * slot_count),
@@ -165,18 +171,19 @@
 
 
 def solution(mesh):
+    fine = jax.sharding.Mesh(mesh.devices.reshape(SPLIT), AXES)
     return jax.shard_map(
         on_device,
-        mesh=mesh,
+        mesh=fine,
         in_specs=(
-            P(("gx", "gy", "gz"), None),
-            P(("gx", "gy", "gz"), None),
-            P(("gx", "gy", "gz"), None),
-            P(("gx", "gy", "gz"), None),
-            P(("gx", "gy", "gz")),
-            P(("gx", "gy", "gz")),
-            P(("gx", "gy", "gz")),
-            P("gx", "gy", "gz", None),
+            P(AXES, None),
+            P(AXES, None),
+            P(AXES, None),
+            P(AXES, None),
+            P(AXES),
+            P(AXES),
+            P(AXES),
+            P(GX, GY, GZ, None),
             P(),
             P(),
             P(),
@@ -187,8 +194,8 @@
             P(),
         ),
         out_specs=(
-            P(("gx", "gy", "gz"), None),
-            P(("gx", "gy", "gz"), None),
+            P(AXES, None),
+            P(AXES, None),
             P(),
             P(),
             P(),

time: 581 us -> 236 us (0.41)
  waiting for transfers between devices: 289 us -> 25.6 us
  blocking collectives: 106 us -> 0 us
  starting transfers between devices: 40.2 us -> 73.3 us
  between operations: 14.8 us -> 1.64 us
  local copies, waits for them, and re-layouts: 33.6 us -> 44.7 us
    psum x1 -> x0, waiting for transfers between devices: 259 us -> none  [on_device(): lax.psum((edge_grads[2], edge_grads[3], edge_grads[4], edge_grads[5], nod...]
    psum x1 -> x0, blocking collectives: 106 us -> none  [on_device(): lax.psum((edge_grads[2], edge_grads[3], edge_grads[4], edge_grads[5], nod...]
    all_to_all x0 -> x3, starting transfers between devices: none -> 24.9 us  [the longest x1 11.5 us: sum_all(): lax.all_to_all(jnp.broadcast_to(part, (16, 32, 128)), ('y', 'zh'), 0, 0)]
    ppermute x12 -> x14, waiting for transfers between devices: 30.1 us -> 20.9 us  [the longest x6 19.8 us: exchange(): after = lax.ppermute(low, axis, down)]
    ppermute x12 -> x14, starting transfers between devices: 40.1 us -> 48.4 us  [the longest x6 34.3 us: exchange(): before = lax.ppermute(high, axis, up)]
    unnamed x98 -> x104, local copies, waits for them, and re-layouts: 4.5 us -> 10.6 us
  transfers between devices with their start and end apart: 13 -> 17, of which waited for: 8 -> 7; matrix products, arithmetic and copies ran while one was open for 2% -> 22% of each run, Pallas kernels for 0% -> 0%
where the time goes in v1:
time: 236 us; the launch traced here: 234 us
  starting transfers between devices  73.3 us (31%)
  other arithmetic  57.6 us (24%)
  local copies, waits for them, and re-layouts  44.7 us (19%)
  matrix products  31.3 us (13%)
  waiting for transfers between devices  25.6 us (11%)
    ppermute x6, starting transfers between devices, exchange(): before = lax.ppermute(high, axis, up)  34.3 us
    ppermute x6, waiting for transfers between devices, exchange(): after = lax.ppermute(low, axis, down)  19.8 us
    scatter-add x1, other arithmetic, on_device(): jax.ops.segment_sum(message, receiver, num_segments=num_cells, indices_ar...  13 us
    scatter-add x1, other arithmetic, edge_section(): node_table[receiver]  12.9 us
    scatter-add x1, other arithmetic, edge_section(): node_table[sender]  12 us
    all_to_all x1, starting transfers between devices, sum_all(): lax.all_to_all(jnp.broadcast_to(part, (16, 32, 128)), ('y', 'zh'), 0, 0)  11.5 us
    unnamed x104, local copies, waits for them, and re-layouts  10.6 us
    gather x2, local copies, waits for them, and re-layouts, on_device(): edge_grads = edge_pull(edge_cot + node_grads[1][receiver])  10.3 us
  transfers between devices with their start and end apart: 17, of which 7 were waited for; matrix products, arithmetic and copies ran while one was open for 22% of the time, Pallas kernels for 0%

profile of v1, /device:TPU:1, one launch (start us, length us, event | category | flops | bytes accessed | tf_op | source)
XLA Modules:
  0.0 234.1 jit_solution(16185861191892111258)
XLA Ops:
  1.6 2.8 %gather_fusion = f32[864,128]{1,0:T(8,128)S(1)} fusion(f32[512,128]{1,0:T(8,128)} %param.16, s32[1024]{0:T(1024)S(1)} %pad_clamp_fusion), kind=kCustom, calls=%fused_computation | custom fusion | bytes 888192 | tf_op jit(solution)/shard_map/gather | solution.py:115
  4.6 5.0 %collective-permute-start = (f32[1,3,3,32,128]{4,3,2,1,0:T(8,128)S(1)}, f32[1,3,3,32,128]{4,3,2,1,0:T(8,128)S(1)}, u32[]{:S(2)}, u32[]{:S(2)}) collective-permute-start(f32[1,3,3,32,128]{4,3,2,1,0:T(8,128)S(1)} %get-tuple-element.36), channel_id=1, source_target_pairs={{0,16},{16,32},{32,48},{48,64},{64,80},{80,96},{96,112},{112,128},... | collective-permute-start | bytes 442376 | tf_op jit(solution)/shard_map/ppermute | solution.py:23
  9.6 1.3 collective-permute-start.1
  12.9 1.3 copy.37
  14.1 1.9 fusion.45
  17.7 3.4 %collective-permute-start.2 = (f32[3,1,3,32,128]{4,3,2,1,0:T(8,128)S(1)}, f32[3,1,3,32,128]{4,3,2,1,0:T(8,128)S(1)}, u32[]{:S(2)}, u32[]{:S(2)}) collective-permute-start(f32[3,1,3,32,128]{4,3,2,1,0:T(8,128)S(1)} %get-tuple-element.33), channel_id=1, source_target_pairs={{0,4},{4,8},{8,12},{1,5},{5,9},{9,13},{2,6},{6,10},{10,14},{3,7},{... | collective-permute-start | bytes 442376 | tf_op jit(solution)/shard_map/ppermute | solution.py:23
  21.1 1.3 collective-permute-start.3
  23.2 3.8 %collective-permute-done.3 = f32[3,1,3,32,128]{4,3,2,1,0:T(8,128)S(1)} collective-permute-done((f32[3,1,3,32,128]{4,3,2,1,0:T(8,128)S(1)}, f32[3,1,3,32,128]{4,3,2,1,0:T(8,128)S(1)}, u32[]{:S(2)}, u32[]{:S(2)}) %collective-permute-start.3) | collective-permute-done | bytes 147488 | tf_op jit(solution)/shard_map/ppermute | solution.py:24
  27.0 12.0 %collective-permute-start.4 = (f32[3,3,1,32,128]{4,3,2,1,0:T(8,128)S(1)}, f32[3,3,1,32,128]{4,3,2,1,0:T(8,128)S(1)}, u32[]{:S(2)}, u32[]{:S(2)}) collective-permute-start(f32[3,3,1,32,128]{4,3,2,1,0:T(8,128)S(1)} %get-tuple-element.30), channel_id=1, source_target_pairs={{0,1},{1,2},{2,3},{4,5},{5,6},{6,7},{8,9},{9,10},{10,11},{12,13},{... | collective-permute-start | bytes 442376 | tf_op jit(solution)/shard_map/ppermute | solution.py:23
  39.0 1.9 collective-permute-start.5
  41.6 8.2 %collective-permute-done.5 = f32[3,3,1,32,128]{4,3,2,1,0:T(8,128)S(1)} collective-permute-done((f32[3,3,1,32,128]{4,3,2,1,0:T(8,128)S(1)}, f32[3,3,1,32,128]{4,3,2,1,0:T(8,128)S(1)}, u32[]{:S(2)}, u32[]{:S(2)}) %collective-permute-start.5) | collective-permute-done | bytes 147488 | tf_op jit(solution)/shard_map/ppermute | solution.py:24
  50.0 7.6 %gather_fusion.2 = f32[2048,128]{1,0:T(8,128)} fusion(f32[1376,128]{1,0:T(8,128)S(1)} %pad_maximum_fusion, s32[2048]{0:T(1024)S(1)} %get-tuple-element.47), kind=kCustom, calls=%fused_computation.2 | custom fusion | bytes 2105344 | tf_op jit(solution)/shard_map/jvp()/gather | solution.py:69
  57.6 5.5 %gather_fusion.1 = f32[2048,128]{1,0:T(8,128)S(1)} fusion(f32[1376,128]{1,0:T(8,128)S(1)} %pad_maximum_fusion, s32[2048]{0:T(1024)S(1)} %get-tuple-element.45), kind=kCustom, calls=%fused_computation.1 | custom fusion | bytes 2105344 | tf_op jit(solution)/shard_map/jvp()/gather | solution.py:67
  63.1 2.6 %convolution_add_fusion.2 = f32[2048,128]{1,0:T(8,128)S(1)} fusion(f32[2048,128]{1,0:T(8,128)} %fusion.45, f32[2048,128]{1,0:T(8,128)S(1)} %gather_fusion.1, f32[384,128]{1,0:T(8,128)S(1)} %copy-done.21), kind=kOutput, calls=%fused_computation.11 | convolution fusion | flops 402915328 | bytes 3211264 | tf_op jit(solution)/shard_map/jvp()/dot_general | solution.py:66
  66.7 1.3 fusion.73
  69.7 1.3 copy.36
  71.0 13.0 %scatter_custom_fusion = f32[512,128]{1,0:T(8,128)S(1)} fusion(s32[2048]{0:T(1024)} %param.21, f32[2048,128]{1,0:T(8,128)} %copy.36, f32[]{:T(128)} %constant.19.clone.1), kind=kCustom, calls=%fused_computation.71 | custom fusion | flops 262144 | bytes 262656 | tf_op jit(solution)/shard_map/scatter-add | solution.py:132
  92.6 7.6 %gather_fusion.3 = f32[2048,128]{1,0:T(8,128)} fusion(f32[512,128]{1,0:T(8,128)S(1)} %fusion.35, s32[2048]{0:T(1024)S(1)} %copy-done.35), kind=kCustom, calls=%fused_computation.3 | custom fusion | bytes 2105344 | tf_op jit(solution)/shard_map/gather | solution.py:138
  100.3 2.7 %copy.38 = f32[2048,128]{0,1:T(8,128)} copy(f32[2048,128]{1,0:T(8,128)} %gather_fusion.3) | data formatting | bytes 2097152 | tf_op jit(solution)/shard_map/gather | solution.py:138
  103.0 1.6 multiply_reduce_fusion
  105.9 2.0 fusion.6
  107.9 1.9 fusion.75
  109.8 1.8 fusion.77
  111.6 1.8 fusion.78
  113.5 1.8 convolution_bitcast_fusion
  115.3 2.0 fusion.41
  120.5 2.1 collective-permute-start.12
  122.7 2.0 fusion.38
  124.6 12.0 %scatter_custom_fusion.2 = f32[1376,128]{1,0:T(8,128)S(1)} fusion(s32[2048]{0:T(1024)} %get-tuple-element.44, f32[2048,128]{1,0:T(8,128)} %fusion.41, f32[]{:T(128)} %constant.19.clone.1), kind=kCustom, calls=%fused_computation.45 | custom fusion | flops 262144 | bytes 705024 | tf_op jit(solution)/shard_map/transpose(jvp())/scatter-add | solution.py:67
  136.6 12.9 %scatter_custom_fusion.1 = f32[1376,128]{1,0:T(8,128)S(1)} fusion(s32[2048]{0:T(1024)} %get-tuple-element.48, f32[2048,128]{1,0:T(8,128)} %fusion.38, f32[]{:T(128)} %constant.19.clone.1), kind=kCustom, calls=%fused_computation.47 | custom fusion | flops 262144 | bytes 705024 | tf_op jit(solution)/shard_map/transpose(jvp())/scatter-add | solution.py:69
  150.9 1.7 bitcast_add_fusion
  152.6 8.8 %all-to-all-start = ((f32[16,32,128]{2,1,0:T(8,128)}), f32[16,32,128]{2,1,0:T(8,128)S(1)}, u32[]{:S(2)}, u32[]{:S(2)}) async-start(f32[16,32,128]{2,1,0:T(8,128)} %bitcast.14), calls=%async_computation | async-start | bytes 524288 | tf_op jit(solution)/shard_map/all_to_all | solution.py:36
  161.4 3.3 %collective-permute-start.6 = (f32[1,3,3,32,128]{4,3,2,1,0:T(8,128)S(1)}, f32[1,3,3,32,128]{4,3,2,1,0:T(8,128)S(1)}, u32[]{:S(2)}, u32[]{:S(2)}) collective-permute-start(f32[1,3,3,32,128]{4,3,2,1,0:T(8,128)S(1)} %get-tuple-element.27), channel_id=1, source_target_pairs={{0,16},{16,32},{32,48},{48,64},{64,80},{80,96},{96,112},{112,128},... | collective-permute-start | bytes 442376 | tf_op jit(solution)/shard_map/ppermute | solution.py:23
  164.7 1.3 collective-permute-start.7
  168.4 3.2 %collective-permute-done.7 = f32[1,3,3,32,128]{4,3,2,1,0:T(8,128)S(1)} collective-permute-done((f32[1,3,3,32,128]{4,3,2,1,0:T(8,128)S(1)}, f32[1,3,3,32,128]{4,3,2,1,0:T(8,128)S(1)}, u32[]{:S(2)}, u32[]{:S(2)}) %collective-permute-start.7) | collective-permute-done | bytes 147488 | tf_op jit(solution)/shard_map/ppermute | solution.py:24
  173.2 11.5 %all-to-all-start.1 = ((f32[16,32,128]{2,1,0:T(8,128)}), f32[16,32,128]{2,1,0:T(8,128)S(1)}, u32[]{:S(2)}, u32[]{:S(2)}) async-start(f32[16,32,128]{2,1,0:T(8,128)} %broadcast_in_dim.51), calls=%async_computation.1 | async-start | bytes 524288 | tf_op jit(solution)/shard_map/all_to_all | solution.py:37
  184.7 1.8 fusion.68
  186.5 3.8 %collective-permute-start.8 = (f32[3,1,3,32,128]{4,3,2,1,0:T(8,128)}, f32[3,1,3,32,128]{4,3,2,1,0:T(8,128)}, u32[]{:S(2)}, u32[]{:S(2)}) collective-permute-start(f32[3,1,3,32,128]{4,3,2,1,0:T(8,128)} %get-tuple-element.24), channel_id=1, source_target_pairs={{0,4},{4,8},{8,12},{1,5},{5,9},{9,13},{2,6},{6,10},{10,14},{3,7},{... | collective-permute-start | bytes 442376 | tf_op jit(solution)/shard_map/ppermute | solution.py:23
  190.3 1.3 collective-permute-start.9
  191.6 2.8 %convolution_add_fusion = f32[2048,128]{1,0:T(8,128)} fusion(f32[2048,128]{1,0:T(8,128)S(1)} %copy-done.8, f32[2048,128]{1,0:T(8,128)S(1)} %get-tuple-element.54, f32[384,128]{1,0:T(8,128)} %param.24), kind=kOutput, calls=%fused_computation.8 | convolution fusion | flops 402915328 | bytes 3211264 | tf_op jit(solution)/shard_map/transpose(jvp())/dot_general | solution.py:65
  194.4 4.6 %all-to-all-done.1 = f32[16,32,128]{2,1,0:T(8,128)S(1)} async-done(((f32[16,32,128]{2,1,0:T(8,128)}), f32[16,32,128]{2,1,0:T(8,128)S(1)}, u32[]{:S(2)}, u32[]{:S(2)}) %all-to-all-start.1) | async-done | bytes 262176 | tf_op jit(solution)/shard_map/all_to_all | solution.py:37
  199.8 4.6 %all-to-all-start.2 = ((f32[16,32,128]{2,1,0:T(8,128)}), f32[16,32,128]{2,1,0:T(8,128)S(1)}, u32[]{:S(2)}, u32[]{:S(2)}) async-start(f32[16,32,128]{2,1,0:T(8,128)} %broadcast_in_dim.52), calls=%async_computation.2 | async-start | bytes 524288 | tf_op jit(solution)/shard_map/all_to_all | solution.py:38
  205.6 6.9 %collective-permute-start.10 = (f32[3,3,1,32,128]{4,3,2,1,0:T(8,128)S(1)}, f32[3,3,1,32,128]{4,3,2,1,0:T(8,128)S(1)}, u32[]{:S(2)}, u32[]{:S(2)}) collective-permute-start(f32[3,3,1,32,128]{4,3,2,1,0:T(8,128)S(1)} %get-tuple-element.21), channel_id=1, source_target_pairs={{0,1},{1,2},{2,3},{4,5},{5,6},{6,7},{8,9},{9,10},{10,11},{12,13},{... | collective-permute-start | bytes 442376 | tf_op jit(solution)/shard_map/ppermute | solution.py:23
  212.5 1.9 collective-permute-start.11
  214.4 1.3 fusion.1
  215.8 3.0 %collective-permute-start.13 = (f32[512,128]{1,0:T(8,128)S(1)}, f32[512,128]{1,0:T(8,128)S(1)}, u32[]{:S(2)}, u32[]{:S(2)}) collective-permute-start(f32[512,128]{1,0:T(8,128)S(1)} %bitcast.61), channel_id=1, source_target_pairs={{0,1},{1,0},{2,3},{3,2},{4,5},{5,4},{6,7},{7,6},{8,9},{9,8},{10,11... | collective-permute-start | bytes 786440 | tf_op jit(solution)/shard_map/ppermute | solution.py:40
  218.8 4.5 %collective-permute-done.11 = f32[3,3,1,32,128]{4,3,2,1,0:T(8,128)S(1)} collective-permute-done((f32[3,3,1,32,128]{4,3,2,1,0:T(8,128)S(1)}, f32[3,3,1,32,128]{4,3,2,1,0:T(8,128)S(1)}, u32[]{:S(2)}, u32[]{:S(2)}) %collective-permute-start.11) | collective-permute-done | bytes 147488 | tf_op jit(solution)/shard_map/ppermute | solution.py:24
  224.7 6.1 %scatter_fusion = f32[512,128]{1,0:T(8,128)S(1)} fusion(f32[512,128]{1,0:T(8,128)S(1)} %fusion.1, s32[864]{0:T(1024)S(1)} %copy-done.36, f32[864,128]{1,0:T(8,128)S(1)} %bitcast_multiply_fusion), kind=kCustom, calls=%fused_computation.7 | custom fusion | flops 110592 | bytes 1330560 | tf_op jit(solution)/shard_map/scatter-add | solution.py:152
  (179 shorter events, 33.5 us)
Async XLA Ops:
  0.6 13.5 %copy-start = (f32[2048,128]{1,0:T(8,128)S(1)}, f32[2048,128]{1,0:T(8,128)}, u32[]{:S(2)}) copy-start(f32[2048,128]{1,0:T(8,128)} %param.17) | copy-start | bytes 3145732
  0.7 3.8 %copy-start.27 = (f32[3,3,3]{2,1,0:T(4,128)}, f32[3,3,3]{2,1,0:T(4,128)S(1)}, u32[]{:S(2)}) copy-start(f32[3,3,3]{2,1,0:T(4,128)S(1)} %fusion.55) | copy-start | bytes 328
  4.4 6.5 %copy-start.23 = (f32[256,128]{1,0:T(8,128)S(1)}, f32[256,128]{1,0:T(8,128)}, u32[]{:S(2)}) copy-start(f32[256,128]{1,0:T(8,128)} %param.28) | copy-start | bytes 393220
  4.4 7.5 %copy-start.16 = (f32[512,128]{1,0:T(8,128)S(1)}, f32[512,128]{1,0:T(8,128)}, u32[]{:S(2)}) copy-start(f32[512,128]{1,0:T(8,128)} %param.18) | copy-start | bytes 786436
  4.6 6.4 %copy-start.1 = (f32[512,128]{1,0:T(8,128)S(1)}, f32[512,128]{1,0:T(8,128)}, u32[]{:S(2)}) copy-start(f32[512,128]{1,0:T(8,128)} %param.16) | copy-start | bytes 786436
  4.6 8.3 %copy-start.7 = (f32[2048,128]{1,0:T(8,128)S(1)}, f32[2048,128]{1,0:T(8,128)}, u32[]{:S(2)}) copy-start(f32[2048,128]{1,0:T(8,128)} %param.19) | copy-start | bytes 3145732
  4.6 12.1 %collective-permute-start = (f32[1,3,3,32,128]{4,3,2,1,0:T(8,128)S(1)}, f32[1,3,3,32,128]{4,3,2,1,0:T(8,128)S(1)}, u32[]{:S(2)}, u32[]{:S(2)}) collective-permute-start(f32[1,3,3,32,128]{4,3,2,1,0:T(8,128)S(1)} %get-tuple-element.36), channel_id=1, source_target_pairs={{0,16},{16,32},{32,48},{48,64},{64,80},{80,96},{96,112},{112,128},... | collective-permute-start | bytes 442376 | tf_op jit(solution)/shard_map/ppermute | solution.py:23
  9.6 7.1 %collective-permute-start.1 = (f32[1,3,3,32,128]{4,3,2,1,0:T(8,128)S(1)}, f32[1,3,3,32,128]{4,3,2,1,0:T(8,128)}, u32[]{:S(2)}, u32[]{:S(2)}) collective-permute-start(f32[1,3,3,32,128]{4,3,2,1,0:T(8,128)S(1)} %get-tuple-element.37), channel_id=1, source_target_pairs={{16,0},{32,16},{48,32},{64,48},{80,64},{96,80},{112,96},{128,112},... | collective-permute-start | bytes 442376 | tf_op jit(solution)/shard_map/ppermute | solution.py:24
  14.1 1.9 copy-start.39
  17.7 4.7 %copy-start.38 = (s32[2048]{0:T(1024)S(1)}, s32[2048]{0:T(1024)}, u32[]{:S(2)}) copy-start(s32[2048]{0:T(1024)} %param.20) | copy-start | bytes 24580
  17.7 5.4 %collective-permute-start.2 = (f32[3,1,3,32,128]{4,3,2,1,0:T(8,128)S(1)}, f32[3,1,3,32,128]{4,3,2,1,0:T(8,128)S(1)}, u32[]{:S(2)}, u32[]{:S(2)}) collective-permute-start(f32[3,1,3,32,128]{4,3,2,1,0:T(8,128)S(1)} %get-tuple-element.33), channel_id=1, source_target_pairs={{0,4},{4,8},{8,12},{1,5},{5,9},{9,13},{2,6},{6,10},{10,14},{3,7},{... | collective-permute-start | bytes 442376 | tf_op jit(solution)/shard_map/ppermute | solution.py:23
  21.1 5.9 %collective-permute-start.3 = (f32[3,1,3,32,128]{4,3,2,1,0:T(8,128)S(1)}, f32[3,1,3,32,128]{4,3,2,1,0:T(8,128)S(1)}, u32[]{:S(2)}, u32[]{:S(2)}) collective-permute-start(f32[3,1,3,32,128]{4,3,2,1,0:T(8,128)S(1)} %get-tuple-element.34), channel_id=1, source_target_pairs={{4,0},{8,4},{12,8},{5,1},{9,5},{13,9},{6,2},{10,6},{14,10},{7,3},{... | collective-permute-start | bytes 442376 | tf_op jit(solution)/shard_map/ppermute | solution.py:24
  27.0 13.9 %copy-start.46 = (s32[16]{0:T(128)S(1)}, s32[16]{0:T(128)}, u32[]{:S(2)}) copy-start(s32[16]{0:T(128)} %param.22) | copy-start | bytes 196
  27.0 14.6 %collective-permute-start.4 = (f32[3,3,1,32,128]{4,3,2,1,0:T(8,128)S(1)}, f32[3,3,1,32,128]{4,3,2,1,0:T(8,128)S(1)}, u32[]{:S(2)}, u32[]{:S(2)}) collective-permute-start(f32[3,3,1,32,128]{4,3,2,1,0:T(8,128)S(1)} %get-tuple-element.30), channel_id=1, source_target_pairs={{0,1},{1,2},{2,3},{4,5},{5,6},{6,7},{8,9},{9,10},{10,11},{12,13},{... | collective-permute-start | bytes 442376 | tf_op jit(solution)/shard_map/ppermute | solution.py:23
  39.0 10.9 %collective-permute-start.5 = (f32[3,3,1,32,128]{4,3,2,1,0:T(8,128)S(1)}, f32[3,3,1,32,128]{4,3,2,1,0:T(8,128)S(1)}, u32[]{:S(2)}, u32[]{:S(2)}) collective-permute-start(f32[3,3,1,32,128]{4,3,2,1,0:T(8,128)S(1)} %get-tuple-element.31), channel_id=1, source_target_pairs={{1,0},{2,1},{3,2},{5,4},{6,5},{7,6},{9,8},{10,9},{11,10},{13,12},{... | collective-permute-start | bytes 442376 | tf_op jit(solution)/shard_map/ppermute | solution.py:24
  63.1 2.6 %copy-start.3 = (f32[2048,128]{1,0:T(8,128)}, f32[2048,128]{1,0:T(8,128)S(1)}, u32[]{:S(2)}) copy-start(f32[2048,128]{1,0:T(8,128)S(1)} %gather_fusion.1) | copy-start | bytes 3145732
  63.1 2.6 %copy-start.5 = (f32[2048,128]{1,0:T(8,128)S(1)}, f32[2048,128]{1,0:T(8,128)}, u32[]{:S(2)}) copy-start(f32[2048,128]{1,0:T(8,128)} %gather_fusion.2) | copy-start | bytes 3145732
  63.1 2.6 %copy-start.47 = (f32[128]{0:T(128)S(1)}, f32[128]{0:T(128)}, u32[]{:S(2)}) copy-start(f32[128]{0:T(128)} %param.25) | copy-start | bytes 1540
  66.7 1.4 copy-start.19
  71.0 13.0 %copy-start.18 = (f32[512,128]{1,0:T(8,128)S(1)}, f32[512,128]{1,0:T(8,128)}, u32[]{:S(2)}) copy-start(f32[512,128]{1,0:T(8,128)} %fusion.48) | copy-start | bytes 786436
  71.0 13.0 %copy-start.45 = (f32[128]{0:T(128)S(1)}, f32[128]{0:T(128)}, u32[]{:S(2)}) copy-start(f32[128]{0:T(128)} %param.29) | copy-start | bytes 1540
  89.5 2.5 %copy-start.10 = (f32[512,128]{1,0:T(8,128)}, f32[512,128]{1,0:T(8,128)S(1)}, u32[]{:S(2)}) copy-start(f32[512,128]{1,0:T(8,128)S(1)} %get-tuple-element.56) | copy-start | bytes 786436
  100.3 2.7 %copy-start.9 = (f32[2048,128]{0,1:T(8,128)S(1)}, f32[2048,128]{0,1:T(8,128)}, u32[]{:S(2)}) copy-start(f32[2048,128]{0,1:T(8,128)} %copy.37) | copy-start | bytes 3145732
  100.3 2.7 %copy-start.30 = (f32[2048]{0:T(1024)S(1)}, f32[2048]{0:T(1024)}, u32[]{:S(2)}) copy-start(f32[2048]{0:T(1024)} %convert_bitcast_fusion) | copy-start | bytes 24580
  100.3 2.7 %copy-start.41 = (f32[128]{0:T(128)S(1)}, f32[128]{0:T(128)}, u32[]{:S(2)}) copy-start(f32[128]{0:T(128)} %param.27) | copy-start | bytes 1540
  103.0 1.7 copy-start.32
  105.9 2.0 copy-start.50
  107.8 1.9 copy-start.6
  109.8 1.8 copy-start.4
  113.5 1.8 copy-start.22
  115.3 2.0 copy-start.25
  115.3 2.0 copy-start.26
  120.5 29.9 %collective-permute-start.12 = (f32[512,128]{1,0:T(8,128)}, f32[512,128]{1,0:T(8,128)}, u32[]{:S(2)}, u32[]{:S(2)}) collective-permute-start(f32[512,128]{1,0:T(8,128)} %dynamic-slice_bitcast_fusion), channel_id=1, source_target_pairs={{0,1},{1,0},{2,3},{3,2},{4,5},{5,4},{6,7},{7,6},{8,9},{9,8},{10,11... | collective-permute-start | bytes 786440 | tf_op jit(solution)/shard_map/ppermute | solution.py:35
  152.6 19.9 %all-to-all-start = ((f32[16,32,128]{2,1,0:T(8,128)}), f32[16,32,128]{2,1,0:T(8,128)S(1)}, u32[]{:S(2)}, u32[]{:S(2)}) async-start(f32[16,32,128]{2,1,0:T(8,128)} %bitcast.14), calls=%async_computation | async-start | bytes 524288 | tf_op jit(solution)/shard_map/all_to_all | solution.py:36
  161.4 4.6 %copy-start.33 = (s32[3,3,3,32]{3,2,1,0:T(4,128)S(1)}, s32[3,3,3,32]{3,2,1,0:T(4,128)}, u32[]{:S(2)}) copy-start(s32[3,3,3,32]{3,2,1,0:T(4,128)} %param.23) | copy-start | bytes 10372
  161.4 7.0 %collective-permute-start.6 = (f32[1,3,3,32,128]{4,3,2,1,0:T(8,128)S(1)}, f32[1,3,3,32,128]{4,3,2,1,0:T(8,128)S(1)}, u32[]{:S(2)}, u32[]{:S(2)}) collective-permute-start(f32[1,3,3,32,128]{4,3,2,1,0:T(8,128)S(1)} %get-tuple-element.27), channel_id=1, source_target_pairs={{0,16},{16,32},{32,48},{48,64},{64,80},{80,96},{96,112},{112,128},... | collective-permute-start | bytes 442376 | tf_op jit(solution)/shard_map/ppermute | solution.py:23
  164.7 6.9 %collective-permute-start.7 = (f32[1,3,3,32,128]{4,3,2,1,0:T(8,128)S(1)}, f32[1,3,3,32,128]{4,3,2,1,0:T(8,128)S(1)}, u32[]{:S(2)}, u32[]{:S(2)}) collective-permute-start(f32[1,3,3,32,128]{4,3,2,1,0:T(8,128)S(1)} %get-tuple-element.28), channel_id=1, source_target_pairs={{16,0},{32,16},{48,32},{64,48},{80,64},{96,80},{112,96},{128,112},... | collective-permute-start | bytes 442376 | tf_op jit(solution)/shard_map/ppermute | solution.py:24
  172.4 19.1 %copy-start.8 = (f32[2048,128]{1,0:T(8,128)S(1)}, f32[2048,128]{1,0:T(8,128)}, u32[]{:S(2)}) copy-start(f32[2048,128]{1,0:T(8,128)} %param.19) | copy-start | bytes 3145732
  173.2 25.8 %all-to-all-start.1 = ((f32[16,32,128]{2,1,0:T(8,128)}), f32[16,32,128]{2,1,0:T(8,128)S(1)}, u32[]{:S(2)}, u32[]{:S(2)}) async-start(f32[16,32,128]{2,1,0:T(8,128)} %broadcast_in_dim.51), calls=%async_computation.1 | async-start | bytes 524288 | tf_op jit(solution)/shard_map/all_to_all | solution.py:37
  186.5 17.9 %collective-permute-start.8 = (f32[3,1,3,32,128]{4,3,2,1,0:T(8,128)}, f32[3,1,3,32,128]{4,3,2,1,0:T(8,128)}, u32[]{:S(2)}, u32[]{:S(2)}) collective-permute-start(f32[3,1,3,32,128]{4,3,2,1,0:T(8,128)} %get-tuple-element.24), channel_id=1, source_target_pairs={{0,4},{4,8},{8,12},{1,5},{5,9},{9,13},{2,6},{6,10},{10,14},{3,7},{... | collective-permute-start | bytes 442376 | tf_op jit(solution)/shard_map/ppermute | solution.py:23
  190.3 14.2 %collective-permute-start.9 = (f32[3,1,3,32,128]{4,3,2,1,0:T(8,128)}, f32[3,1,3,32,128]{4,3,2,1,0:T(8,128)}, u32[]{:S(2)}, u32[]{:S(2)}) collective-permute-start(f32[3,1,3,32,128]{4,3,2,1,0:T(8,128)} %get-tuple-element.25), channel_id=1, source_target_pairs={{4,0},{8,4},{12,8},{5,1},{9,5},{13,9},{6,2},{10,6},{14,10},{7,3},{... | collective-permute-start | bytes 442376 | tf_op jit(solution)/shard_map/ppermute | solution.py:24
  199.8 16.0 %all-to-all-start.2 = ((f32[16,32,128]{2,1,0:T(8,128)}), f32[16,32,128]{2,1,0:T(8,128)S(1)}, u32[]{:S(2)}, u32[]{:S(2)}) async-start(f32[16,32,128]{2,1,0:T(8,128)} %broadcast_in_dim.52), calls=%async_computation.2 | async-start | bytes 524288 | tf_op jit(solution)/shard_map/all_to_all | solution.py:38
  205.5 8.9 %copy-start.11 = (f32[512,128]{1,0:T(8,128)S(1)}, f32[512,128]{1,0:T(8,128)}, u32[]{:S(2)}) copy-start(f32[512,128]{1,0:T(8,128)} %copy-done.10) | copy-start | bytes 786436
  205.5 8.9 %copy-start.17 = (f32[512,128]{1,0:T(8,128)S(1)}, f32[512,128]{1,0:T(8,128)}, u32[]{:S(2)}) copy-start(f32[512,128]{1,0:T(8,128)} %param.18) | copy-start | bytes 786436
  205.5 8.9 %copy-start.24 = (f32[256,128]{1,0:T(8,128)S(1)}, f32[256,128]{1,0:T(8,128)}, u32[]{:S(2)}) copy-start(f32[256,128]{1,0:T(8,128)} %param.28) | copy-start | bytes 393220
  205.6 13.3 %collective-permute-start.10 = (f32[3,3,1,32,128]{4,3,2,1,0:T(8,128)S(1)}, f32[3,3,1,32,128]{4,3,2,1,0:T(8,128)S(1)}, u32[]{:S(2)}, u32[]{:S(2)}) collective-permute-start(f32[3,3,1,32,128]{4,3,2,1,0:T(8,128)S(1)} %get-tuple-element.21), channel_id=1, source_target_pairs={{0,1},{1,2},{2,3},{4,5},{5,6},{6,7},{8,9},{9,10},{10,11},{12,13},{... | collective-permute-start | bytes 442376 | tf_op jit(solution)/shard_map/ppermute | solution.py:23
  212.5 10.9 %collective-permute-start.11 = (f32[3,3,1,32,128]{4,3,2,1,0:T(8,128)S(1)}, f32[3,3,1,32,128]{4,3,2,1,0:T(8,128)S(1)}, u32[]{:S(2)}, u32[]{:S(2)}) collective-permute-start(f32[3,3,1,32,128]{4,3,2,1,0:T(8,128)S(1)} %get-tuple-element.22), channel_id=1, source_target_pairs={{1,0},{2,1},{3,2},{5,4},{6,5},{7,6},{9,8},{10,9},{11,10},{13,12},{... | collective-permute-start | bytes 442376 | tf_op jit(solution)/shard_map/ppermute | solution.py:24
  215.8 15.1 %collective-permute-start.13 = (f32[512,128]{1,0:T(8,128)S(1)}, f32[512,128]{1,0:T(8,128)S(1)}, u32[]{:S(2)}, u32[]{:S(2)}) collective-permute-start(f32[512,128]{1,0:T(8,128)S(1)} %bitcast.61), channel_id=1, source_target_pairs={{0,1},{1,0},{2,3},{3,2},{4,5},{5,4},{6,7},{7,6},{8,9},{9,8},{10,11... | collective-permute-start | bytes 786440 | tf_op jit(solution)/shard_map/ppermute | solution.py:40
  (20 other events, 17.1 us)

commit v2 on v1

v2 whole, which is shorter than its diff:
```python
import functools
import math

import jax
import jax.numpy as jnp
from jax import lax
from jax.experimental import pallas as pl
from jax.experimental.pallas import tpu as pltpu
from jax.sharding import PartitionSpec as P

NORM_EPS = 1e-05
AXES = ("y", "zl", "x", "zh", "c")
SPLIT = (8, 4, 4, 2, 2)
GX, GY, GZ = (("y", "zl"), ("x",), ("zh", "c"))
HID, CELLS, EDGES, SLOT = 128, 512, 2048, 32
SLAB = 9 * SLOT
HALO = 896
BLOCK = 512
F32, BF16 = jnp.float32, jnp.bfloat16
VMEM = pl.BlockSpec(memory_space=pltpu.VMEM)
SMEM = pl.BlockSpec(memory_space=pltpu.SMEM)


def split(value):
    high = value.astype(BF16)
    low = (value - high.astype(F32)).astype(BF16)
    return jnp.concatenate([high, low], axis=1)


def fold(value):
    return value[:, :HID] + value[:, HID:]


def mix(weight):
    high = weight.astype(BF16)
    low = (weight - high.astype(F32)).astype(BF16)
    top = jnp.concatenate([high, low], axis=1)
    bottom = jnp.concatenate([high, jnp.zeros_like(low)], axis=1)
    return jnp.concatenate([top, bottom], axis=0)


def mul(left, right):
    return jnp.dot(left, right, preferred_element_type=F32)


def mul_rows(left, right):
    return lax.dot_general(left, right, (((0,), (0,)), ((), ())), preferred_element_type=F32)


def quad(value):
    top, bottom = value[:HID], value[HID:]
    return fold(top) + fold(bottom)


def centred(weight):
    return weight - jnp.mean(weight, axis=1, keepdims=True)


def silu_parts(preact):
    gate = 1.0 / (1.0 + jnp.exp(-preact))
    hidden = preact * gate
    return hidden, gate + hidden * (1.0 - gate)


def spread_columns(index, out_ref):
    turned = jnp.transpose(index.astype(F32)).astype(jnp.int32)
    for block in range(EDGES // HID):
        column = turned[:, block : block + 1]
        out_ref[block * HID : (block + 1) * HID, :] = jnp.broadcast_to(column, (HID, HID))


def hot_rows(column, width, base=0):
    lane = lax.broadcasted_iota(jnp.int32, column.shape, 1)
    parts = [
        (column == lane + (base + start)).astype(F32).astype(BF16) for start in range(0, width, HID)
    ]
    return jnp.concatenate(parts, axis=1)


def hot_columns(ref, first, height, base=0):
    level = lax.broadcasted_iota(jnp.int32, (height, HID), 0) + base
    parts = []
    for j in range(BLOCK // HID):
        row = ref[pl.ds(first + j, 1), :]
        parts.append((level == row).astype(F32).astype(BF16))
    return jnp.concatenate(parts, axis=1)


def list_rows(lists_ref):
    turned = jnp.transpose(lists_ref[...].astype(F32)).astype(jnp.int32)
    cell = lax.broadcasted_iota(jnp.int32, (SLOT, CELLS), 1)
    parts = []
    for d in range(27):
        hot = (turned[:SLOT, d : d + 1] == cell).astype(F32)
        parts.append((hot if d != 13 else hot * 0.0).astype(BF16))
    return jnp.concatenate(parts, axis=0)


def packet_kernel(node_ref, lists_ref, low_ref, mid_ref, high_ref):
    rows = fold(mul(list_rows(lists_ref), split(node_ref[...])))
    low_ref[...] = rows[:SLAB]
    mid_ref[...] = rows[SLAB : 2 * SLAB]
    high_ref[...] = rows[2 * SLAB :]


def before_kernel(
    node_ref, edge_ref, sender_ref, receiver_ref, weight_ref, bias_ref, out_ref, send_ref, recv_ref
):
    spread_columns(sender_ref[...], send_ref)
    spread_columns(receiver_ref[...], recv_ref)
    own = split(node_ref[...])
    sent = fold(mul(own, mix(weight_ref[HID : 2 * HID, :])))
    got = fold(mul(own, mix(weight_ref[2 * HID :, :])))
    table = jnp.concatenate([split(sent), split(got)], axis=0)
    first = mix(weight_ref[:HID, :])
    bias = bias_ref[...]

    def step(i, carry):
        rows = pl.ds(pl.multiple_of(i * BLOCK, BLOCK), BLOCK)
        hot = jnp.concatenate(
            [hot_rows(send_ref[rows, :], CELLS), hot_rows(recv_ref[rows, :], CELLS)], axis=1
        )
        value = mul(hot, table) + mul(split(edge_ref[rows, :]), first)
        out_ref[rows, :] = fold(value) + bias
        return carry

    lax.fori_loop(0, EDGES // BLOCK, step, 0)


def main_kernel(
    count_ref,
    side_ref,
    pre_ref,
    halo0_ref,
    halo1_ref,
    halo2_ref,
    edge_ref,
    cot_ref,
    sender_ref,
    receiver_ref,
    node_ref,
    node_cot_ref,
    ein_ref,
    eout_ref,
    egain_ref,
    nin_ref,
    nbias_ref,
    nout_ref,
    ngain_ref,
    keep_ref,
    give_ref,
    back0_ref,
    back1_ref,
    back2_ref,
    own_ref,
    got_ref,
    base_ref,
    dpre_ref,
    send_ref,
    recv_ref,
    order_ref,
    hid_ref,
    slope_ref,
    norm_ref,
    inv_ref,
    sum_ref,
    table_ref,
    grads_ref,
    acc_ref,
    row_ref,
    turn_ref,
):
    raw = sender_ref[...]
    slot = raw - CELLS
    direction = slot >> 5
    third = (direction * 43) >> 7
    moved = CELLS + SLAB * (direction - 3 * third) + SLOT * third + (slot & (SLOT - 1))
    order_ref[...] = jnp.where(raw < CELLS, raw, moved)
    spread_columns(order_ref[...], send_ref)
    spread_columns(receiver_ref[...], recv_ref)
    halo = jnp.concatenate([halo0_ref[...], halo1_ref[...], halo2_ref[...]], axis=0)
    halo = jnp.concatenate([halo, jnp.zeros((HALO - 3 * SLAB, HID), F32)], axis=0)
    halo_split = split(halo)
    table_ref[...] = split(fold(mul(halo_split, mix(ein_ref[HID : 2 * HID, :]))))
    out_weight = centred(eout_ref[...])
    out_mix = mix(out_weight)
    turn_ref[...] = mix(jnp.transpose(out_weight))
    gain = egain_ref[...]
    sum_ref[...] = jnp.zeros_like(sum_ref)

    def live(i):
        row = lax.broadcasted_iota(jnp.int32, (HID, HID), 0)
        blocks = BLOCK // HID
        return jnp.concatenate([row < count_ref[i * blocks + j] for j in range(blocks)], axis=0)

    def forward(i, carry):
        rows = pl.ds(pl.multiple_of(i * BLOCK, BLOCK), BLOCK)
        hot = hot_rows(send_ref[rows, :], HALO, CELLS)
        preact = pre_ref[rows, :] + fold(mul(hot, table_ref[...]))
        hidden, slope = silu_parts(preact)
        hidden = split(hidden)
        hid_ref[rows, :] = hidden
        slope_ref[rows, :] = slope
        value = fold(mul(hidden, out_mix))
        inv = lax.rsqrt(jnp.mean(value * value, axis=1, keepdims=True) + NORM_EPS)
        norm = value * inv
        norm_ref[rows, :] = norm
        inv_ref[rows, :] = jnp.broadcast_to(inv, norm.shape)
        message = jnp.where(live(i), norm * gain, 0.0)
        first = i * (BLOCK // HID)
        sum_ref[...] += mul(hot_columns(receiver_ref, first, CELLS), split(message))
        return carry

    lax.fori_loop(0, EDGES // BLOCK, forward, 0)

    node_split = split(node_ref[...])

    @pl.when(count_ref[0] >= 0)
    def _():
        summed = split(fold(sum_ref[...]))
        preact = fold(mul(node_split, mix(nin_ref[:HID, :]))) + fold(mul(summed, mix(nin_ref[HID:, :])))
        hidden, slope = silu_parts(preact + nbias_ref[...])
        hidden = split(hidden)
        node_weight = centred(nout_ref[...])
        value = fold(mul(hidden, mix(node_weight)))
        inv = lax.rsqrt(jnp.mean(value * value, axis=1, keepdims=True) + NORM_EPS)
        norm = value * inv
        cot = node_cot_ref[...]
        dnorm = cot * ngain_ref[...]
        dvalue = split(inv * (dnorm - norm * jnp.mean(dnorm * norm, axis=1, keepdims=True)))
        dpre = fold(mul(dvalue, mix(jnp.transpose(node_weight)))) * slope
        dpre_split = split(dpre)
        grads_ref[1, 0:HID, :] = quad(mul_rows(node_split, dpre_split))
        grads_ref[1, HID : 2 * HID, :] = quad(mul_rows(summed, dpre_split))
        grads_ref[1, 2 * HID : 3 * HID, :] = centred(quad(mul_rows(hidden, dvalue)))
        grads_ref[1, 3 * HID :, :] = jnp.zeros((HID, HID), F32)
        grads_ref[1, 3 * HID + 2 : 3 * HID + 3, :] = jnp.sum(dpre, axis=0, keepdims=True)
        grads_ref[1, 3 * HID + 3 : 3 * HID + 4, :] = jnp.sum(cot * norm, axis=0, keepdims=True)
        base_ref[...] = cot + fold(mul(dpre_split, mix(jnp.transpose(nin_ref[:HID, :]))))
        table_ref[:CELLS, :] = split(fold(mul(dpre_split, mix(jnp.transpose(nin_ref[HID:, :])))))

    sum_ref[...] = jnp.zeros_like(sum_ref)
    row_ref[...] = jnp.zeros_like(row_ref)
    acc_ref[...] = jnp.zeros_like(acc_ref)

    def backward(i, carry):
        rows = pl.ds(pl.multiple_of(i * BLOCK, BLOCK), BLOCK)
        grad = cot_ref[rows, :] + fold(mul(hot_rows(recv_ref[rows, :], CELLS), table_ref[:CELLS, :]))
        grad = jnp.where(live(i), grad, 0.0)
        norm = norm_ref[rows, :]
        dnorm = grad * gain
        dvalue = inv_ref[rows, :] * (dnorm - norm * jnp.mean(dnorm * norm, axis=1, keepdims=True))
        dvalue = split(dvalue)
        dpre = fold(mul(dvalue, turn_ref[...])) * slope_ref[rows, :]
        dpre_ref[rows, :] = dpre
        dpre_split = split(dpre)
        acc_ref[0] += mul_rows(hid_ref[rows, :], dvalue)
        acc_ref[1] += mul_rows(split(edge_ref[rows, :]), dpre_split)
        first = i * (BLOCK // HID)
        sum_ref[...] += mul(hot_columns(receiver_ref, first, CELLS), dpre_split)
        row_ref[...] += mul(hot_columns(order_ref, first, CELLS + HALO), dpre_split)
        bias_grad, gain_grad = carry
        return (
            bias_grad + jnp.sum(dpre, axis=0, keepdims=True),
            gain_grad + jnp.sum(grad * norm, axis=0, keepdims=True),
        )

    zero = jnp.zeros((1, HID), F32)
    bias_grad, gain_grad = lax.fori_loop(0, EDGES // BLOCK, backward, (zero, zero))
    own = fold(row_ref[:CELLS, :])
    back = fold(row_ref[CELLS:, :])
    got = fold(sum_ref[...])
    own_ref[...] = own
    got_ref[...] = got
    back0_ref[...] = back[:SLAB]
    back1_ref[...] = back[SLAB : 2 * SLAB]
    back2_ref[...] = back[2 * SLAB : 3 * SLAB]
    grads_ref[0, 0:HID, :] = quad(acc_ref[1])
    grads_ref[0, HID : 2 * HID, :] = quad(mul_rows(node_split, split(own))) + quad(mul_rows(halo_split, split(back)))
    grads_ref[0, 2 * HID : 3 * HID, :] = quad(mul_rows(node_split, split(got)))
    grads_ref[0, 3 * HID :, :] = centred(quad(acc_ref[0]))
    grads_ref[1, 3 * HID : 3 * HID + 1, :] = bias_grad
    grads_ref[1, 3 * HID + 1 : 3 * HID + 2, :] = gain_grad
    side = side_ref[0]
    keep_ref[...] = grads_ref[side]
    give_ref[...] = grads_ref[1 - side]


def edge_kernel(cot_ref, dpre_ref, base_ref, own_ref, got_ref, weight_ref, edge_ref, part_ref):
    first = mix(jnp.transpose(weight_ref[:HID, :]))

    def step(i, carry):
        rows = pl.ds(pl.multiple_of(i * BLOCK, BLOCK), BLOCK)
        edge_ref[rows, :] = cot_ref[rows, :] + fold(mul(split(dpre_ref[rows, :]), first))
        return carry

    lax.fori_loop(0, EDGES // BLOCK, step, 0)
    second = mix(jnp.transpose(weight_ref[HID : 2 * HID, :]))
    third = mix(jnp.transpose(weight_ref[2 * HID :, :]))
    value = mul(split(own_ref[...]), second) + mul(split(got_ref[...]), third)
    part_ref[...] = base_ref[...] + fold(value)


def node_kernel(lists_ref, low_ref, mid_ref, high_ref, part_ref, weight_ref, out_ref):
    back = jnp.concatenate([low_ref[...], mid_ref[...], high_ref[...]], axis=0)
    summed = fold(mul_rows(list_rows(lists_ref), split(back)))
    turned = mix(jnp.transpose(weight_ref[HID : 2 * HID, :]))
    out_ref[...] = part_ref[...] + fold(mul(split(summed), turned))


def finish_kernel(
    side_ref, part_ref, other_ref, ein_ref, eout_ref, nin_ref, nout_ref, eb, eg, nb, ng, *, scale
):
    mine = side_ref[0] == 0
    part, other = part_ref[...] * scale, other_ref[...] * scale
    low = jnp.where(mine, part, other)
    high = jnp.where(mine, other, part)
    ein_ref[...] = low[: 3 * HID]
    eout_ref[...] = low[3 * HID :]
    nin_ref[...] = high[: 2 * HID]
    nout_ref[...] = high[2 * HID : 3 * HID]
    for k, ref in enumerate((eb, eg, nb, ng)):
        ref[...] = high[3 * HID + k : 3 * HID + k + 1]


def call(body, outs, ins, scratch=(), smem=(), flops=0):
    shapes = [jax.ShapeDtypeStruct(shape, F32) for shape in outs]
    size = 4 * sum(math.prod(shape) for shape in outs) + sum(4 * v.size for v in ins)
    return pl.pallas_call(
        body,
        out_shape=shapes,
        in_specs=[SMEM] * len(smem) + [VMEM] * len(ins),
        out_specs=[VMEM] * len(outs),
        scratch_shapes=[pltpu.VMEM(shape, kind) for shape, kind in scratch],
        cost_estimate=pl.CostEstimate(flops=flops, bytes_accessed=size, transcendentals=0),
        compiler_params=pltpu.CompilerParams(vmem_limit_bytes=40 * 1024 * 1024),
    )(*smem, *ins)


def make_packets(node_feat, lists):
    return call(packet_kernel, [(SLAB, HID)] * 3, [node_feat, lists], flops=10**9)


def edge_before(node_feat, edge_feat, sender, receiver, weight, bias):
    return call(
        before_kernel,
        [(EDGES, HID)],
        [node_feat, edge_feat, sender, receiver, weight, bias],
        scratch=[((EDGES, HID), jnp.int32)] * 2,
        flops=3 * 10**9,
    )[0]


def main_step(count, side, operands):
    return call(
        main_kernel,
        [(CELLS, HID)] * 2 + [(SLAB, HID)] * 3 + [(CELLS, HID)] * 3 + [(EDGES, HID)],
        operands,
        scratch=[
            ((EDGES, HID), jnp.int32),
            ((EDGES, HID), jnp.int32),
            ((EDGES // HID, HID), jnp.int32),
            ((EDGES, 2 * HID), BF16),
            ((EDGES, HID), F32),
            ((EDGES, HID), F32),
            ((EDGES, HID), F32),
            ((CELLS, 2 * HID), F32),
            ((HALO, 2 * HID), BF16),
            ((2, CELLS, HID), F32),
            ((2, 2 * HID, 2 * HID), F32),
            ((CELLS + HALO, 2 * HID), F32),
            ((2 * HID, 2 * HID), BF16),
        ],
        smem=[count, side],
        flops=10**10,
    )


def edge_after(cot, dpre, base, own, got, weight):
    return call(
        edge_kernel,
        [(EDGES, HID), (CELLS, HID)],
        [cot, dpre, base, own, got, weight],
        flops=10**9,
    )


def node_after(lists, back, part, weight):
    return call(node_kernel, [(CELLS, HID)], [lists, *back, part, weight], flops=10**9)[0]


def finish(side, part, other, scale):
    shapes = [(3 * HID, HID), (HID, HID), (2 * HID, HID), (HID, HID)] + [(1, HID)] * 4
    return call(
        functools.partial(finish_kernel, scale=scale), shapes, [part, other], smem=[side], flops=10**6
    )


def from_both(low, high, axis):
    peers = lax.axis_size(axis)
    up = [(i, i + 1) for i in range(peers - 1)]
    down = [(j, i) for i, j in up]
    return lax.ppermute(high, axis, up), lax.ppermute(low, axis, down)


def exchange_out(low, mid, high):
    before, after = from_both(low, high, GX)
    pieces = [piece.reshape(3, 3, SLOT, HID) for piece in (before, mid, after)]
    low, mid, high = (jnp.stack([piece[k] for piece in pieces]) for k in range(3))
    before, after = from_both(low, high, GY)
    pieces = (before, mid, after)
    low, mid, high = (jnp.stack([piece[:, k] for piece in pieces], axis=1) for k in range(3))
    before, after = from_both(low, high, GZ)
    return [piece.reshape(SLAB, HID) for piece in (before, mid, after)]


def exchange_back(low, mid, high):
    before, after = from_both(low, high, GZ)
    pieces = [piece.reshape(3, 3, SLOT, HID) for piece in (before, mid, after)]
    low, mid, high = (jnp.stack([piece[:, k] for piece in pieces], axis=1) for k in range(3))
    before, after = from_both(low, high, GY)
    pieces = (before, mid, after)
    low, mid, high = (jnp.stack([piece[k] for piece in pieces], axis=0) for k in range(3))
    before, after = from_both(low, high, GX)
    return [piece.reshape(SLAB, HID) for piece in (before, mid, after)]


def sum_half(keep, give):
    swap = [(0, 1), (1, 0)]
    part = keep + lax.ppermute(give, "c", swap)
    part = lax.all_to_all(part.reshape(16, 32, HID), ("x", "zl"), 0, 0).sum(0)
    part = lax.all_to_all(jnp.broadcast_to(part, (16, 32, HID)), ("y", "zh"), 0, 0).sum(0)
    part = lax.all_to_all(jnp.broadcast_to(part, (16, 32, HID)), ("x", "zl"), 0, 0)
    part = part.reshape(CELLS, HID)
    return part, lax.ppermute(part, "c", swap)


def on_device(
    node_feat,
    edge_feat,
    node_cot,
    edge_cot,
    sender,
    receiver,
    block_count,
    send_rows,
    edge_in_weight,
    edge_bias,
    edge_out_weight,
    edge_gain,
    node_in_weight,
    node_bias,
    node_out_weight,
    node_gain,
):
    scale = 1.0 / math.sqrt(lax.axis_size(AXES) * EDGES)
    side = lax.axis_index("c").astype(jnp.int32).reshape(1)
    lists = jnp.pad(send_rows.reshape(27, SLOT), ((0, 5), (0, HID - SLOT)))
    sender = sender.reshape(EDGES // HID, HID)
    receiver = receiver.reshape(EDGES // HID, HID)
    edge_bias, edge_gain, node_bias, node_gain = (
        row.reshape(1, HID) for row in (edge_bias, edge_gain, node_bias, node_gain)
    )
    halo = exchange_out(*make_packets(node_feat, lists))
    before = edge_before(node_feat, edge_feat, sender, receiver, edge_in_weight, edge_bias)
    operands = [before, *halo, edge_feat, edge_cot, sender, receiver, node_feat, node_cot]
    operands += [edge_in_weight, edge_out_weight, edge_gain]
    operands += [node_in_weight, node_bias, node_out_weight, node_gain]
    keep, give, back0, back1, back2, own, got, base, dpre = main_step(block_count, side, operands)
    part, other = sum_half(keep, give)
    edge_grad, own_part = edge_after(edge_cot, dpre, base, own, got, edge_in_weight)
    back = exchange_back(back0, back1, back2)
    node_grad = node_after(lists, back, own_part, edge_in_weight)
    ein, eout, nin, nout, eb, eg, nb, ng = finish(side, part, other, scale)
    vectors = [row.reshape(HID) for row in (eb, eg, nb, ng)]
    return (
        node_grad,
        edge_grad,
        ein,
        vectors[0],
        eout,
        vectors[1],
        nin,
        vectors[2],
        nout,
        vectors[3],
    )


def solution(mesh):
    fine = jax.sharding.Mesh(mesh.devices.reshape(SPLIT), AXES)
    return jax.shard_map(
        on_device,
        mesh=fine,
        in_specs=(
            P(AXES, None),
            P(AXES, None),
            P(AXES, None),
            P(AXES, None),
            P(AXES),
            P(AXES),
            P(AXES),
            P(GX, GY, GZ, None),
            P(),
            P(),
            P(),
            P(),
            P(),
            P(),
            P(),
            P(),
        ),
        out_specs=(
            P(AXES, None),
            P(AXES, None),
            P(),
            P(),
            P(),
            P(),
            P(),
            P(),
            P(),
            P(),
        ),
        check_vma=False,
    )
```

time: 236 us -> 149 us (0.63)
  other arithmetic: 57.6 us -> 4.23 us
  matrix products: 31.3 us -> 0 us
  local copies, waits for them, and re-layouts: 44.7 us -> 13.8 us
  Pallas kernels: 0 us -> 21.8 us
  waiting for transfers between devices: 25.6 us -> 30.5 us
    scatter-add x4 -> x0, other arithmetic: 44 us -> none  [the longest x1 13 us: on_device(): jax.ops.segment_sum(message, receiver, num_segments=num_cells, indices_ar...]
    dot_general x21 -> x0, matrix products: 31.3 us -> none  [the longest x3 6.56 us: edge_section(): preact = jnp.dot(edge_feat, edge_in_weight[:width], precision=HIGHEST)]
    gather x5 -> x0, local copies, waits for them, and re-layouts: 26.2 us -> none  [the longest x2 10.3 us: on_device(): edge_grads = edge_pull(edge_cot + node_grads[1][receiver])]
    pallas_call x0 -> x6, Pallas kernels: none -> 21.8 us  [call(): pl.pallas_call(body, out_shape=shapes, in_specs=[SMEM] * len(smem) + [VME...]
    all_to_all x3, waiting for transfers between devices: 4.63 us -> 10.6 us  [the longest x1 8.24 us: sum_half(): lax.all_to_all(jnp.broadcast_to(part, (16, 32, HID)), ('y', 'zh'), 0, 0)]
    another operation x0 -> x12, other arithmetic: none -> 3.45 us  [the longest x3 1.36 us: exchange_back(): jnp.stack([piece[:, k] for piece in pieces], axis=1)]
    mul x8 -> x0, other arithmetic: 3.09 us -> none  [the longest x1 0.69 us: on_device(): edge_weights[0] * grad_scale]
    reduce_sum x8 -> x2, other arithmetic: 2.97 us -> 0.04 us  [the longest x1 0.02 us: sum_half(): part = lax.all_to_all(part.reshape(16, 32, HID), ('x', 'zl'), 0, 0).sum(0)]
  transfers between devices with their start and end apart: 17 -> 17, of which waited for: 7 -> 9; matrix products, arithmetic and copies ran while one was open for 22% -> 4% of each run, Pallas kernels for 0% -> 5%
where the time goes in v2:
time: 149 us; the launch traced here: 146 us
  starting transfers between devices  74.1 us (50%)
  waiting for transfers between devices  30.5 us (20%)
  Pallas kernels  21.8 us (15%)
  local copies, waits for them, and re-layouts  13.8 us (9%)
  other arithmetic  4.23 us (3%)
    ppermute x12, starting transfers between devices, from_both(): return (lax.ppermute(high, axis, up), lax.ppermute(low, axis, down))  41.2 us
    pallas_call x6, Pallas kernels, call(): pl.pallas_call(body, out_shape=shapes, in_specs=[SMEM] * len(smem) + [VME...  21.8 us
    ppermute x12, waiting for transfers between devices, from_both(): return (lax.ppermute(high, axis, up), lax.ppermute(low, axis, down))  19.9 us
    all_to_all x1, starting transfers between devices, sum_half(): part = lax.all_to_all(part.reshape(16, 32, HID), ('x', 'zl'), 0, 0).sum(0)  10.6 us
    unnamed x56, local copies, waits for them, and re-layouts  10.6 us
    all_to_all x1, waiting for transfers between devices, sum_half(): lax.all_to_all(jnp.broadcast_to(part, (16, 32, HID)), ('y', 'zh'), 0, 0)  8.24 us
    all_to_all x1, starting transfers between devices, sum_half(): lax.all_to_all(jnp.broadcast_to(part, (16, 32, HID)), ('x', 'zl'), 0, 0)  7.82 us
    all_to_all x1, starting transfers between devices, sum_half(): lax.all_to_all(jnp.broadcast_to(part, (16, 32, HID)), ('y', 'zh'), 0, 0)  7.12 us
  transfers between devices with their start and end apart: 17, of which 9 were waited for; matrix products, arithmetic and copies ran while one was open for 4% of the time, Pallas kernels for 5%

profile of v2, /device:TPU:1, one launch (start us, length us, event | category | flops | bytes accessed | tf_op | source)
XLA Modules:
  0.0 145.7 jit_solution(8744876912626670695)
XLA Ops:
  0.6 0.7 reshape.101
  1.4 0.9 copy-done.2
  2.9 4.8 %collective-permute-start = (f32[288,128]{1,0:T(8,128)S(1)}, f32[288,128]{1,0:T(8,128)S(1)}, u32[]{:S(2)}, u32[]{:S(2)}) collective-permute-start(f32[288,128]{1,0:T(8,128)S(1)} %get-tuple-element.32), channel_id=1, source_target_pairs={{0,16},{16,32},{32,48},{48,64},{64,80},{80,96},{96,112},{112,128},... | collective-permute-start | bytes 442376 | tf_op jit(solution)/shard_map/ppermute | solution.py:403
  7.7 1.3 collective-permute-start.1
  9.0 0.8 collective-permute-done
  9.8 4.4 %collective-permute-done.1 = f32[288,128]{1,0:T(8,128)S(1)} collective-permute-done((f32[288,128]{1,0:T(8,128)S(1)}, f32[288,128]{1,0:T(8,128)S(1)}, u32[]{:S(2)}, u32[]{:S(2)}) %collective-permute-start.1) | collective-permute-done | bytes 147488 | tf_op jit(solution)/shard_map/ppermute | solution.py:403
  14.3 1.3 collective-permute-start.3
  15.6 4.6 %collective-permute-start.2 = (f32[3,3,32,128]{3,2,1,0:T(8,128)S(1)}, f32[3,3,32,128]{3,2,1,0:T(8,128)S(1)}, u32[]{:S(2)}, u32[]{:S(2)}) collective-permute-start(f32[3,3,32,128]{3,2,1,0:T(8,128)S(1)} %pad_maximum_fusion), channel_id=1, source_target_pairs={{0,4},{4,8},{8,12},{1,5},{5,9},{9,13},{2,6},{6,10},{10,14},{3,7},{... | collective-permute-start | bytes 442376 | tf_op jit(solution)/shard_map/ppermute | solution.py:403
  20.6 1.6 %collective-permute-done.2 = f32[3,3,32,128]{3,2,1,0:T(8,128)S(1)} collective-permute-done((f32[3,3,32,128]{3,2,1,0:T(8,128)S(1)}, f32[3,3,32,128]{3,2,1,0:T(8,128)S(1)}, u32[]{:S(2)}, u32[]{:S(2)}) %collective-permute-start.2) | collective-permute-done | bytes 147488 | tf_op jit(solution)/shard_map/ppermute | solution.py:403
  22.3 0.7 pad_maximum_fusion.3
  23.0 12.0 %collective-permute-start.4 = (f32[3,3,32,128]{3,2,1,0:T(8,128)}, f32[3,3,32,128]{3,2,1,0:T(8,128)S(1)}, u32[]{:S(2)}, u32[]{:S(2)}) collective-permute-start(f32[3,3,32,128]{3,2,1,0:T(8,128)} %pad_maximum_fusion.3), channel_id=1, source_target_pairs={{0,1},{1,2},{2,3},{4,5},{5,6},{6,7},{8,9},{9,10},{10,11},{12,13},{... | collective-permute-start | bytes 442376 | tf_op jit(solution)/shard_map/ppermute | solution.py:403
  35.0 0.7 pad_maximum_fusion.5
  35.7 1.9 %collective-permute-start.5 = (f32[3,3,32,128]{3,2,1,0:T(8,128)}, f32[3,3,32,128]{3,2,1,0:T(8,128)S(1)}, u32[]{:S(2)}, u32[]{:S(2)}) collective-permute-start(f32[3,3,32,128]{3,2,1,0:T(8,128)} %pad_maximum_fusion.5), channel_id=1, source_target_pairs={{1,0},{2,1},{3,2},{5,4},{6,5},{7,6},{9,8},{10,9},{11,10},{13,12},{... | collective-permute-start | bytes 442376 | tf_op jit(solution)/shard_map/ppermute | solution.py:403
  38.3 2.9 %shard_map.231.pre_ref = f32[2048,128]{1,0:T(8,128)S(1)} custom-call(f32[512,128]{1,0:T(8,128)S(1)} %copy-done.2, f32[2048,128]{1,0:T(8,128)S(1)} %copy-done, s32[16,128]{1,0:T(8,128)S(1)} %bitcast.40, s32[16,128]{1,0:T(8,128)S(1)} %bitcast.42, f32[384,128]{1,0:T(8,128)S(1)} %copy-done.5, f32[1,128]{1,0:T(1,128)S(1)} %bitcast.44), custom_call_target="tpu_custom_call" | custom-call | flops 3000000000 | bytes 2572800 | tf_op jit(solution)/shard_map/pallas_call | solution.py:329
  41.2 1.0 copy-done.26
  42.2 4.2 %collective-permute-done.5 = f32[3,3,32,128]{3,2,1,0:T(8,128)S(1)} collective-permute-done((f32[3,3,32,128]{3,2,1,0:T(8,128)}, f32[3,3,32,128]{3,2,1,0:T(8,128)S(1)}, u32[]{:S(2)}, u32[]{:S(2)}) %collective-permute-start.5) | collective-permute-done | bytes 147488 | tf_op jit(solution)/shard_map/ppermute | solution.py:403
  47.7 0.9 copy-done.7
  48.6 0.9 copy-done.8
  49.5 0.8 copy-done.10
  50.4 1.2 copy-done.27
  51.6 13.9 %shard_map.233 = (f32[512,128]{1,0:T(8,128)S(1)}, f32[512,128]{1,0:T(8,128)S(1)}, f32[288,128]{1,0:T(8,128)S(1)}, f32[288,128]{1,0:T(8,128)S(1)}, f32[288,128]{1...) custom-call(s32[16]{0:T(128)S(1)} %copy-done.14, ...), custom_call_target="tpu_custom_call" | custom-call | flops 10000000000 | bytes 7390720 | tf_op jit(solution)/shard_map/pallas_call | solution.py:329
  65.5 1.0 copy-done.18
  66.5 1.9 %collective-permute-start.12 = (f32[512,128]{1,0:T(8,128)S(1)}, f32[512,128]{1,0:T(8,128)S(1)}, u32[]{:S(2)}, u32[]{:S(2)}) collective-permute-start(f32[512,128]{1,0:T(8,128)S(1)} %get-tuple-element.45), channel_id=1, source_target_pairs={{0,1},{1,0},{2,3},{3,2},{4,5},{5,4},{6,7},{7,6},{8,9},{9,8},{10,11... | collective-permute-start | bytes 786440 | tf_op jit(solution)/shard_map/ppermute | solution.py:430
  68.4 3.4 %collective-permute-start.6 = (f32[288,128]{1,0:T(8,128)S(1)}, f32[288,128]{1,0:T(8,128)S(1)}, u32[]{:S(2)}, u32[]{:S(2)}) collective-permute-start(f32[288,128]{1,0:T(8,128)S(1)} %get-tuple-element.35), channel_id=1, source_target_pairs={{0,1},{1,2},{2,3},{4,5},{5,6},{6,7},{8,9},{9,10},{10,11},{12,13},{... | collective-permute-start | bytes 442376 | tf_op jit(solution)/shard_map/ppermute | solution.py:403
  71.8 0.7 add.5
  72.6 10.6 %all-to-all-start = ((f32[16,32,128]{2,1,0:T(8,128)}), f32[16,32,128]{2,1,0:T(8,128)S(1)}, u32[]{:S(2)}, u32[]{:S(2)}) async-start(f32[16,32,128]{2,1,0:T(8,128)} %bitcast.25), calls=%async_computation | async-start | bytes 524288 | tf_op jit(solution)/shard_map/all_to_all | solution.py:431
  83.2 1.9 %collective-permute-start.7 = (f32[288,128]{1,0:T(8,128)S(1)}, f32[288,128]{1,0:T(8,128)S(1)}, u32[]{:S(2)}, u32[]{:S(2)}) collective-permute-start(f32[288,128]{1,0:T(8,128)S(1)} %get-tuple-element.37), channel_id=1, source_target_pairs={{1,0},{2,1},{3,2},{5,4},{6,5},{7,6},{9,8},{10,9},{11,10},{13,12},{... | collective-permute-start | bytes 442376 | tf_op jit(solution)/shard_map/ppermute | solution.py:403
  85.2 8.5 %collective-permute-done.7 = f32[288,128]{1,0:T(8,128)S(1)} collective-permute-done((f32[288,128]{1,0:T(8,128)S(1)}, f32[288,128]{1,0:T(8,128)S(1)}, u32[]{:S(2)}, u32[]{:S(2)}) %collective-permute-start.7) | collective-permute-done | bytes 147488 | tf_op jit(solution)/shard_map/ppermute | solution.py:403
  94.1 0.7 broadcast_in_dim.6
  94.8 7.1 %all-to-all-start.1 = ((f32[16,32,128]{2,1,0:T(8,128)}), f32[16,32,128]{2,1,0:T(8,128)S(1)}, u32[]{:S(2)}, u32[]{:S(2)}) async-start(f32[16,32,128]{2,1,0:T(8,128)} %broadcast_in_dim.6), calls=%async_computation.1 | async-start | bytes 524288 | tf_op jit(solution)/shard_map/all_to_all | solution.py:432
  101.9 0.7 pad_maximum_fusion.8
  102.6 1.3 collective-permute-start.9
  103.9 0.7 pad_maximum_fusion.6
  104.6 4.0 %collective-permute-start.8 = (f32[3,3,32,128]{3,2,1,0:T(8,128)}, f32[3,3,32,128]{3,2,1,0:T(8,128)S(1)}, u32[]{:S(2)}, u32[]{:S(2)}) collective-permute-start(f32[3,3,32,128]{3,2,1,0:T(8,128)} %pad_maximum_fusion.6), channel_id=1, source_target_pairs={{0,4},{4,8},{8,12},{1,5},{5,9},{9,13},{2,6},{6,10},{10,14},{3,7},{... | collective-permute-start | bytes 442376 | tf_op jit(solution)/shard_map/ppermute | solution.py:403
  108.6 8.2 %all-to-all-done.1 = f32[16,32,128]{2,1,0:T(8,128)S(1)} async-done(((f32[16,32,128]{2,1,0:T(8,128)}), f32[16,32,128]{2,1,0:T(8,128)S(1)}, u32[]{:S(2)}, u32[]{:S(2)}) %all-to-all-start.1) | async-done | bytes 262176 | tf_op jit(solution)/shard_map/all_to_all | solution.py:432
  116.9 0.7 broadcast_in_dim.7
  117.6 7.8 %all-to-all-start.2 = ((f32[16,32,128]{2,1,0:T(8,128)}), f32[16,32,128]{2,1,0:T(8,128)S(1)}, u32[]{:S(2)}, u32[]{:S(2)}) async-start(f32[16,32,128]{2,1,0:T(8,128)} %broadcast_in_dim.7), calls=%async_computation.2 | async-start | bytes 524288 | tf_op jit(solution)/shard_map/all_to_all | solution.py:433
  125.5 0.9 fusion.2
  126.4 3.4 %collective-permute-start.10 = (f32[3,3,32,128]{3,2,1,0:T(8,128)S(1)}, f32[3,3,32,128]{3,2,1,0:T(8,128)S(1)}, u32[]{:S(2)}, u32[]{:S(2)}) collective-permute-start(f32[3,3,32,128]{3,2,1,0:T(8,128)S(1)} %pad_maximum_fusion.9), channel_id=1, source_target_pairs={{0,16},{16,32},{32,48},{48,64},{64,80},{80,96},{96,112},{112,128},... | collective-permute-start | bytes 442376 | tf_op jit(solution)/shard_map/ppermute | solution.py:403
  129.8 0.7 pad_maximum_fusion.11
  130.5 1.3 collective-permute-start.11
  131.8 2.0 %all-to-all-done.2 = f32[16,32,128]{2,1,0:T(8,128)S(1)} async-done(((f32[16,32,128]{2,1,0:T(8,128)}), f32[16,32,128]{2,1,0:T(8,128)S(1)}, u32[]{:S(2)}, u32[]{:S(2)}) %all-to-all-start.2) | async-done | bytes 262176 | tf_op jit(solution)/shard_map/all_to_all | solution.py:433
  133.7 5.5 %collective-permute-start.13 = (f32[512,128]{1,0:T(8,128)S(1)}, f32[512,128]{1,0:T(8,128)S(1)}, u32[]{:S(2)}, u32[]{:S(2)}) collective-permute-start(f32[512,128]{1,0:T(8,128)S(1)} %bitcast.31), channel_id=1, source_target_pairs={{0,1},{1,0},{2,3},{3,2},{4,5},{5,4},{6,7},{7,6},{8,9},{9,8},{10,11... | collective-permute-start | bytes 786440 | tf_op jit(solution)/shard_map/ppermute | solution.py:435
  139.3 0.9 copy-done.23
  140.2 0.9 copy-done.25
  141.1 2.0 %shard_map.234 = (f32[2048,128]{1,0:T(8,128)}, f32[512,128]{1,0:T(8,128)S(1)}) custom-call(f32[2048,128]{1,0:T(8,128)S(1)} %copy-done.1, f32[2048,128]{1,0:T(8,128)S(1)} %copy-done.19, f32[512,128]{1,0:T(8,128)S(1)} %copy-done.25, f32[512,128]{1,0:T(8,128)S(1)} %copy-done.21, f32[512,128]{1,0:T(8,128)S(1)} %copy-done.23, f32[384,128]{1,0:T(8,128)S(1)} %copy-done.5), custom_call_target="tpu_custom_call" | custom-call | flops 1000000000 | bytes 4390912 | tf_op jit(solution)/shard_map/pallas_call | solution.py:329
  143.2 1.7 %shard_map.235 = f32[512,128]{1,0:T(8,128)} custom-call(s32[32,128]{1,0:T(8,128)S(1)} %pad.4.lists_ref, f32[288,128]{1,0:T(8,128)S(1)} %bitcast.36, f32[288,128]{1,0:T(8,128)S(1)} %bitcast.35, f32[288,128]{1,0:T(8,128)S(1)} %bitcast.38, f32[512,128]{1,0:T(8,128)S(1)} %get-tuple-element.42.part_ref, f32[384,128]{1,0:T(8,128)S(1)} %copy-done.5), custom_call_target="tpu_custom_call" | custom-call | flops 1000000000 | bytes 1179648 | tf_op jit(solution)/shard_map/pallas_call | solution.py:329
  144.9 0.8 shard_map.236
  (79 shorter events, 3.5 us)
Async XLA Ops:
  1.4 1.0 copy-start.2
  2.9 6.9 %collective-permute-start = (f32[288,128]{1,0:T(8,128)S(1)}, f32[288,128]{1,0:T(8,128)S(1)}, u32[]{:S(2)}, u32[]{:S(2)}) collective-permute-start(f32[288,128]{1,0:T(8,128)S(1)} %get-tuple-element.32), channel_id=1, source_target_pairs={{0,16},{16,32},{32,48},{48,64},{64,80},{80,96},{96,112},{112,128},... | collective-permute-start | bytes 442376 | tf_op jit(solution)/shard_map/ppermute | solution.py:403
  7.7 6.5 %collective-permute-start.1 = (f32[288,128]{1,0:T(8,128)S(1)}, f32[288,128]{1,0:T(8,128)S(1)}, u32[]{:S(2)}, u32[]{:S(2)}) collective-permute-start(f32[288,128]{1,0:T(8,128)S(1)} %get-tuple-element.34), channel_id=1, source_target_pairs={{16,0},{32,16},{48,32},{64,48},{80,64},{96,80},{112,96},{128,112},... | collective-permute-start | bytes 442376 | tf_op jit(solution)/shard_map/ppermute | solution.py:403
  14.3 6.4 %collective-permute-start.3 = (f32[3,3,32,128]{3,2,1,0:T(8,128)S(1)}, f32[3,3,32,128]{3,2,1,0:T(8,128)S(1)}, u32[]{:S(2)}, u32[]{:S(2)}) collective-permute-start(f32[3,3,32,128]{3,2,1,0:T(8,128)S(1)} %pad_maximum_fusion.2), channel_id=1, source_target_pairs={{4,0},{8,4},{12,8},{5,1},{9,5},{13,9},{6,2},{10,6},{14,10},{7,3},{... | collective-permute-start | bytes 442376 | tf_op jit(solution)/shard_map/ppermute | solution.py:403
  15.6 22.1 %copy-start = (f32[2048,128]{1,0:T(8,128)S(1)}, f32[2048,128]{1,0:T(8,128)}, u32[]{:S(2)}) copy-start(f32[2048,128]{1,0:T(8,128)} %edge_ref.3) | copy-start | bytes 3145732
  15.6 6.7 %collective-permute-start.2 = (f32[3,3,32,128]{3,2,1,0:T(8,128)S(1)}, f32[3,3,32,128]{3,2,1,0:T(8,128)S(1)}, u32[]{:S(2)}, u32[]{:S(2)}) collective-permute-start(f32[3,3,32,128]{3,2,1,0:T(8,128)S(1)} %pad_maximum_fusion), channel_id=1, source_target_pairs={{0,4},{4,8},{8,12},{1,5},{5,9},{9,13},{2,6},{6,10},{10,14},{3,7},{... | collective-permute-start | bytes 442376 | tf_op jit(solution)/shard_map/ppermute | solution.py:403
  23.0 14.7 %copy-start.5 = (f32[384,128]{1,0:T(8,128)S(1)}, f32[384,128]{1,0:T(8,128)}, u32[]{:S(2)}) copy-start(f32[384,128]{1,0:T(8,128)} %weight_ref.5) | copy-start | bytes 589828
  23.0 19.2 %collective-permute-start.4 = (f32[3,3,32,128]{3,2,1,0:T(8,128)}, f32[3,3,32,128]{3,2,1,0:T(8,128)S(1)}, u32[]{:S(2)}, u32[]{:S(2)}) collective-permute-start(f32[3,3,32,128]{3,2,1,0:T(8,128)} %pad_maximum_fusion.3), channel_id=1, source_target_pairs={{0,1},{1,2},{2,3},{4,5},{5,6},{6,7},{8,9},{9,10},{10,11},{12,13},{... | collective-permute-start | bytes 442376 | tf_op jit(solution)/shard_map/ppermute | solution.py:403
  35.0 2.6 %copy-start.11 = (s32[2048]{0:T(1024)S(1)}, s32[2048]{0:T(1024)}, u32[]{:S(2)}) copy-start(s32[2048]{0:T(1024)} %param.20) | copy-start | bytes 24580
  35.0 2.6 %copy-start.12 = (s32[2048]{0:T(1024)S(1)}, s32[2048]{0:T(1024)}, u32[]{:S(2)}) copy-start(s32[2048]{0:T(1024)} %param.21) | copy-start | bytes 24580
  35.7 10.7 %collective-permute-start.5 = (f32[3,3,32,128]{3,2,1,0:T(8,128)}, f32[3,3,32,128]{3,2,1,0:T(8,128)S(1)}, u32[]{:S(2)}, u32[]{:S(2)}) collective-permute-start(f32[3,3,32,128]{3,2,1,0:T(8,128)} %pad_maximum_fusion.5), channel_id=1, source_target_pairs={{1,0},{2,1},{3,2},{5,4},{6,5},{7,6},{9,8},{10,9},{11,10},{13,12},{... | collective-permute-start | bytes 442376 | tf_op jit(solution)/shard_map/ppermute | solution.py:403
  37.6 0.7 copy-start.13
  38.3 8.8 %copy-start.1 = (f32[2048,128]{1,0:T(8,128)S(1)}, f32[2048,128]{1,0:T(8,128)}, u32[]{:S(2)}) copy-start(f32[2048,128]{1,0:T(8,128)} %cot_ref.3) | copy-start | bytes 3145732
  38.3 8.8 %copy-start.4 = (f32[512,128]{1,0:T(8,128)S(1)}, f32[512,128]{1,0:T(8,128)}, u32[]{:S(2)}) copy-start(f32[512,128]{1,0:T(8,128)} %node_cot_ref.1) | copy-start | bytes 786436
  38.3 8.8 %copy-start.9 = (f32[128,128]{1,0:T(8,128)S(1)}, f32[128,128]{1,0:T(8,128)}, u32[]{:S(2)}) copy-start(f32[128,128]{1,0:T(8,128)} %eout_ref.1) | copy-start | bytes 196612
  41.2 1.0 copy-start.26
  42.1 4.9 %copy-start.3 = (f32[512,128]{1,0:T(8,128)S(1)}, f32[512,128]{1,0:T(8,128)}, u32[]{:S(2)}) copy-start(f32[512,128]{1,0:T(8,128)} %node_ref.5) | copy-start | bytes 786436
  42.1 4.9 %copy-start.17 = (f32[128]{0:T(128)S(1)}, f32[128]{0:T(128)}, u32[]{:S(2)}) copy-start(f32[128]{0:T(128)} %param.31) | copy-start | bytes 1540
  46.4 0.7 copy-start.6
  47.0 0.7 copy-start.14
  47.0 0.7 copy-start.15
  47.0 0.7 copy-start.16
  47.7 0.9 copy-start.7
  48.6 0.9 copy-start.8
  49.5 0.8 copy-start.10
  50.4 1.2 copy-start.27
  65.5 1.0 copy-start.18
  66.5 6.0 %copy-start.20 = (f32[512,128]{1,0:T(8,128)}, f32[512,128]{1,0:T(8,128)S(1)}, u32[]{:S(2)}) copy-start(f32[512,128]{1,0:T(8,128)S(1)} %get-tuple-element.40.own_ref) | copy-start | bytes 786436
  66.5 6.0 %copy-start.22 = (f32[512,128]{1,0:T(8,128)}, f32[512,128]{1,0:T(8,128)S(1)}, u32[]{:S(2)}) copy-start(f32[512,128]{1,0:T(8,128)S(1)} %get-tuple-element.41.got_ref) | copy-start | bytes 786436
  66.5 6.0 %copy-start.24 = (f32[512,128]{1,0:T(8,128)}, f32[512,128]{1,0:T(8,128)S(1)}, u32[]{:S(2)}) copy-start(f32[512,128]{1,0:T(8,128)S(1)} %get-tuple-element.39.base_ref) | copy-start | bytes 786436
  66.5 5.3 %collective-permute-start.12 = (f32[512,128]{1,0:T(8,128)S(1)}, f32[512,128]{1,0:T(8,128)S(1)}, u32[]{:S(2)}, u32[]{:S(2)}) collective-permute-start(f32[512,128]{1,0:T(8,128)S(1)} %get-tuple-element.45), channel_id=1, source_target_pairs={{0,1},{1,0},{2,3},{3,2},{4,5},{5,4},{6,7},{7,6},{8,9},{9,8},{10,11... | collective-permute-start | bytes 786440 | tf_op jit(solution)/shard_map/ppermute | solution.py:430
  68.4 16.7 %collective-permute-start.6 = (f32[288,128]{1,0:T(8,128)S(1)}, f32[288,128]{1,0:T(8,128)S(1)}, u32[]{:S(2)}, u32[]{:S(2)}) collective-permute-start(f32[288,128]{1,0:T(8,128)S(1)} %get-tuple-element.35), channel_id=1, source_target_pairs={{0,1},{1,2},{2,3},{4,5},{5,6},{6,7},{8,9},{9,10},{10,11},{12,13},{... | collective-permute-start | bytes 442376 | tf_op jit(solution)/shard_map/ppermute | solution.py:403
  72.6 21.5 %all-to-all-start = ((f32[16,32,128]{2,1,0:T(8,128)}), f32[16,32,128]{2,1,0:T(8,128)S(1)}, u32[]{:S(2)}, u32[]{:S(2)}) async-start(f32[16,32,128]{2,1,0:T(8,128)} %bitcast.25), calls=%async_computation | async-start | bytes 524288 | tf_op jit(solution)/shard_map/all_to_all | solution.py:431
  83.2 10.5 %collective-permute-start.7 = (f32[288,128]{1,0:T(8,128)S(1)}, f32[288,128]{1,0:T(8,128)S(1)}, u32[]{:S(2)}, u32[]{:S(2)}) collective-permute-start(f32[288,128]{1,0:T(8,128)S(1)} %get-tuple-element.37), channel_id=1, source_target_pairs={{1,0},{2,1},{3,2},{5,4},{6,5},{7,6},{9,8},{10,9},{11,10},{13,12},{... | collective-permute-start | bytes 442376 | tf_op jit(solution)/shard_map/ppermute | solution.py:403
  94.8 22.0 %all-to-all-start.1 = ((f32[16,32,128]{2,1,0:T(8,128)}), f32[16,32,128]{2,1,0:T(8,128)S(1)}, u32[]{:S(2)}, u32[]{:S(2)}) async-start(f32[16,32,128]{2,1,0:T(8,128)} %broadcast_in_dim.6), calls=%async_computation.1 | async-start | bytes 524288 | tf_op jit(solution)/shard_map/all_to_all | solution.py:432
  102.6 22.8 %collective-permute-start.9 = (f32[3,3,32,128]{3,2,1,0:T(8,128)}, f32[3,3,32,128]{3,2,1,0:T(8,128)}, u32[]{:S(2)}, u32[]{:S(2)}) collective-permute-start(f32[3,3,32,128]{3,2,1,0:T(8,128)} %pad_maximum_fusion.8), channel_id=1, source_target_pairs={{4,0},{8,4},{12,8},{5,1},{9,5},{13,9},{6,2},{10,6},{14,10},{7,3},{... | collective-permute-start | bytes 442376 | tf_op jit(solution)/shard_map/ppermute | solution.py:403
  104.6 21.7 %collective-permute-start.8 = (f32[3,3,32,128]{3,2,1,0:T(8,128)}, f32[3,3,32,128]{3,2,1,0:T(8,128)S(1)}, u32[]{:S(2)}, u32[]{:S(2)}) collective-permute-start(f32[3,3,32,128]{3,2,1,0:T(8,128)} %pad_maximum_fusion.6), channel_id=1, source_target_pairs={{0,4},{4,8},{8,12},{1,5},{5,9},{9,13},{2,6},{6,10},{10,14},{3,7},{... | collective-permute-start | bytes 442376 | tf_op jit(solution)/shard_map/ppermute | solution.py:403
  116.9 22.3 %copy-start.19 = (f32[2048,128]{1,0:T(8,128)S(1)}, f32[2048,128]{1,0:T(8,128)}, u32[]{:S(2)}) copy-start(f32[2048,128]{1,0:T(8,128)} %copy-done.18) | copy-start | bytes 3145732
  117.6 16.1 %all-to-all-start.2 = ((f32[16,32,128]{2,1,0:T(8,128)}), f32[16,32,128]{2,1,0:T(8,128)S(1)}, u32[]{:S(2)}, u32[]{:S(2)}) async-start(f32[16,32,128]{2,1,0:T(8,128)} %broadcast_in_dim.7), calls=%async_computation.2 | async-start | bytes 524288 | tf_op jit(solution)/shard_map/all_to_all | solution.py:433
  126.4 12.9 %copy-start.21 = (f32[512,128]{1,0:T(8,128)S(1)}, f32[512,128]{1,0:T(8,128)}, u32[]{:S(2)}) copy-start(f32[512,128]{1,0:T(8,128)} %copy-done.20) | copy-start | bytes 786436
  126.4 16.8 %collective-permute-start.10 = (f32[3,3,32,128]{3,2,1,0:T(8,128)S(1)}, f32[3,3,32,128]{3,2,1,0:T(8,128)S(1)}, u32[]{:S(2)}, u32[]{:S(2)}) collective-permute-start(f32[3,3,32,128]{3,2,1,0:T(8,128)S(1)} %pad_maximum_fusion.9), channel_id=1, source_target_pairs={{0,16},{16,32},{32,48},{48,64},{64,80},{80,96},{96,112},{112,128},... | collective-permute-start | bytes 442376 | tf_op jit(solution)/shard_map/ppermute | solution.py:403
  130.5 12.7 %collective-permute-start.11 = (f32[3,3,32,128]{3,2,1,0:T(8,128)}, f32[3,3,32,128]{3,2,1,0:T(8,128)S(1)}, u32[]{:S(2)}, u32[]{:S(2)}) collective-permute-start(f32[3,3,32,128]{3,2,1,0:T(8,128)} %pad_maximum_fusion.11), channel_id=1, source_target_pairs={{16,0},{32,16},{48,32},{64,48},{80,64},{96,80},{112,96},{128,112},... | collective-permute-start | bytes 442376 | tf_op jit(solution)/shard_map/ppermute | solution.py:403
  133.7 11.2 %collective-permute-start.13 = (f32[512,128]{1,0:T(8,128)S(1)}, f32[512,128]{1,0:T(8,128)S(1)}, u32[]{:S(2)}, u32[]{:S(2)}) collective-permute-start(f32[512,128]{1,0:T(8,128)S(1)} %bitcast.31), channel_id=1, source_target_pairs={{0,1},{1,0},{2,3},{3,2},{4,5},{5,4},{6,7},{7,6},{8,9},{9,8},{10,11... | collective-permute-start | bytes 786440 | tf_op jit(solution)/shard_map/ppermute | solution.py:435
  139.2 1.0 copy-start.23
  140.2 0.9 copy-start.25

commit v3 on v2

v3 whole, which is shorter than its diff:
```python
import functools
import math

import jax
import jax.numpy as jnp
from jax import lax
from jax.experimental import pallas as pl
from jax.experimental.pallas import tpu as pltpu
from jax.sharding import PartitionSpec as P

NORM_EPS = 1e-05
AXES = ("y", "zl", "x", "zh", "c")
SPLIT = (8, 4, 4, 2, 2)
GX, GY, GZ = (("y", "zl"), ("x",), ("zh", "c"))
SWAP = [(0, 1), (1, 0)]
HID, CELLS, EDGES, SLOT = 128, 512, 2048, 32
SLAB = 9 * SLOT
HALO = 896
BLOCK = 512
F32, BF16 = jnp.float32, jnp.bfloat16
VMEM = pl.BlockSpec(memory_space=pltpu.VMEM)
SMEM = pl.BlockSpec(memory_space=pltpu.SMEM)


def split(value):
    high = value.astype(BF16)
    low = (value - high.astype(F32)).astype(BF16)
    return jnp.concatenate([high, low], axis=1)


def fold(value):
    return value[:, :HID] + value[:, HID:]


def mix(weight):
    high = weight.astype(BF16)
    low = (weight - high.astype(F32)).astype(BF16)
    top = jnp.concatenate([high, low], axis=1)
    bottom = jnp.concatenate([high, jnp.zeros_like(low)], axis=1)
    return jnp.concatenate([top, bottom], axis=0)


def mul(left, right):
    return jnp.dot(left, right, preferred_element_type=F32)


def mul_rows(left, right):
    return lax.dot_general(left, right, (((0,), (0,)), ((), ())), preferred_element_type=F32)


def quad(value):
    top, bottom = value[:HID], value[HID:]
    return fold(top) + fold(bottom)


def centred(weight):
    return weight - jnp.mean(weight, axis=1, keepdims=True)


def silu_parts(preact):
    gate = 1.0 / (1.0 + jnp.exp(-preact))
    hidden = preact * gate
    return hidden, gate + hidden * (1.0 - gate)


def spread_columns(index, out_ref):
    turned = jnp.transpose(index.astype(F32)).astype(jnp.int32)
    for block in range(EDGES // HID):
        column = turned[:, block : block + 1]
        out_ref[block * HID : (block + 1) * HID, :] = jnp.broadcast_to(column, (HID, HID))


def hot_rows(column, width, base=0):
    lane = lax.broadcasted_iota(jnp.int32, column.shape, 1)
    parts = [
        (column == lane + (base + start)).astype(F32).astype(BF16) for start in range(0, width, HID)
    ]
    return jnp.concatenate(parts, axis=1)


def hot_columns(ref, first, height, base=0):
    level = lax.broadcasted_iota(jnp.int32, (height, HID), 0) + base
    parts = []
    for j in range(BLOCK // HID):
        row = ref[pl.ds(first + j, 1), :]
        parts.append((level == row).astype(F32).astype(BF16))
    return jnp.concatenate(parts, axis=1)


def parity(dim):
    return lax.axis_index(("zl", "x", "c")[dim]) & 1


def near_first(odd, entry):
    return entry if entry == 1 else jnp.where(odd == 0, 2 - entry, entry)


def list_rows(lists_ref, index_ref):
    index_ref[...] = jnp.zeros_like(index_ref)
    for k in range(27):
        x, y, z = (
            near_first(parity(dim), entry) for dim, entry in enumerate((k // 9, k // 3 % 3, k % 3))
        )
        index_ref[k : k + 1, :SLOT] = lists_ref[x, y, pl.ds(z, 1), :]
    turned = jnp.transpose(index_ref[...].astype(F32)).astype(jnp.int32)
    cell = lax.broadcasted_iota(jnp.int32, (SLOT, CELLS), 1)
    parts = []
    for k in range(27):
        hot = (turned[:SLOT, k : k + 1] == cell).astype(F32)
        parts.append((hot if k != 13 else hot * 0.0).astype(BF16))
    return jnp.concatenate(parts, axis=0)


def packet_kernel(node_ref, lists_ref, first_ref, mid_ref, second_ref, index_ref):
    rows = fold(mul(list_rows(lists_ref, index_ref), split(node_ref[...])))
    first_ref[...] = rows[:SLAB]
    mid_ref[...] = rows[SLAB : 2 * SLAB]
    second_ref[...] = rows[2 * SLAB :]


def regroup_kernel(in0, in1, in2, out0, out1, out2, *, chunk):
    for i, source in enumerate((in0, in1, in2)):
        base = source.shape[0] - SLAB if i == 0 else 0
        for j, target in enumerate((out0, out1, out2)):
            for k in range(SLAB // (3 * chunk)):
                to = (3 * k + i) * chunk
                at = base + (3 * k + j) * chunk
                target[to : to + chunk, :] = source[at : at + chunk, :]


def before_kernel(
    node_ref,
    edge_ref,
    sender_ref,
    receiver_ref,
    ein_ref,
    ebias_ref,
    eout_ref,
    nin_ref,
    nbias_ref,
    nout_ref,
    pre_ref,
    node_pre_ref,
    send_ref,
    recv_ref,
    order_ref,
    mix_ref,
):
    raw = sender_ref[...]
    slot = raw - CELLS
    direction = slot >> 5
    third = (direction * 43) >> 7
    ninth = (third * 43) >> 7
    x, y, z = (
        2 - entry + parity(dim) * (2 * entry - 2)
        for dim, entry in enumerate((ninth, third - 3 * ninth, direction - 3 * third))
    )
    moved = CELLS + SLAB * z + SLOT * (3 * x + y) + (slot & (SLOT - 1))
    order_ref[...] = jnp.where(raw < CELLS, raw, moved)
    spread_columns(order_ref[...], send_ref)
    spread_columns(receiver_ref[...], recv_ref)
    own = split(node_ref[...])
    halo_mix = mix(ein_ref[HID : 2 * HID, :])
    sent = fold(mul(own, halo_mix))
    got = fold(mul(own, mix(ein_ref[2 * HID :, :])))
    table = jnp.concatenate([split(sent), split(got)], axis=0)
    first = mix(ein_ref[:HID, :])
    for i in range(EDGES // BLOCK):
        rows = slice(i * BLOCK, (i + 1) * BLOCK)
        hot = jnp.concatenate(
            [hot_rows(send_ref[rows, :], CELLS), hot_rows(recv_ref[rows, :], CELLS)], axis=1
        )
        value = mul(hot, table) + mul(split(edge_ref[rows, :]), first)
        pre_ref[rows, :] = fold(value) + ebias_ref[...]
    node_pre_ref[...] = fold(mul(own, mix(nin_ref[:HID, :]))) + nbias_ref[...]
    edge_out, node_out = centred(eout_ref[...]), centred(nout_ref[...])
    mix_ref[0] = halo_mix
    mix_ref[1] = mix(edge_out)
    mix_ref[2] = mix(jnp.transpose(edge_out))
    mix_ref[3] = mix(nin_ref[HID:, :])
    mix_ref[4] = mix(node_out)
    mix_ref[5] = mix(jnp.transpose(node_out))
    mix_ref[6] = mix(jnp.transpose(nin_ref[:HID, :]))
    mix_ref[7] = mix(jnp.transpose(nin_ref[HID:, :]))


def main_kernel(
    count_ref,
    halo0_ref,
    halo1_ref,
    halo2_ref,
    pre_ref,
    node_pre_ref,
    send_ref,
    recv_ref,
    order_ref,
    mix_ref,
    receiver_ref,
    node_ref,
    node_cot_ref,
    cot_ref,
    edge_ref,
    egain_ref,
    ngain_ref,
    back0_ref,
    back1_ref,
    back2_ref,
    own_ref,
    got_ref,
    base_ref,
    dpre_ref,
    acc_ref,
    rest_ref,
    hid_ref,
    slope_ref,
    norm_ref,
    inv_ref,
    sum_ref,
    table_ref,
    row_ref,
):
    halo = [halo0_ref[...], halo1_ref[...], halo2_ref[...], jnp.zeros((HALO - 3 * SLAB, HID), F32)]
    halo_split = split(jnp.concatenate(halo, axis=0))
    table_ref[...] = split(fold(mul(halo_split, mix_ref[0])))
    gain = egain_ref[...]

    def live(i):
        row = lax.broadcasted_iota(jnp.int32, (HID, HID), 0)
        blocks = BLOCK // HID
        return jnp.concatenate([row < count_ref[i * blocks + j] for j in range(blocks)], axis=0)

    for i in range(EDGES // BLOCK):
        rows = slice(i * BLOCK, (i + 1) * BLOCK)
        hot = hot_rows(send_ref[rows, :], HALO, CELLS)
        preact = pre_ref[rows, :] + fold(mul(hot, table_ref[...]))
        hidden, slope = silu_parts(preact)
        hidden = split(hidden)
        hid_ref[rows, :] = hidden
        slope_ref[rows, :] = slope
        value = fold(mul(hidden, mix_ref[1]))
        inv = lax.rsqrt(jnp.mean(value * value, axis=1, keepdims=True) + NORM_EPS)
        norm = value * inv
        norm_ref[rows, :] = norm
        inv_ref[rows, :] = jnp.broadcast_to(inv, norm.shape)
        message = jnp.where(live(i), norm * gain, 0.0)
        term = mul(hot_columns(receiver_ref, i * (BLOCK // HID), CELLS), split(message))
        sum_ref[...] = term if i == 0 else sum_ref[...] + term

    node_split = split(node_ref[...])
    summed = split(fold(sum_ref[...]))
    hidden, slope = silu_parts(node_pre_ref[...] + fold(mul(summed, mix_ref[3])))
    hidden = split(hidden)
    value = fold(mul(hidden, mix_ref[4]))
    inv = lax.rsqrt(jnp.mean(value * value, axis=1, keepdims=True) + NORM_EPS)
    norm = value * inv
    cot = node_cot_ref[...]
    dnorm = cot * ngain_ref[...]
    dvalue = split(inv * (dnorm - norm * jnp.mean(dnorm * norm, axis=1, keepdims=True)))
    dpre = fold(mul(dvalue, mix_ref[5])) * slope
    dpre_split = split(dpre)
    table_ref[:CELLS, :] = split(fold(mul(dpre_split, mix_ref[7])))
    base_ref[...] = cot + fold(mul(dpre_split, mix_ref[6]))
    rest_ref[0:HID, :] = quad(mul_rows(node_split, dpre_split))
    rest_ref[HID : 2 * HID, :] = quad(mul_rows(summed, dpre_split))
    rest_ref[2 * HID : 3 * HID, :] = centred(quad(mul_rows(hidden, dvalue)))
    rest_ref[3 * HID :, :] = jnp.zeros((HID, HID), F32)
    rest_ref[3 * HID + 2 : 3 * HID + 3, :] = jnp.sum(dpre, axis=0, keepdims=True)
    rest_ref[3 * HID + 3 : 3 * HID + 4, :] = jnp.sum(cot * norm, axis=0, keepdims=True)

    bias_grad = gain_grad = jnp.zeros((1, HID), F32)
    for i in range(EDGES // BLOCK):
        rows = slice(i * BLOCK, (i + 1) * BLOCK)
        hot = hot_rows(recv_ref[rows, :], CELLS)
        grad = cot_ref[rows, :] + fold(mul(hot, table_ref[:CELLS, :]))
        grad = jnp.where(live(i), grad, 0.0)
        norm = norm_ref[rows, :]
        dnorm = grad * gain
        dvalue = inv_ref[rows, :] * (dnorm - norm * jnp.mean(dnorm * norm, axis=1, keepdims=True))
        dvalue = split(dvalue)
        dpre = fold(mul(dvalue, mix_ref[2])) * slope_ref[rows, :]
        dpre_ref[rows, :] = dpre
        dpre_split = split(dpre)
        first = i * (BLOCK // HID)
        terms = (
            mul(hot_columns(order_ref, first, CELLS + HALO), dpre_split),
            mul(hot_columns(receiver_ref, first, CELLS), dpre_split),
            mul_rows(hid_ref[rows, :], dvalue),
            mul_rows(split(edge_ref[rows, :]), dpre_split),
        )
        targets = (row_ref, sum_ref, acc_ref.at[0], acc_ref.at[1])
        for target, term in zip(targets, terms):
            target[...] = term if i == 0 else target[...] + term
        bias_grad += jnp.sum(dpre, axis=0, keepdims=True)
        gain_grad += jnp.sum(grad * norm, axis=0, keepdims=True)
    own_ref[...] = fold(row_ref[:CELLS, :])
    got_ref[...] = fold(sum_ref[...])
    for k, ref in enumerate((back0_ref, back1_ref, back2_ref)):
        start = CELLS + k * SLAB
        ref[...] = fold(row_ref[start : start + SLAB, :])
    rest_ref[3 * HID : 3 * HID + 1, :] = bias_grad
    rest_ref[3 * HID + 1 : 3 * HID + 2, :] = gain_grad


def weight_kernel(
    node_ref,
    halo0_ref,
    halo1_ref,
    halo2_ref,
    back0_ref,
    back1_ref,
    back2_ref,
    own_ref,
    got_ref,
    acc_ref,
    rest_ref,
    keep_ref,
    give_ref,
    grads_ref,
):
    node_split = split(node_ref[...])
    sent = quad(mul_rows(node_split, split(own_ref[...])))
    for halo, back in ((halo0_ref, back0_ref), (halo1_ref, back1_ref), (halo2_ref, back2_ref)):
        sent += quad(mul_rows(split(halo[...]), split(back[...])))
    grads_ref[0, 0:HID, :] = quad(acc_ref[1])
    grads_ref[0, HID : 2 * HID, :] = sent
    grads_ref[0, 2 * HID : 3 * HID, :] = quad(mul_rows(node_split, split(got_ref[...])))
    grads_ref[0, 3 * HID :, :] = centred(quad(acc_ref[0]))
    grads_ref[1] = rest_ref[...]
    side = parity(2)
    keep_ref[...] = grads_ref[side]
    give_ref[:CELLS, :] = grads_ref[1 - side]
    give_ref[CELLS:, :] = back0_ref[...]


def spread_kernel(terms_ref, out_ref):
    total = terms_ref[0]
    for k in range(1, terms_ref.shape[0]):
        total += terms_ref[k]
    for k in range(out_ref.shape[0]):
        out_ref[k] = total


def add_kernel(keep_ref, taken_ref, out_ref):
    out_ref[...] = keep_ref[...] + taken_ref[:CELLS, :]


def edge_kernel(cot_ref, dpre_ref, base_ref, own_ref, got_ref, weight_ref, edge_ref, part_ref):
    first = mix(jnp.transpose(weight_ref[:HID, :]))

    def step(i, carry):
        rows = pl.ds(pl.multiple_of(i * BLOCK, BLOCK), BLOCK)
        edge_ref[rows, :] = cot_ref[rows, :] + fold(mul(split(dpre_ref[rows, :]), first))
        return carry

    lax.fori_loop(0, EDGES // BLOCK, step, 0)
    second = mix(jnp.transpose(weight_ref[HID : 2 * HID, :]))
    third = mix(jnp.transpose(weight_ref[2 * HID :, :]))
    value = mul(split(own_ref[...]), second) + mul(split(got_ref[...]), third)
    part_ref[...] = base_ref[...] + fold(value)


def node_kernel(
    lists_ref, first_ref, mid_ref, second_ref, part_ref, weight_ref, out_ref, index_ref
):
    back = jnp.concatenate([first_ref[...], mid_ref[...], second_ref[...]], axis=0)
    summed = fold(mul_rows(list_rows(lists_ref, index_ref), split(back)))
    turned = mix(jnp.transpose(weight_ref[HID : 2 * HID, :]))
    out_ref[...] = part_ref[...] + fold(mul(split(summed), turned))


def finish_kernel(
    part_ref, other_ref, ein_ref, eout_ref, nin_ref, nout_ref, eb, eg, nb, ng, *, scale
):
    mine = parity(2) == 0
    part, other = part_ref[...] * scale, other_ref[...] * scale
    low = jnp.where(mine, part, other)
    high = jnp.where(mine, other, part)
    ein_ref[...] = low[: 3 * HID]
    eout_ref[...] = low[3 * HID :]
    nin_ref[...] = high[: 2 * HID]
    nout_ref[...] = high[2 * HID : 3 * HID]
    for k, ref in enumerate((eb, eg, nb, ng)):
        ref[...] = high[3 * HID + k : 3 * HID + k + 1]


def call(body, outs, ins, scratch=(), smem=(), flops=0, limit=12):
    outs = [out if isinstance(out[0], tuple) else (out, F32) for out in outs]
    shapes = [jax.ShapeDtypeStruct(shape, kind) for shape, kind in outs]
    size = 4 * sum(math.prod(shape) for shape, _ in outs) + sum(4 * v.size for v in ins)
    return pl.pallas_call(
        body,
        out_shape=shapes,
        in_specs=[SMEM] * len(smem) + [VMEM] * len(ins),
        out_specs=[VMEM] * len(outs),
        scratch_shapes=[pltpu.VMEM(shape, kind) for shape, kind in scratch],
        cost_estimate=pl.CostEstimate(flops=flops, bytes_accessed=size, transcendentals=0),
        compiler_params=pltpu.CompilerParams(vmem_limit_bytes=limit * 1024 * 1024),
    )(*smem, *ins)


def make_packets(node_feat, lists):
    return call(
        packet_kernel,
        [(SLAB, HID)] * 3,
        [node_feat, lists],
        scratch=[((SLOT, HID), jnp.int32)],
        flops=10**9,
    )


def regroup(pieces, chunk):
    body = functools.partial(regroup_kernel, chunk=chunk)
    return call(body, [(SLAB, HID)] * 3, pieces)


def edge_before(*operands):
    wide = (EDGES, HID)
    return call(
        before_kernel,
        [
            wide,
            (CELLS, HID),
            (wide, jnp.int32),
            (wide, jnp.int32),
            ((EDGES // HID, HID), jnp.int32),
            ((8, 2 * HID, 2 * HID), BF16),
        ],
        operands,
        flops=3 * 10**9,
        limit=20,
    )


def main_step(count, operands):
    square = (2 * HID, 2 * HID)
    wide = (EDGES, HID)
    return call(
        main_kernel,
        [(SLAB, HID)] * 3 + [(CELLS, HID)] * 3 + [wide, (2, *square), (CELLS, HID)],
        operands,
        scratch=[
            ((EDGES, 2 * HID), BF16),
            (wide, F32),
            (wide, F32),
            (wide, F32),
            ((CELLS, 2 * HID), F32),
            ((HALO, 2 * HID), BF16),
            ((CELLS + HALO, 2 * HID), F32),
        ],
        smem=[count],
        flops=10**10,
        limit=28,
    )


def weight_step(*operands):
    return call(
        weight_kernel,
        [(CELLS, HID), (CELLS + SLAB, HID)],
        operands,
        scratch=[((2, CELLS, HID), F32)],
        flops=10**9,
    )


def edge_after(cot, dpre, base, own, got, weight):
    return call(
        edge_kernel,
        [(EDGES, HID), (CELLS, HID)],
        [cot, dpre, base, own, got, weight],
        flops=10**9,
    )


def node_after(lists, back, part, weight):
    return call(
        node_kernel,
        [(CELLS, HID)],
        [lists, *back, part, weight],
        scratch=[((SLOT, HID), jnp.int32)],
        flops=10**9,
    )[0]


def finish(part, other, scale):
    shapes = [(3 * HID, HID), (HID, HID), (2 * HID, HID), (HID, HID)] + [(1, HID)] * 4
    return call(
        functools.partial(finish_kernel, scale=scale), shapes, [part, other], flops=10**6
    )


def swaps(axis):
    peers = lax.axis_size(axis)
    pairs = [[(i, i + 1) for i in range(start, peers - 1, 2)] for start in (0, 1)]
    return [sorted(some + [(j, i) for i, j in some]) for some in pairs]


def trade(first, second, axis):
    near, far = swaps(axis)
    second = lax.ppermute(second, axis, far)
    return lax.ppermute(first, axis, near), second


def join(values):
    return lax.optimization_barrier(values)


def sum_spread(terms, copies):
    return call(spread_kernel, [(copies, *terms.shape[1:])], [terms])[0]


def scatter_half(part):
    return lax.all_to_all(part.reshape(32, 16, HID), ("x", "zl", "zh"), 0, 0)


def every_term(terms):
    return lax.all_to_all(sum_spread(terms, 8), "y", 0, 0)


def gather_half(terms):
    part = lax.all_to_all(sum_spread(terms, 32), ("x", "zl", "zh"), 0, 0)
    return part.reshape(CELLS, HID)


def on_device(
    node_feat,
    edge_feat,
    node_cot,
    edge_cot,
    sender,
    receiver,
    block_count,
    send_rows,
    edge_in_weight,
    edge_bias,
    edge_out_weight,
    edge_gain,
    node_in_weight,
    node_bias,
    node_out_weight,
    node_gain,
):
    scale = 1.0 / math.sqrt(lax.axis_size(AXES) * EDGES)
    sender = sender.reshape(EDGES // HID, HID)
    receiver = receiver.reshape(EDGES // HID, HID)
    edge_bias, edge_gain, node_bias, node_gain = (
        row.reshape(1, HID) for row in (edge_bias, edge_gain, node_bias, node_gain)
    )
    first, mid, second = make_packets(node_feat, send_rows)
    first, second = trade(first, second, GX)
    before = edge_before(
        node_feat,
        edge_feat,
        sender,
        receiver,
        edge_in_weight,
        edge_bias,
        edge_out_weight,
        node_in_weight,
        node_bias,
        node_out_weight,
    )
    first, second, before = join((first, second, before))
    first, mid, second = regroup((first, mid, second), 3 * SLOT)
    first, second = trade(first, second, GY)
    first, mid, second = regroup((first, mid, second), SLOT)
    first, second = trade(first, second, GZ)
    halo = (first, mid, second)
    rest = (receiver, node_feat, node_cot, edge_cot, edge_feat, edge_gain, node_gain)
    *back, own, got, base, dpre, square, rows = main_step(block_count, (*halo, *before, *rest))
    second = lax.ppermute(back[2], GZ, swaps(GZ)[1])
    keep, give = weight_step(node_feat, *halo, *back, own, got, square, rows)
    mid = back[1]
    taken = lax.ppermute(give, "c", SWAP)
    part = scatter_half(call(add_kernel, [(CELLS, HID)], [keep, taken])[0])
    edge_grad, own_part = edge_after(edge_cot, dpre, base, own, got, edge_in_weight)
    first, mid, second = regroup((taken, mid, second), SLOT)
    part, first, mid, second, edge_grad, own_part = join(
        (part, first, mid, second, edge_grad, own_part)
    )
    part = every_term(part)
    first, second = trade(first, second, GY)
    first, mid, second = regroup((first, mid, second), 3 * SLOT)
    part, first, mid, second = join((part, first, mid, second))
    part = gather_half(part)
    first, second = trade(first, second, GX)
    node_grad = node_after(send_rows, (first, mid, second), own_part, edge_in_weight)
    part, node_grad = join((part, node_grad))
    other = lax.ppermute(part, "c", SWAP)
    ein, eout, nin, nout, eb, eg, nb, ng = finish(part, other, scale)
    vectors = [row.reshape(HID) for row in (eb, eg, nb, ng)]
    return (
        node_grad,
        edge_grad,
        ein,
        vectors[0],
        eout,
        vectors[1],
        nin,
        vectors[2],
        nout,
        vectors[3],
    )


def solution(mesh):
    fine = jax.sharding.Mesh(mesh.devices.reshape(SPLIT), AXES)
    return jax.shard_map(
        on_device,
        mesh=fine,
        in_specs=(
            P(AXES, None),
            P(AXES, None),
            P(AXES, None),
            P(AXES, None),
            P(AXES),
            P(AXES),
            P(AXES),
            P(GX, GY, GZ, None),
            P(),
            P(),
            P(),
            P(),
            P(),
            P(),
            P(),
            P(),
        ),
        out_specs=(
            P(AXES, None),
            P(AXES, None),
            P(),
            P(),
            P(),
            P(),
            P(),
            P(),
            P(),
            P(),
        ),
        check_vma=False,
    )
```

time: 149 us -> 134 us (0.90)
  waiting for transfers between devices: 30.5 us -> 22.7 us
  starting transfers between devices: 74.1 us -> 81.2 us
  local copies, waits for them, and re-layouts: 13.8 us -> 6.83 us
  other arithmetic: 4.23 us -> 0 us
  Pallas kernels: 21.8 us -> 20.1 us
    all_to_all x3, starting transfers between devices: 25.6 us -> 31.8 us  [the longest x1 17 us: scatter_half(): return lax.all_to_all(part.reshape(32, 16, HID), ('x', 'zl', 'zh'), 0, 0)]
    ppermute x14 -> x13, waiting for transfers between devices: 20 us -> 14.4 us  [the longest x5 5.43 us: trade(): return (lax.ppermute(first, axis, near), second)]
    unnamed x56 -> x52, local copies, waits for them, and re-layouts: 10.6 us -> 6.83 us
    another operation x12 -> x0, other arithmetic: 3.45 us -> none  [the longest x3 1.36 us: exchange_back(): jnp.stack([piece[:, k] for piece in pieces], axis=1)]
    all_to_all x3, waiting for transfers between devices: 10.6 us -> 8.31 us  [the longest x1 7.17 us: every_term(): return lax.all_to_all(sum_spread(terms, 8), 'y', 0, 0)]
    pallas_call x6 -> x14, Pallas kernels: 21.8 us -> 20.1 us  [call(): pl.pallas_call(body, out_shape=shapes, in_specs=[SMEM] * len(smem) + [VME...]
    ppermute x14 -> x13, starting transfers between devices: 48.6 us -> 49.4 us  [the longest x5 23.1 us: trade(): return (lax.ppermute(first, axis, near), second)]
  transfers between devices with their start and end apart: 17 -> 16, of which waited for: 9 -> 8; matrix products, arithmetic and copies ran while one was open for 4% -> 0% of each run, Pallas kernels for 5% -> 5%
where the time goes in v3:
time: 134 us; the launch traced here: 132 us
  starting transfers between devices  81.2 us (61%)
  waiting for transfers between devices  22.7 us (17%)
  Pallas kernels  20.1 us (15%)
  local copies, waits for them, and re-layouts  6.83 us (5%)
    ppermute x5, starting transfers between devices, trade(): return (lax.ppermute(first, axis, near), second)  23.1 us
    pallas_call x14, Pallas kernels, call(): pl.pallas_call(body, out_shape=shapes, in_specs=[SMEM] * len(smem) + [VME...  20.1 us
    all_to_all x1, starting transfers between devices, scatter_half(): return lax.all_to_all(part.reshape(32, 16, HID), ('x', 'zl', 'zh'), 0, 0)  17 us
    ppermute x5, starting transfers between devices, trade(): second = lax.ppermute(second, axis, far)  8.47 us
    all_to_all x1, starting transfers between devices, every_term(): return lax.all_to_all(sum_spread(terms, 8), 'y', 0, 0)  8.4 us
    ppermute x1, starting transfers between devices, on_device(): other = lax.ppermute(part, 'c', SWAP)  8.03 us
    ppermute x1, starting transfers between devices, on_device(): second = lax.ppermute(back[2], GZ, swaps(GZ)[1])  7.86 us
    all_to_all x1, waiting for transfers between devices, every_term(): return lax.all_to_all(sum_spread(terms, 8), 'y', 0, 0)  7.17 us
  transfers between devices with their start and end apart: 16, of which 8 were waited for; matrix products, arithmetic and copies ran while one was open for 0% of the time, Pallas kernels for 5%

profile of v3, /device:TPU:1, one launch (start us, length us, event | category | flops | bytes accessed | tf_op | source)
XLA Modules:
  0.0 131.9 jit_solution(8483328927309939695)
XLA Ops:
  0.7 1.0 copy-done.3
  1.7 0.7 copy-done.9
  2.4 0.5 shard_map.231
  3.0 4.8 %collective-permute-start = (f32[288,128]{1,0:T(8,128)S(1)}, f32[288,128]{1,0:T(8,128)S(1)}, u32[]{:S(2)}, u32[]{:S(2)}) collective-permute-start(f32[288,128]{1,0:T(8,128)S(1)} %get-tuple-element.72), channel_id=1, source_target_pairs={{0,16},{16,0},{32,48},{48,32},{64,80},{80,64},{96,112},{112,96},{1... | collective-permute-start | bytes 442376 | tf_op jit(solution)/shard_map/ppermute | solution.py:501
  7.8 0.7 collective-permute-start.1
  8.6 0.6 copy-done.13
  9.2 0.0 copy-done.14
  9.2 2.1 %shard_map.232 = (f32[2048,128]{1,0:T(8,128)S(1)}, f32[512,128]{1,0:T(8,128)S(1)}, s32[2048,128]{1,0:T(8,128)S(1)}, s32[2048,128]{1,0:T(8,128)S(1)}, s32[16,128]...) custom-call(f32[512,128]{1,0:T(8,128)S(1)} %copy-done.4, f32[2048,128]{1,0:T(8,128)S(1)} %copy-done, s32[16,128]{1,0:T(8,128)S(1)} %bitcast.14, ...), custom_call_target="tpu_custom_call" | custom-call | flops 3000000000 | bytes 7300096 | tf_op jit(solution)/shard_map/pallas_call | solution.py:390
  11.3 3.4 %collective-permute-start.2 = (f32[288,128]{1,0:T(8,128)S(1)}, f32[288,128]{1,0:T(8,128)S(1)}, u32[]{:S(2)}, u32[]{:S(2)}) collective-permute-start(f32[288,128]{1,0:T(8,128)S(1)} %get-tuple-element.83), channel_id=1, source_target_pairs={{0,4},{4,0},{8,12},{12,8},{1,5},{5,1},{9,13},{13,9},{2,6},{6,2},{1... | collective-permute-start | bytes 442376 | tf_op jit(solution)/shard_map/ppermute | solution.py:501
  14.7 0.7 collective-permute-start.3
  15.4 2.0 %collective-permute-done.2.in0 = f32[288,128]{1,0:T(8,128)S(1)} collective-permute-done((f32[288,128]{1,0:T(8,128)S(1)}, f32[288,128]{1,0:T(8,128)S(1)}, u32[]{:S(2)}, u32[]{:S(2)}) %collective-permute-start.2) | collective-permute-done | bytes 147488 | tf_op jit(solution)/shard_map/ppermute | solution.py:501
  17.4 8.7 %collective-permute-start.4 = (f32[288,128]{1,0:T(8,128)S(1)}, f32[288,128]{1,0:T(8,128)S(1)}, u32[]{:S(2)}, u32[]{:S(2)}) collective-permute-start(f32[288,128]{1,0:T(8,128)S(1)} %get-tuple-element.86), channel_id=1, source_target_pairs={{0,1},{1,0},{2,3},{3,2},{4,5},{5,4},{6,7},{7,6},{8,9},{9,8},{10,11... | collective-permute-start | bytes 442376 | tf_op jit(solution)/shard_map/ppermute | solution.py:501
  26.1 5.8 %collective-permute-start.5 = (f32[288,128]{1,0:T(8,128)S(1)}, f32[288,128]{1,0:T(8,128)S(1)}, u32[]{:S(2)}, u32[]{:S(2)}) collective-permute-start(f32[288,128]{1,0:T(8,128)S(1)} %get-tuple-element.88), channel_id=1, source_target_pairs={{1,2},{2,1},{5,6},{6,5},{9,10},{10,9},{13,14},{14,13},{17,18},{18,... | collective-permute-start | bytes 442376 | tf_op jit(solution)/shard_map/ppermute | solution.py:500
  31.9 4.6 %collective-permute-done.5.halo2_ref = f32[288,128]{1,0:T(8,128)S(1)} collective-permute-done((f32[288,128]{1,0:T(8,128)S(1)}, f32[288,128]{1,0:T(8,128)S(1)}, u32[]{:S(2)}, u32[]{:S(2)}) %collective-permute-start.5) | collective-permute-done | bytes 147488 | tf_op jit(solution)/shard_map/ppermute | solution.py:500
  36.5 0.6 copy-done.15
  37.1 0.0 copy-done.16
  37.1 0.0 copy-done.17
  37.2 10.1 %shard_map.235 = (f32[288,128]{1,0:T(8,128)S(1)}, f32[288,128]{1,0:T(8,128)S(1)}, f32[288,128]{1,0:T(8,128)S(1)}, f32[512,128]{1,0:T(8,128)S(1)}, f32[512,128]{1...) custom-call(s32[16]{0:T(128)S(1)} %copy-done.15, ...), custom_call_target="tpu_custom_call" | custom-call | flops 10000000000 | bytes 11650048 | tf_op jit(solution)/shard_map/pallas_call | solution.py:390
  47.2 0.6 shard_map.236
  47.9 0.1 copy-done.20
  47.9 0.1 copy-done.22
  48.0 0.1 copy-done.24
  48.1 1.9 %collective-permute-start.6 = (f32[800,128]{1,0:T(8,128)S(1)}, f32[800,128]{1,0:T(8,128)S(1)}, u32[]{:S(2)}, u32[]{:S(2)}) collective-permute-start(f32[800,128]{1,0:T(8,128)S(1)} %get-tuple-element.103), channel_id=1, source_target_pairs={{0,1},{1,0},{2,3},{3,2},{4,5},{5,4},{6,7},{7,6},{8,9},{9,8},{10,11... | collective-permute-start | bytes 1228808 | tf_op jit(solution)/shard_map/ppermute | solution.py:574
  50.0 1.7 %collective-permute-done.6.taken_ref.in0 = f32[800,128]{1,0:T(8,128)S(1)} collective-permute-done((f32[800,128]{1,0:T(8,128)S(1)}, f32[800,128]{1,0:T(8,128)S(1)}, u32[]{:S(2)}, u32[]{:S(2)}) %collective-permute-start.6) | collective-permute-done | bytes 409632 | tf_op jit(solution)/shard_map/ppermute | solution.py:574
  51.7 0.7 shard_map.237
  52.5 17.0 %all-to-all-start = ((f32[32,16,128]{2,1,0:T(8,128)}), f32[32,16,128]{2,1,0:T(8,128)S(1)}, u32[]{:S(2)}, u32[]{:S(2)}) async-start(f32[32,16,128]{2,1,0:T(8,128)} %bitcast.6), calls=%async_computation | async-start | bytes 524288 | tf_op jit(solution)/shard_map/all_to_all | solution.py:513
  69.4 7.9 %collective-permute-start.7 = (f32[288,128]{1,0:T(8,128)S(1)}, f32[288,128]{1,0:T(8,128)S(1)}, u32[]{:S(2)}, u32[]{:S(2)}) collective-permute-start(f32[288,128]{1,0:T(8,128)S(1)} %get-tuple-element.97.back2_ref), channel_id=1, source_target_pairs={{1,2},{2,1},{5,6},{6,5},{9,10},{10,9},{13,14},{14,13},{17,18},{18,... | collective-permute-start | bytes 442376 | tf_op jit(solution)/shard_map/ppermute | solution.py:571
  77.3 0.9 copy-done.21
  78.3 0.9 copy-done.23
  79.2 0.9 copy-done.25
  80.2 2.0 %shard_map.239 = (f32[2048,128]{1,0:T(8,128)}, f32[512,128]{1,0:T(8,128)S(1)}) custom-call(f32[2048,128]{1,0:T(8,128)S(1)} %copy-done.1, f32[2048,128]{1,0:T(8,128)S(1)} %get-tuple-element.107.dpre_ref, f32[512,128]{1,0:T(8,128)S(1)} %copy-done.25, f32[512,128]{1,0:T(8,128)S(1)} %copy-done.21, f32[512,128]{1,0:T(8,128)S(1)} %copy-done.23, ...), custom_call_target="tpu_custom_call" | custom-call | flops 1000000000 | bytes 4390912 | tf_op jit(solution)/shard_map/pallas_call | solution.py:390
  82.2 0.7 copy-done.18
  82.9 1.5 %collective-permute-done.7.in2 = f32[288,128]{1,0:T(8,128)S(1)} collective-permute-done((f32[288,128]{1,0:T(8,128)S(1)}, f32[288,128]{1,0:T(8,128)S(1)}, u32[]{:S(2)}, u32[]{:S(2)}) %collective-permute-start.7) | collective-permute-done | bytes 147488 | tf_op jit(solution)/shard_map/ppermute | solution.py:571
  84.4 3.1 %collective-permute-start.8 = (f32[288,128]{1,0:T(8,128)S(1)}, f32[288,128]{1,0:T(8,128)S(1)}, u32[]{:S(2)}, u32[]{:S(2)}) collective-permute-start(f32[288,128]{1,0:T(8,128)S(1)} %get-tuple-element.112), channel_id=1, source_target_pairs={{0,4},{4,0},{8,12},{12,8},{1,5},{5,1},{9,13},{13,9},{2,6},{6,2},{1... | collective-permute-start | bytes 442376 | tf_op jit(solution)/shard_map/ppermute | solution.py:501
  87.5 0.7 collective-permute-start.9
  88.2 0.7 shard_map.240
  88.9 8.4 %all-to-all-start.1 = ((f32[8,16,128]{2,1,0:T(8,128)}), f32[8,16,128]{2,1,0:T(8,128)S(1)}, u32[]{:S(2)}, u32[]{:S(2)}) async-start(f32[8,16,128]{2,1,0:T(8,128)} %shard_map.240), calls=%async_computation.1 | async-start | bytes 131072 | tf_op jit(solution)/shard_map/all_to_all | solution.py:517
  97.3 7.2 %all-to-all-done.1.terms_ref = f32[8,16,128]{2,1,0:T(8,128)S(1)} async-done(((f32[8,16,128]{2,1,0:T(8,128)}), f32[8,16,128]{2,1,0:T(8,128)S(1)}, u32[]{:S(2)}, u32[]{:S(2)}) %all-to-all-start.1) | async-done | bytes 65568 | tf_op jit(solution)/shard_map/all_to_all | solution.py:517
  104.5 0.7 shard_map.242
  105.2 6.5 %all-to-all-start.2 = ((f32[32,16,128]{2,1,0:T(8,128)}), f32[32,16,128]{2,1,0:T(8,128)S(1)}, u32[]{:S(2)}, u32[]{:S(2)}) async-start(f32[32,16,128]{2,1,0:T(8,128)} %shard_map.242), calls=%async_computation.2 | async-start | bytes 524288 | tf_op jit(solution)/shard_map/all_to_all | solution.py:521
  111.7 3.1 %collective-permute-start.10 = (f32[288,128]{1,0:T(8,128)S(1)}, f32[288,128]{1,0:T(8,128)S(1)}, u32[]{:S(2)}, u32[]{:S(2)}) collective-permute-start(f32[288,128]{1,0:T(8,128)S(1)} %get-tuple-element.119), channel_id=1, source_target_pairs={{0,16},{16,0},{32,48},{48,32},{64,80},{80,64},{96,112},{112,96},{1... | collective-permute-start | bytes 442376 | tf_op jit(solution)/shard_map/ppermute | solution.py:501
  114.9 0.7 collective-permute-start.11
  115.5 3.4 %collective-permute-done.10.first_ref = f32[288,128]{1,0:T(8,128)S(1)} collective-permute-done((f32[288,128]{1,0:T(8,128)S(1)}, f32[288,128]{1,0:T(8,128)S(1)}, u32[]{:S(2)}, u32[]{:S(2)}) %collective-permute-start.10) | collective-permute-done | bytes 147488 | tf_op jit(solution)/shard_map/ppermute | solution.py:501
  119.0 1.7 %shard_map.243 = f32[512,128]{1,0:T(8,128)} custom-call(s32[3,3,3,32]{3,2,1,0:T(4,128)S(1)} %copy-done.10, f32[288,128]{1,0:T(8,128)S(1)} %collective-permute-done.10.first_ref, f32[288,128]{1,0:T(8,128)S(1)} %get-tuple-element.120.mid_ref, f32[288,128]{1,0:T(8,128)S(1)} %collective-permute-done.11.second_ref, f32[512,128]{1,0:T(8,128)S(1)} %copy-done.19, ...), custom_call_target="tpu_custom_call" | custom-call | flops 1000000000 | bytes 1166720 | tf_op jit(solution)/shard_map/pallas_call | solution.py:390
  120.7 1.1 all-to-all-done.2
  121.9 8.0 %collective-permute-start.12 = (f32[512,128]{1,0:T(8,128)S(1)}, f32[512,128]{1,0:T(8,128)S(1)}, u32[]{:S(2)}, u32[]{:S(2)}) collective-permute-start(f32[512,128]{1,0:T(8,128)S(1)} %bitcast.12), channel_id=1, source_target_pairs={{0,1},{1,0},{2,3},{3,2},{4,5},{5,4},{6,7},{7,6},{8,9},{9,8},{10,11... | collective-permute-start | bytes 786440 | tf_op jit(solution)/shard_map/ppermute | solution.py:589
  129.9 1.1 collective-permute-done.12.other_ref
  131.1 0.8 shard_map.244
  (50 shorter events, 0.2 us)
Async XLA Ops:
  0.6 7.9 %copy-start = (f32[2048,128]{1,0:T(8,128)S(1)}, f32[2048,128]{1,0:T(8,128)}, u32[]{:S(2)}) copy-start(f32[2048,128]{1,0:T(8,128)} %edge_ref.3) | copy-start | bytes 3145732
  0.7 1.0 copy-start.3
  1.7 0.7 copy-start.9
  2.4 6.1 %copy-start.4 = (f32[512,128]{1,0:T(8,128)S(1)}, f32[512,128]{1,0:T(8,128)}, u32[]{:S(2)}) copy-start(f32[512,128]{1,0:T(8,128)} %node_ref.7) | copy-start | bytes 786436
  2.4 6.2 %copy-start.5 = (f32[384,128]{1,0:T(8,128)S(1)}, f32[384,128]{1,0:T(8,128)}, u32[]{:S(2)}) copy-start(f32[384,128]{1,0:T(8,128)} %weight_ref.3) | copy-start | bytes 589828
  2.4 6.2 %copy-start.6 = (f32[256,128]{1,0:T(8,128)S(1)}, f32[256,128]{1,0:T(8,128)}, u32[]{:S(2)}) copy-start(f32[256,128]{1,0:T(8,128)} %nin_ref.1) | copy-start | bytes 393220
  2.4 6.2 %copy-start.7 = (f32[128,128]{1,0:T(8,128)S(1)}, f32[128,128]{1,0:T(8,128)}, u32[]{:S(2)}) copy-start(f32[128,128]{1,0:T(8,128)} %eout_ref.1) | copy-start | bytes 196612
  2.4 6.2 %copy-start.8 = (f32[128,128]{1,0:T(8,128)S(1)}, f32[128,128]{1,0:T(8,128)}, u32[]{:S(2)}) copy-start(f32[128,128]{1,0:T(8,128)} %nout_ref.1) | copy-start | bytes 196612
  2.4 6.2 %copy-start.12 = (s32[2048]{0:T(1024)S(1)}, s32[2048]{0:T(1024)}, u32[]{:S(2)}) copy-start(s32[2048]{0:T(1024)} %param.21) | copy-start | bytes 24580
  3.0 5.6 %copy-start.11 = (s32[2048]{0:T(1024)S(1)}, s32[2048]{0:T(1024)}, u32[]{:S(2)}) copy-start(s32[2048]{0:T(1024)} %param.20) | copy-start | bytes 24580
  3.0 8.3 %collective-permute-start = (f32[288,128]{1,0:T(8,128)S(1)}, f32[288,128]{1,0:T(8,128)S(1)}, u32[]{:S(2)}, u32[]{:S(2)}) collective-permute-start(f32[288,128]{1,0:T(8,128)S(1)} %get-tuple-element.72), channel_id=1, source_target_pairs={{0,16},{16,0},{32,48},{48,32},{64,80},{80,64},{96,112},{112,96},{1... | collective-permute-start | bytes 442376 | tf_op jit(solution)/shard_map/ppermute | solution.py:501
  7.8 3.4 %collective-permute-start.1 = (f32[288,128]{1,0:T(8,128)S(1)}, f32[288,128]{1,0:T(8,128)S(1)}, u32[]{:S(2)}, u32[]{:S(2)}) collective-permute-start(f32[288,128]{1,0:T(8,128)S(1)} %get-tuple-element.73), channel_id=1, source_target_pairs={{16,32},{32,16},{48,64},{64,48},{80,96},{96,80},{112,128},{128,112... | collective-permute-start | bytes 442376 | tf_op jit(solution)/shard_map/ppermute | solution.py:500
  8.5 0.7 copy-start.13
  8.5 0.7 copy-start.14
  9.2 27.3 %copy-start.1 = (f32[2048,128]{1,0:T(8,128)S(1)}, f32[2048,128]{1,0:T(8,128)}, u32[]{:S(2)}) copy-start(f32[2048,128]{1,0:T(8,128)} %cot_ref.3) | copy-start | bytes 3145732
  11.3 25.2 %copy-start.2 = (f32[512,128]{1,0:T(8,128)S(1)}, f32[512,128]{1,0:T(8,128)}, u32[]{:S(2)}) copy-start(f32[512,128]{1,0:T(8,128)} %node_cot_ref.1) | copy-start | bytes 786436
  11.3 6.0 %collective-permute-start.2 = (f32[288,128]{1,0:T(8,128)S(1)}, f32[288,128]{1,0:T(8,128)S(1)}, u32[]{:S(2)}, u32[]{:S(2)}) collective-permute-start(f32[288,128]{1,0:T(8,128)S(1)} %get-tuple-element.83), channel_id=1, source_target_pairs={{0,4},{4,0},{8,12},{12,8},{1,5},{5,1},{9,13},{13,9},{2,6},{6,2},{1... | collective-permute-start | bytes 442376 | tf_op jit(solution)/shard_map/ppermute | solution.py:501
  14.7 2.7 %collective-permute-start.3 = (f32[288,128]{1,0:T(8,128)S(1)}, f32[288,128]{1,0:T(8,128)S(1)}, u32[]{:S(2)}, u32[]{:S(2)}) collective-permute-start(f32[288,128]{1,0:T(8,128)S(1)} %get-tuple-element.85), channel_id=1, source_target_pairs={{4,8},{8,4},{5,9},{9,5},{6,10},{10,6},{7,11},{11,7},{20,24},{24,20... | collective-permute-start | bytes 442376 | tf_op jit(solution)/shard_map/ppermute | solution.py:500
  17.4 14.5 %collective-permute-start.4 = (f32[288,128]{1,0:T(8,128)S(1)}, f32[288,128]{1,0:T(8,128)S(1)}, u32[]{:S(2)}, u32[]{:S(2)}) collective-permute-start(f32[288,128]{1,0:T(8,128)S(1)} %get-tuple-element.86), channel_id=1, source_target_pairs={{0,1},{1,0},{2,3},{3,2},{4,5},{5,4},{6,7},{7,6},{8,9},{9,8},{10,11... | collective-permute-start | bytes 442376 | tf_op jit(solution)/shard_map/ppermute | solution.py:501
  26.1 10.4 %collective-permute-start.5 = (f32[288,128]{1,0:T(8,128)S(1)}, f32[288,128]{1,0:T(8,128)S(1)}, u32[]{:S(2)}, u32[]{:S(2)}) collective-permute-start(f32[288,128]{1,0:T(8,128)S(1)} %get-tuple-element.88), channel_id=1, source_target_pairs={{1,2},{2,1},{5,6},{6,5},{9,10},{10,9},{13,14},{14,13},{17,18},{18,... | collective-permute-start | bytes 442376 | tf_op jit(solution)/shard_map/ppermute | solution.py:500
  36.5 0.7 copy-start.15
  36.5 0.7 copy-start.16
  36.5 0.7 copy-start.17
  47.2 0.7 copy-start.20
  47.2 0.8 copy-start.22
  47.2 0.9 copy-start.24
  48.1 3.6 %collective-permute-start.6 = (f32[800,128]{1,0:T(8,128)S(1)}, f32[800,128]{1,0:T(8,128)S(1)}, u32[]{:S(2)}, u32[]{:S(2)}) collective-permute-start(f32[800,128]{1,0:T(8,128)S(1)} %get-tuple-element.103), channel_id=1, source_target_pairs={{0,1},{1,0},{2,3},{3,2},{4,5},{5,4},{6,7},{7,6},{8,9},{9,8},{10,11... | collective-permute-start | bytes 1228808 | tf_op jit(solution)/shard_map/ppermute | solution.py:574
  52.5 32.0 %all-to-all-start = ((f32[32,16,128]{2,1,0:T(8,128)}), f32[32,16,128]{2,1,0:T(8,128)S(1)}, u32[]{:S(2)}, u32[]{:S(2)}) async-start(f32[32,16,128]{2,1,0:T(8,128)} %bitcast.6), calls=%async_computation | async-start | bytes 524288 | tf_op jit(solution)/shard_map/all_to_all | solution.py:513
  69.4 15.0 %collective-permute-start.7 = (f32[288,128]{1,0:T(8,128)S(1)}, f32[288,128]{1,0:T(8,128)S(1)}, u32[]{:S(2)}, u32[]{:S(2)}) collective-permute-start(f32[288,128]{1,0:T(8,128)S(1)} %get-tuple-element.97.back2_ref), channel_id=1, source_target_pairs={{1,2},{2,1},{5,6},{6,5},{9,10},{10,9},{13,14},{14,13},{17,18},{18,... | collective-permute-start | bytes 442376 | tf_op jit(solution)/shard_map/ppermute | solution.py:571
  77.3 1.0 copy-start.21
  78.3 0.9 copy-start.23
  79.2 0.9 copy-start.25
  82.2 0.7 copy-start.18
  84.4 12.9 %collective-permute-start.8 = (f32[288,128]{1,0:T(8,128)S(1)}, f32[288,128]{1,0:T(8,128)S(1)}, u32[]{:S(2)}, u32[]{:S(2)}) collective-permute-start(f32[288,128]{1,0:T(8,128)S(1)} %get-tuple-element.112), channel_id=1, source_target_pairs={{0,4},{4,0},{8,12},{12,8},{1,5},{5,1},{9,13},{13,9},{2,6},{6,2},{1... | collective-permute-start | bytes 442376 | tf_op jit(solution)/shard_map/ppermute | solution.py:501
  87.5 9.8 %collective-permute-start.9 = (f32[288,128]{1,0:T(8,128)S(1)}, f32[288,128]{1,0:T(8,128)S(1)}, u32[]{:S(2)}, u32[]{:S(2)}) collective-permute-start(f32[288,128]{1,0:T(8,128)S(1)} %get-tuple-element.114), channel_id=1, source_target_pairs={{4,8},{8,4},{5,9},{9,5},{6,10},{10,6},{7,11},{11,7},{20,24},{24,20... | collective-permute-start | bytes 442376 | tf_op jit(solution)/shard_map/ppermute | solution.py:500
  88.9 15.6 %all-to-all-start.1 = ((f32[8,16,128]{2,1,0:T(8,128)}), f32[8,16,128]{2,1,0:T(8,128)S(1)}, u32[]{:S(2)}, u32[]{:S(2)}) async-start(f32[8,16,128]{2,1,0:T(8,128)} %shard_map.240), calls=%async_computation.1 | async-start | bytes 131072 | tf_op jit(solution)/shard_map/all_to_all | solution.py:517
  105.2 13.8 %copy-start.10 = (s32[3,3,3,32]{3,2,1,0:T(4,128)S(1)}, s32[3,3,3,32]{3,2,1,0:T(4,128)}, u32[]{:S(2)}) copy-start(s32[3,3,3,32]{3,2,1,0:T(4,128)} %lists_ref.3) | copy-start | bytes 10372
  105.2 13.8 %copy-start.19 = (f32[512,128]{1,0:T(8,128)S(1)}, f32[512,128]{1,0:T(8,128)}, u32[]{:S(2)}) copy-start(f32[512,128]{1,0:T(8,128)} %copy-done.18) | copy-start | bytes 786436
  105.2 16.6 %all-to-all-start.2 = ((f32[32,16,128]{2,1,0:T(8,128)}), f32[32,16,128]{2,1,0:T(8,128)S(1)}, u32[]{:S(2)}, u32[]{:S(2)}) async-start(f32[32,16,128]{2,1,0:T(8,128)} %shard_map.242), calls=%async_computation.2 | async-start | bytes 524288 | tf_op jit(solution)/shard_map/all_to_all | solution.py:521
  111.7 7.3 %collective-permute-start.10 = (f32[288,128]{1,0:T(8,128)S(1)}, f32[288,128]{1,0:T(8,128)S(1)}, u32[]{:S(2)}, u32[]{:S(2)}) collective-permute-start(f32[288,128]{1,0:T(8,128)S(1)} %get-tuple-element.119), channel_id=1, source_target_pairs={{0,16},{16,0},{32,48},{48,32},{64,80},{80,64},{96,112},{112,96},{1... | collective-permute-start | bytes 442376 | tf_op jit(solution)/shard_map/ppermute | solution.py:501
  114.9 4.1 %collective-permute-start.11 = (f32[288,128]{1,0:T(8,128)S(1)}, f32[288,128]{1,0:T(8,128)S(1)}, u32[]{:S(2)}, u32[]{:S(2)}) collective-permute-start(f32[288,128]{1,0:T(8,128)S(1)} %get-tuple-element.121), channel_id=1, source_target_pairs={{16,32},{32,16},{48,64},{64,48},{80,96},{96,80},{112,128},{128,112... | collective-permute-start | bytes 442376 | tf_op jit(solution)/shard_map/ppermute | solution.py:500
  121.9 9.2 %collective-permute-start.12 = (f32[512,128]{1,0:T(8,128)S(1)}, f32[512,128]{1,0:T(8,128)S(1)}, u32[]{:S(2)}, u32[]{:S(2)}) collective-permute-start(f32[512,128]{1,0:T(8,128)S(1)} %bitcast.12), channel_id=1, source_target_pairs={{0,1},{1,0},{2,3},{3,2},{4,5},{5,4},{6,7},{7,6},{8,9},{9,8},{10,11... | collective-permute-start | bytes 786440 | tf_op jit(solution)/shard_map/ppermute | solution.py:589

commit v4 on v3

--- a/solution.py
+++ b/solution.py
@@ -182,6 +182,7 @@
     mix_ref[5] = mix(jnp.transpose(node_out))
     mix_ref[6] = mix(jnp.transpose(nin_ref[:HID, :]))
     mix_ref[7] = mix(jnp.transpose(nin_ref[HID:, :]))
+    mix_ref[8] = mix(jnp.transpose(ein_ref[:HID, :]))
 
 
 def main_kernel(
@@ -208,7 +209,7 @@
     own_ref,
     got_ref,
     base_ref,
-    dpre_ref,
+    edge_grad_ref,
     acc_ref,
     rest_ref,
     hid_ref,
@@ -278,8 +279,8 @@
         dvalue = inv_ref[rows, :] * (dnorm - norm * jnp.mean(dnorm * norm, axis=1, keepdims=True))
         dvalue = split(dvalue)
         dpre = fold(mul(dvalue, mix_ref[2])) * slope_ref[rows, :]
-        dpre_ref[rows, :] = dpre
         dpre_split = split(dpre)
+        edge_grad_ref[rows, :] = cot_ref[rows, :] + fold(mul(dpre_split, mix_ref[8]))
         first = i * (BLOCK // HID)
         terms = (
             mul(hot_columns(order_ref, first, CELLS + HALO), dpre_split),
@@ -344,28 +345,23 @@
     out_ref[...] = keep_ref[...] + taken_ref[:CELLS, :]
 
 
-def edge_kernel(cot_ref, dpre_ref, base_ref, own_ref, got_ref, weight_ref, edge_ref, part_ref):
-    first = mix(jnp.transpose(weight_ref[:HID, :]))
-
-    def step(i, carry):
-        rows = pl.ds(pl.multiple_of(i * BLOCK, BLOCK), BLOCK)
-        edge_ref[rows, :] = cot_ref[rows, :] + fold(mul(split(dpre_ref[rows, :]), first))
-        return carry
-
-    lax.fori_loop(0, EDGES // BLOCK, step, 0)
-    second = mix(jnp.transpose(weight_ref[HID : 2 * HID, :]))
-    third = mix(jnp.transpose(weight_ref[2 * HID :, :]))
-    value = mul(split(own_ref[...]), second) + mul(split(got_ref[...]), third)
-    part_ref[...] = base_ref[...] + fold(value)
-
-
 def node_kernel(
-    lists_ref, first_ref, mid_ref, second_ref, part_ref, weight_ref, out_ref, index_ref
+    lists_ref,
+    first_ref,
+    mid_ref,
+    second_ref,
+    base_ref,
+    own_ref,
+    got_ref,
+    weight_ref,
+    out_ref,
+    index_ref,
 ):
     back = jnp.concatenate([first_ref[...], mid_ref[...], second_ref[...]], axis=0)
-    summed = fold(mul_rows(list_rows(lists_ref, index_ref), split(back)))
-    turned = mix(jnp.transpose(weight_ref[HID : 2 * HID, :]))
-    out_ref[...] = part_ref[...] + fold(mul(split(summed), turned))
+    sent = own_ref[...] + fold(mul_rows(list_rows(lists_ref, index_ref), split(back)))
+    value = mul(split(sent), mix(jnp.transpose(weight_ref[HID : 2 * HID, :])))
+    value += mul(split(got_ref[...]), mix(jnp.transpose(weight_ref[2 * HID :, :])))
+    out_ref[...] = base_ref[...] + fold(value)
 
 
 def finish_kernel(
@@ -408,9 +404,9 @@
     )
 
 
-def regroup(pieces, chunk):
+def regroup(pieces, chunk, flops=0):
     body = functools.partial(regroup_kernel, chunk=chunk)
-    return call(body, [(SLAB, HID)] * 3, pieces)
+    return call(body, [(SLAB, HID)] * 3, pieces, flops=flops)
 
 
 def edge_before(*operands):
@@ -423,7 +419,7 @@
             (wide, jnp.int32),
             (wide, jnp.int32),
             ((EDGES // HID, HID), jnp.int32),
-            ((8, 2 * HID, 2 * HID), BF16),
+            ((9, 2 * HID, 2 * HID), BF16),
         ],
         operands,
         flops=3 * 10**9,
@@ -459,26 +455,17 @@
         [(CELLS, HID), (CELLS + SLAB, HID)],
         operands,
         scratch=[((2, CELLS, HID), F32)],
-        flops=10**9,
-    )
-
-
-def edge_after(cot, dpre, base, own, got, weight):
-    return call(
-        edge_kernel,
-        [(EDGES, HID), (CELLS, HID)],
-        [cot, dpre, base, own, got, weight],
-        flops=10**9,
-    )
-
-
-def node_after(lists, back, part, weight):
+        flops=1000000000,
+    )
+
+
+def node_after(*operands):
     return call(
         node_kernel,
         [(CELLS, HID)],
-        [lists, *back, part, weight],
+        operands,
         scratch=[((SLOT, HID), jnp.int32)],
-        flops=10**9,
+        flops=1000000000000,
     )[0]
 
 
@@ -560,31 +547,32 @@
         node_bias,
         node_out_weight,
     )
-    first, second, before = join((first, second, before))
+    second, first, before = join((second, first, before))
     first, mid, second = regroup((first, mid, second), 3 * SLOT)
     first, second = trade(first, second, GY)
     first, mid, second = regroup((first, mid, second), SLOT)
     first, second = trade(first, second, GZ)
+    second, first = join((second, first))
     halo = (first, mid, second)
     rest = (receiver, node_feat, node_cot, edge_cot, edge_feat, edge_gain, node_gain)
-    *back, own, got, base, dpre, square, rows = main_step(block_count, (*halo, *before, *rest))
+    *back, own, got, base, edge_grad, square, rows = main_step(block_count, (*halo, *before, *rest))
+    keep, give = weight_step(node_feat, *halo, *back, own, got, square, rows)
+    taken = lax.ppermute(give, "c", SWAP)
+    part = call(add_kernel, [(CELLS, HID)], [keep, taken])[0]
+    part = scatter_half(part)
     second = lax.ppermute(back[2], GZ, swaps(GZ)[1])
-    keep, give = weight_step(node_feat, *halo, *back, own, got, square, rows)
-    mid = back[1]
-    taken = lax.ppermute(give, "c", SWAP)
-    part = scatter_half(call(add_kernel, [(CELLS, HID)], [keep, taken])[0])
-    edge_grad, own_part = edge_after(edge_cot, dpre, base, own, got, edge_in_weight)
-    first, mid, second = regroup((taken, mid, second), SLOT)
-    part, first, mid, second, edge_grad, own_part = join(
-        (part, first, mid, second, edge_grad, own_part)
-    )
+    first, mid, second = regroup((taken, back[1], second), SLOT, 1000000000000)
+    part, _ = join((part, mid))
     part = every_term(part)
     first, second = trade(first, second, GY)
-    first, mid, second = regroup((first, mid, second), 3 * SLOT)
+    first, mid, second = regroup((first, mid, second), 3 * SLOT, 0)
     part, first, mid, second = join((part, first, mid, second))
     part = gather_half(part)
     first, second = trade(first, second, GX)
-    node_grad = node_after(send_rows, (first, mid, second), own_part, edge_in_weight)
+    second, first = join((second, first))
+    node_grad = node_after(
+        send_rows, first, mid, second, base, own, got, edge_in_weight
+    )
     part, node_grad = join((part, node_grad))
     other = lax.ppermute(part, "c", SWAP)
     ein, eout, nin, nout, eb, eg, nb, ng = finish(part, other, scale)

time: 134 us -> 131 us (0.978)
  waiting for transfers between devices: 22.7 us -> 31.8 us
  starting transfers between devices: 81.2 us -> 74.1 us
  local copies, waits for them, and re-layouts: 6.83 us -> 2.01 us
    all_to_all x1, waiting for transfers between devices: 0.01 us -> 7.77 us  [scatter_half(): return lax.all_to_all(part.reshape(32, 16, HID), ('x', 'zl', 'zh'), 0, 0)]
    all_to_all x1, waiting for transfers between devices: 1.14 us -> 8.29 us  [gather_half(): part = lax.all_to_all(sum_spread(terms, 32), ('x', 'zl', 'zh'), 0, 0)]
    all_to_all x1, starting transfers between devices: 17 us -> 11.1 us  [scatter_half(): return lax.all_to_all(part.reshape(32, 16, HID), ('x', 'zl', 'zh'), 0, 0)]
    ppermute x5, starting transfers between devices: 8.47 us -> 13.8 us  [trade(): second = lax.ppermute(second, axis, far)]
    unnamed x52 -> x46, local copies, waits for them, and re-layouts: 6.83 us -> 2.01 us
    ppermute x5, waiting for transfers between devices: 4.58 us -> 0.81 us  [trade(): second = lax.ppermute(second, axis, far)]
    ppermute x5, starting transfers between devices: 23.1 us -> 19.8 us  [trade(): return (lax.ppermute(first, axis, near), second)]
    ppermute x1, starting transfers between devices: 8.03 us -> 6.04 us  [on_device(): other = lax.ppermute(part, 'c', SWAP)]
where the time goes in v4:
time: 131 us; the launch traced here: 130 us
  starting transfers between devices  74.1 us (57%)
  waiting for transfers between devices  31.8 us (24%)
  Pallas kernels  20.9 us (16%)
  local copies, waits for them, and re-layouts  2.01 us (2%)
    pallas_call x13, Pallas kernels, call(): pl.pallas_call(body, out_shape=shapes, in_specs=[SMEM] * len(smem) + [VME...  20.9 us
    ppermute x5, starting transfers between devices, trade(): return (lax.ppermute(first, axis, near), second)  19.8 us
    ppermute x5, starting transfers between devices, trade(): second = lax.ppermute(second, axis, far)  13.8 us
    all_to_all x1, starting transfers between devices, scatter_half(): return lax.all_to_all(part.reshape(32, 16, HID), ('x', 'zl', 'zh'), 0, 0)  11.1 us
    all_to_all x1, waiting for transfers between devices, gather_half(): part = lax.all_to_all(sum_spread(terms, 32), ('x', 'zl', 'zh'), 0, 0)  8.29 us
    all_to_all x1, waiting for transfers between devices, scatter_half(): return lax.all_to_all(part.reshape(32, 16, HID), ('x', 'zl', 'zh'), 0, 0)  7.77 us
    all_to_all x1, starting transfers between devices, every_term(): return lax.all_to_all(sum_spread(terms, 8), 'y', 0, 0)  7.57 us
    all_to_all x1, waiting for transfers between devices, every_term(): return lax.all_to_all(sum_spread(terms, 8), 'y', 0, 0)  7.18 us
  transfers between devices with their start and end apart: 16, of which 8 were waited for; matrix products, arithmetic and copies ran while one was open for 0% of the time, Pallas kernels for 5%

profile of v4, /device:TPU:1, one launch (start us, length us, event | category | flops | bytes accessed | tf_op | source)
XLA Modules:
  0.0 130.0 jit_solution(5808907386166856725)
XLA Ops:
  0.7 1.0 copy-done.3
  1.7 0.7 copy-done.10
  2.5 0.5 shard_map.231
  3.0 0.7 collective-permute-start
  3.7 8.2 %collective-permute-start.1 = (f32[288,128]{1,0:T(8,128)S(1)}, f32[288,128]{1,0:T(8,128)S(1)}, u32[]{:S(2)}, u32[]{:S(2)}) collective-permute-start(f32[288,128]{1,0:T(8,128)S(1)} %get-tuple-element.70), channel_id=1, source_target_pairs={{0,16},{16,0},{32,48},{48,32},{64,80},{80,64},{96,112},{112,96},{1... | collective-permute-start | bytes 442376 | tf_op jit(solution)/shard_map/ppermute | solution.py:488
  12.0 0.0 copy-start.1
  12.0 0.0 copy-start.2
  12.0 0.0 copy-start.16
  12.0 0.0 copy-start.17
  12.0 0.0 copy-start.18
  12.0 2.1 %shard_map.232 = (f32[2048,128]{1,0:T(8,128)S(1)}, f32[512,128]{1,0:T(8,128)S(1)}, s32[2048,128]{1,0:T(8,128)S(1)}, s32[2048,128]{1,0:T(8,128)S(1)}, s32[16,128]...) custom-call(f32[512,128]{1,0:T(8,128)S(1)} %copy-done.4, f32[2048,128]{1,0:T(8,128)S(1)} %copy-done, s32[16,128]{1,0:T(8,128)S(1)} %bitcast.12, ...), custom_call_target="tpu_custom_call" | custom-call | flops 3000000000 | bytes 7562240 | tf_op jit(solution)/shard_map/pallas_call | solution.py:386
  14.1 3.9 %collective-permute-done.1.in0 = f32[288,128]{1,0:T(8,128)S(1)} collective-permute-done((f32[288,128]{1,0:T(8,128)S(1)}, f32[288,128]{1,0:T(8,128)S(1)}, u32[]{:S(2)}, u32[]{:S(2)}) %collective-permute-start.1) | collective-permute-done | bytes 147488 | tf_op jit(solution)/shard_map/ppermute | solution.py:488
  18.1 3.1 %collective-permute-start.2 = (f32[288,128]{1,0:T(8,128)S(1)}, f32[288,128]{1,0:T(8,128)S(1)}, u32[]{:S(2)}, u32[]{:S(2)}) collective-permute-start(f32[288,128]{1,0:T(8,128)S(1)} %get-tuple-element.80), channel_id=1, source_target_pairs={{0,4},{4,0},{8,12},{12,8},{1,5},{5,1},{9,13},{13,9},{2,6},{6,2},{1... | collective-permute-start | bytes 442376 | tf_op jit(solution)/shard_map/ppermute | solution.py:488
  21.2 0.7 collective-permute-start.3
  21.9 2.1 %collective-permute-done.2.in0 = f32[288,128]{1,0:T(8,128)S(1)} collective-permute-done((f32[288,128]{1,0:T(8,128)S(1)}, f32[288,128]{1,0:T(8,128)S(1)}, u32[]{:S(2)}, u32[]{:S(2)}) %collective-permute-start.2) | collective-permute-done | bytes 147488 | tf_op jit(solution)/shard_map/ppermute | solution.py:488
  24.0 11.2 %collective-permute-start.4 = (f32[288,128]{1,0:T(8,128)S(1)}, f32[288,128]{1,0:T(8,128)S(1)}, u32[]{:S(2)}, u32[]{:S(2)}) collective-permute-start(f32[288,128]{1,0:T(8,128)S(1)} %get-tuple-element.83), channel_id=1, source_target_pairs={{1,2},{2,1},{5,6},{6,5},{9,10},{10,9},{13,14},{14,13},{17,18},{18,... | collective-permute-start | bytes 442376 | tf_op jit(solution)/shard_map/ppermute | solution.py:487
  35.1 2.1 %collective-permute-start.5 = (f32[288,128]{1,0:T(8,128)S(1)}, f32[288,128]{1,0:T(8,128)S(1)}, u32[]{:S(2)}, u32[]{:S(2)}) collective-permute-start(f32[288,128]{1,0:T(8,128)S(1)} %get-tuple-element.84), channel_id=1, source_target_pairs={{0,1},{1,0},{2,3},{3,2},{4,5},{5,4},{6,7},{7,6},{8,9},{9,8},{10,11... | collective-permute-start | bytes 442376 | tf_op jit(solution)/shard_map/ppermute | solution.py:488
  37.3 0.8 collective-permute-done.4.halo2_ref
  38.1 0.4 collective-permute-done.5.halo0_ref
  38.4 10.9 %shard_map.235 = (f32[288,128]{1,0:T(8,128)S(1)}, f32[288,128]{1,0:T(8,128)S(1)}, f32[288,128]{1,0:T(8,128)S(1)}, f32[512,128]{1,0:T(8,128)S(1)}, f32[512,128]{1...) custom-call(s32[16]{0:T(128)S(1)} %copy-done.16, ...), custom_call_target="tpu_custom_call" | custom-call | flops 10000000000 | bytes 11912192 | tf_op jit(solution)/shard_map/pallas_call | solution.py:386
  49.4 0.6 shard_map.236
  50.0 0.1 copy-done.19
  50.1 0.1 copy-done.21
  50.2 2.0 %collective-permute-start.6 = (f32[800,128]{1,0:T(8,128)S(1)}, f32[800,128]{1,0:T(8,128)S(1)}, u32[]{:S(2)}, u32[]{:S(2)}) collective-permute-start(f32[800,128]{1,0:T(8,128)S(1)} %get-tuple-element.102), channel_id=1, source_target_pairs={{0,1},{1,0},{2,3},{3,2},{4,5},{5,4},{6,7},{7,6},{8,9},{9,8},{10,11... | collective-permute-start | bytes 1228808 | tf_op jit(solution)/shard_map/ppermute | solution.py:560
  52.2 7.1 %collective-permute-start.7 = (f32[288,128]{1,0:T(8,128)S(1)}, f32[288,128]{1,0:T(8,128)S(1)}, u32[]{:S(2)}, u32[]{:S(2)}) collective-permute-start(f32[288,128]{1,0:T(8,128)S(1)} %get-tuple-element.96.back2_ref), channel_id=1, source_target_pairs={{1,2},{2,1},{5,6},{6,5},{9,10},{10,9},{13,14},{14,13},{17,18},{18,... | collective-permute-start | bytes 442376 | tf_op jit(solution)/shard_map/ppermute | solution.py:563
  59.3 0.0 collective-permute-done.6.taken_ref.in0
  59.3 0.7 shard_map.237
  60.0 11.1 %all-to-all-start = ((f32[32,16,128]{2,1,0:T(8,128)}), f32[32,16,128]{2,1,0:T(8,128)}, u32[]{:S(2)}, u32[]{:S(2)}) async-start(f32[32,16,128]{2,1,0:T(8,128)} %bitcast.6), calls=%async_computation | async-start | bytes 524288 | tf_op jit(solution)/shard_map/all_to_all | solution.py:500
  71.2 0.0 copy-start.6
  71.2 0.0 copy-start.11
  71.2 0.0 copy-start.20
  71.2 3.2 %collective-permute-start.8 = (f32[288,128]{1,0:T(8,128)S(1)}, f32[288,128]{1,0:T(8,128)S(1)}, u32[]{:S(2)}, u32[]{:S(2)}) collective-permute-start(f32[288,128]{1,0:T(8,128)S(1)} %get-tuple-element.105), channel_id=1, source_target_pairs={{0,4},{4,0},{8,12},{12,8},{1,5},{5,1},{9,13},{13,9},{2,6},{6,2},{1... | collective-permute-start | bytes 442376 | tf_op jit(solution)/shard_map/ppermute | solution.py:488
  74.4 0.7 collective-permute-start.9
  75.1 7.8 %all-to-all-done.terms_ref = f32[32,16,128]{2,1,0:T(8,128)} async-done(((f32[32,16,128]{2,1,0:T(8,128)}), f32[32,16,128]{2,1,0:T(8,128)}, u32[]{:S(2)}, u32[]{:S(2)}) %all-to-all-start) | async-done | bytes 262176 | tf_op jit(solution)/shard_map/all_to_all | solution.py:500
  82.9 1.6 %shard_map.239 = f32[8,16,128]{2,1,0:T(8,128)} custom-call(f32[32,16,128]{2,1,0:T(8,128)} %all-to-all-done.terms_ref), custom_call_target="tpu_custom_call" | custom-call | bytes 327680 | tf_op jit(solution)/shard_map/pallas_call | solution.py:386
  84.5 7.6 %all-to-all-start.1 = ((f32[8,16,128]{2,1,0:T(8,128)}), f32[8,16,128]{2,1,0:T(8,128)S(1)}, u32[]{:S(2)}, u32[]{:S(2)}) async-start(f32[8,16,128]{2,1,0:T(8,128)} %shard_map.239), calls=%async_computation.1 | async-start | bytes 131072 | tf_op jit(solution)/shard_map/all_to_all | solution.py:504
  92.1 0.0 collective-permute-done.8.in0
  92.1 0.0 collective-permute-done.9.in2
  92.1 7.2 %all-to-all-done.1.terms_ref = f32[8,16,128]{2,1,0:T(8,128)S(1)} async-done(((f32[8,16,128]{2,1,0:T(8,128)}), f32[8,16,128]{2,1,0:T(8,128)S(1)}, u32[]{:S(2)}, u32[]{:S(2)}) %all-to-all-start.1) | async-done | bytes 65568 | tf_op jit(solution)/shard_map/all_to_all | solution.py:504
  99.3 0.7 collective-permute-start.10
  100.0 3.2 %collective-permute-start.11 = (f32[288,128]{1,0:T(8,128)S(1)}, f32[288,128]{1,0:T(8,128)S(1)}, u32[]{:S(2)}, u32[]{:S(2)}) collective-permute-start(f32[288,128]{1,0:T(8,128)S(1)} %get-tuple-element.112), channel_id=1, source_target_pairs={{0,16},{16,0},{32,48},{48,32},{64,80},{80,64},{96,112},{112,96},{1... | collective-permute-start | bytes 442376 | tf_op jit(solution)/shard_map/ppermute | solution.py:488
  103.2 0.7 shard_map.241
  103.9 6.7 %all-to-all-start.2 = ((f32[32,16,128]{2,1,0:T(8,128)}), f32[32,16,128]{2,1,0:T(8,128)}, u32[]{:S(2)}, u32[]{:S(2)}) async-start(f32[32,16,128]{2,1,0:T(8,128)} %shard_map.241), calls=%async_computation.2 | async-start | bytes 524288 | tf_op jit(solution)/shard_map/all_to_all | solution.py:508
  110.7 1.8 %shard_map.242 = f32[512,128]{1,0:T(8,128)} custom-call(s32[3,3,3,32]{3,2,1,0:T(4,128)S(1)} %copy-done.11, f32[288,128]{1,0:T(8,128)S(1)} %collective-permute-done.11.first_ref, f32[288,128]{1,0:T(8,128)S(1)} %get-tuple-element.114.mid_ref, f32[288,128]{1,0:T(8,128)S(1)} %collective-permute-done.10.second_ref, f32[512,128]{1,0:T(8,128)S(1)} %get-tuple-element.116.base_ref, ...), custom_call_target="tpu_custom_call" | custom-call | flops 999999995904 | bytes 1691008 | tf_op jit(solution)/shard_map/pallas_call | solution.py:386
  112.5 8.3 %all-to-all-done.2 = f32[32,16,128]{2,1,0:T(8,128)} async-done(((f32[32,16,128]{2,1,0:T(8,128)}), f32[32,16,128]{2,1,0:T(8,128)}, u32[]{:S(2)}, u32[]{:S(2)}) %all-to-all-start.2) | async-done | bytes 262176 | tf_op jit(solution)/shard_map/all_to_all | solution.py:508
  120.8 6.0 %collective-permute-start.12 = (f32[512,128]{1,0:T(8,128)}, f32[512,128]{1,0:T(8,128)S(1)}, u32[]{:S(2)}, u32[]{:S(2)}) collective-permute-start(f32[512,128]{1,0:T(8,128)} %bitcast.7.part_ref), channel_id=1, source_target_pairs={{0,1},{1,0},{2,3},{3,2},{4,5},{5,4},{6,7},{7,6},{8,9},{9,8},{10,11... | collective-permute-start | bytes 786440 | tf_op jit(solution)/shard_map/ppermute | solution.py:577
  126.8 1.4 %collective-permute-done.12.other_ref = f32[512,128]{1,0:T(8,128)S(1)} collective-permute-done((f32[512,128]{1,0:T(8,128)}, f32[512,128]{1,0:T(8,128)S(1)}, u32[]{:S(2)}, u32[]{:S(2)}) %collective-permute-start.12) | collective-permute-done | bytes 262176 | tf_op jit(solution)/shard_map/ppermute | solution.py:577
  128.2 1.8 %shard_map.243 = (f32[384,128]{1,0:T(8,128)}, f32[128,128]{1,0:T(8,128)}, f32[256,128]{1,0:T(8,128)}, f32[128,128]{1,0:T(8,128)}, f32[1,128]{1,0:T(1,128)}, /*in...) custom-call(f32[512,128]{1,0:T(8,128)} %bitcast.7.part_ref, f32[512,128]{1,0:T(8,128)S(1)} %collective-permute-done.12.other_ref), custom_call_target="tpu_custom_call" | custom-call | flops 1000000 | bytes 985088 | tf_op jit(solution)/shard_map/pallas_call | solution.py:386
  (43 shorter events, 0.2 us)
Async XLA Ops:
  0.6 11.2 %copy-start = (f32[2048,128]{1,0:T(8,128)S(1)}, f32[2048,128]{1,0:T(8,128)}, u32[]{:S(2)}) copy-start(f32[2048,128]{1,0:T(8,128)} %edge_ref.3) | copy-start | bytes 3145732
  0.7 1.0 copy-start.3
  1.7 0.7 copy-start.10
  2.4 9.5 %copy-start.4 = (f32[512,128]{1,0:T(8,128)S(1)}, f32[512,128]{1,0:T(8,128)}, u32[]{:S(2)}) copy-start(f32[512,128]{1,0:T(8,128)} %node_ref.7) | copy-start | bytes 786436
  2.4 9.5 %copy-start.5 = (f32[384,128]{1,0:T(8,128)S(1)}, f32[384,128]{1,0:T(8,128)}, u32[]{:S(2)}) copy-start(f32[384,128]{1,0:T(8,128)} %weight_ref.1) | copy-start | bytes 589828
  2.4 9.5 %copy-start.7 = (f32[256,128]{1,0:T(8,128)S(1)}, f32[256,128]{1,0:T(8,128)}, u32[]{:S(2)}) copy-start(f32[256,128]{1,0:T(8,128)} %nin_ref.1) | copy-start | bytes 393220
  2.4 9.5 %copy-start.8 = (f32[128,128]{1,0:T(8,128)S(1)}, f32[128,128]{1,0:T(8,128)}, u32[]{:S(2)}) copy-start(f32[128,128]{1,0:T(8,128)} %eout_ref.1) | copy-start | bytes 196612
  2.4 9.5 %copy-start.9 = (f32[128,128]{1,0:T(8,128)S(1)}, f32[128,128]{1,0:T(8,128)}, u32[]{:S(2)}) copy-start(f32[128,128]{1,0:T(8,128)} %nout_ref.1) | copy-start | bytes 196612
  2.4 9.5 %copy-start.12 = (s32[2048]{0:T(1024)S(1)}, s32[2048]{0:T(1024)}, u32[]{:S(2)}) copy-start(s32[2048]{0:T(1024)} %param.20) | copy-start | bytes 24580
  2.4 9.5 %copy-start.13 = (s32[2048]{0:T(1024)S(1)}, s32[2048]{0:T(1024)}, u32[]{:S(2)}) copy-start(s32[2048]{0:T(1024)} %param.21) | copy-start | bytes 24580
  2.5 9.5 %copy-start.14 = (f32[128]{0:T(128)S(1)}, f32[128]{0:T(128)}, u32[]{:S(2)}) copy-start(f32[128]{0:T(128)} %param.25) | copy-start | bytes 1540
  2.5 9.5 %copy-start.15 = (f32[128]{0:T(128)S(1)}, f32[128]{0:T(128)}, u32[]{:S(2)}) copy-start(f32[128]{0:T(128)} %param.29) | copy-start | bytes 1540
  3.0 11.1 %collective-permute-start = (f32[288,128]{1,0:T(8,128)S(1)}, f32[288,128]{1,0:T(8,128)S(1)}, u32[]{:S(2)}, u32[]{:S(2)}) collective-permute-start(f32[288,128]{1,0:T(8,128)S(1)} %get-tuple-element.69), channel_id=1, source_target_pairs={{16,32},{32,16},{48,64},{64,48},{80,96},{96,80},{112,128},{128,112... | collective-permute-start | bytes 442376 | tf_op jit(solution)/shard_map/ppermute | solution.py:487
  3.7 14.3 %collective-permute-start.1 = (f32[288,128]{1,0:T(8,128)S(1)}, f32[288,128]{1,0:T(8,128)S(1)}, u32[]{:S(2)}, u32[]{:S(2)}) collective-permute-start(f32[288,128]{1,0:T(8,128)S(1)} %get-tuple-element.70), channel_id=1, source_target_pairs={{0,16},{16,0},{32,48},{48,32},{64,80},{80,64},{96,112},{112,96},{1... | collective-permute-start | bytes 442376 | tf_op jit(solution)/shard_map/ppermute | solution.py:488
  12.0 26.4 %copy-start.1 = (f32[2048,128]{1,0:T(8,128)S(1)}, f32[2048,128]{1,0:T(8,128)}, u32[]{:S(2)}) copy-start(f32[2048,128]{1,0:T(8,128)} %cot_ref.1) | copy-start | bytes 3145732
  12.0 26.4 %copy-start.2 = (f32[512,128]{1,0:T(8,128)S(1)}, f32[512,128]{1,0:T(8,128)}, u32[]{:S(2)}) copy-start(f32[512,128]{1,0:T(8,128)} %node_cot_ref.1) | copy-start | bytes 786436
  12.0 26.4 %copy-start.16 = (s32[16]{0:T(128)S(1)}, s32[16]{0:T(128)}, u32[]{:S(2)}) copy-start(s32[16]{0:T(128)} %count_ref.1) | copy-start | bytes 196
  12.0 26.4 %copy-start.17 = (f32[128]{0:T(128)S(1)}, f32[128]{0:T(128)}, u32[]{:S(2)}) copy-start(f32[128]{0:T(128)} %param.27) | copy-start | bytes 1540
  12.0 26.4 %copy-start.18 = (f32[128]{0:T(128)S(1)}, f32[128]{0:T(128)}, u32[]{:S(2)}) copy-start(f32[128]{0:T(128)} %param.31) | copy-start | bytes 1540
  18.1 5.9 %collective-permute-start.2 = (f32[288,128]{1,0:T(8,128)S(1)}, f32[288,128]{1,0:T(8,128)S(1)}, u32[]{:S(2)}, u32[]{:S(2)}) collective-permute-start(f32[288,128]{1,0:T(8,128)S(1)} %get-tuple-element.80), channel_id=1, source_target_pairs={{0,4},{4,0},{8,12},{12,8},{1,5},{5,1},{9,13},{13,9},{2,6},{6,2},{1... | collective-permute-start | bytes 442376 | tf_op jit(solution)/shard_map/ppermute | solution.py:488
  21.2 2.8 %collective-permute-start.3 = (f32[288,128]{1,0:T(8,128)S(1)}, f32[288,128]{1,0:T(8,128)S(1)}, u32[]{:S(2)}, u32[]{:S(2)}) collective-permute-start(f32[288,128]{1,0:T(8,128)S(1)} %get-tuple-element.82), channel_id=1, source_target_pairs={{4,8},{8,4},{5,9},{9,5},{6,10},{10,6},{7,11},{11,7},{20,24},{24,20... | collective-permute-start | bytes 442376 | tf_op jit(solution)/shard_map/ppermute | solution.py:487
  24.0 14.1 %collective-permute-start.4 = (f32[288,128]{1,0:T(8,128)S(1)}, f32[288,128]{1,0:T(8,128)S(1)}, u32[]{:S(2)}, u32[]{:S(2)}) collective-permute-start(f32[288,128]{1,0:T(8,128)S(1)} %get-tuple-element.83), channel_id=1, source_target_pairs={{1,2},{2,1},{5,6},{6,5},{9,10},{10,9},{13,14},{14,13},{17,18},{18,... | collective-permute-start | bytes 442376 | tf_op jit(solution)/shard_map/ppermute | solution.py:487
  35.1 3.3 %collective-permute-start.5 = (f32[288,128]{1,0:T(8,128)S(1)}, f32[288,128]{1,0:T(8,128)S(1)}, u32[]{:S(2)}, u32[]{:S(2)}) collective-permute-start(f32[288,128]{1,0:T(8,128)S(1)} %get-tuple-element.84), channel_id=1, source_target_pairs={{0,1},{1,0},{2,3},{3,2},{4,5},{5,4},{6,7},{7,6},{8,9},{9,8},{10,11... | collective-permute-start | bytes 442376 | tf_op jit(solution)/shard_map/ppermute | solution.py:488
  49.4 0.7 copy-start.19
  49.4 0.8 copy-start.21
  50.2 9.1 %collective-permute-start.6 = (f32[800,128]{1,0:T(8,128)S(1)}, f32[800,128]{1,0:T(8,128)S(1)}, u32[]{:S(2)}, u32[]{:S(2)}) collective-permute-start(f32[800,128]{1,0:T(8,128)S(1)} %get-tuple-element.102), channel_id=1, source_target_pairs={{0,1},{1,0},{2,3},{3,2},{4,5},{5,4},{6,7},{7,6},{8,9},{9,8},{10,11... | collective-permute-start | bytes 1228808 | tf_op jit(solution)/shard_map/ppermute | solution.py:560
  52.2 18.9 %collective-permute-start.7 = (f32[288,128]{1,0:T(8,128)S(1)}, f32[288,128]{1,0:T(8,128)S(1)}, u32[]{:S(2)}, u32[]{:S(2)}) collective-permute-start(f32[288,128]{1,0:T(8,128)S(1)} %get-tuple-element.96.back2_ref), channel_id=1, source_target_pairs={{1,2},{2,1},{5,6},{6,5},{9,10},{10,9},{13,14},{14,13},{17,18},{18,... | collective-permute-start | bytes 442376 | tf_op jit(solution)/shard_map/ppermute | solution.py:563
  60.0 22.8 %all-to-all-start = ((f32[32,16,128]{2,1,0:T(8,128)}), f32[32,16,128]{2,1,0:T(8,128)}, u32[]{:S(2)}, u32[]{:S(2)}) async-start(f32[32,16,128]{2,1,0:T(8,128)} %bitcast.6), calls=%async_computation | async-start | bytes 524288 | tf_op jit(solution)/shard_map/all_to_all | solution.py:500
  71.2 39.5 %copy-start.6 = (f32[384,128]{1,0:T(8,128)S(1)}, f32[384,128]{1,0:T(8,128)}, u32[]{:S(2)}) copy-start(f32[384,128]{1,0:T(8,128)} %weight_ref.1) | copy-start | bytes 589828
  71.2 39.5 %copy-start.11 = (s32[3,3,3,32]{3,2,1,0:T(4,128)S(1)}, s32[3,3,3,32]{3,2,1,0:T(4,128)}, u32[]{:S(2)}) copy-start(s32[3,3,3,32]{3,2,1,0:T(4,128)} %lists_ref.3) | copy-start | bytes 10372
  71.2 39.5 %copy-start.20 = (f32[512,128]{1,0:T(8,128)S(1)}, f32[512,128]{1,0:T(8,128)}, u32[]{:S(2)}) copy-start(f32[512,128]{1,0:T(8,128)} %copy-done.19) | copy-start | bytes 786436
  71.2 39.5 %copy-start.22 = (f32[512,128]{1,0:T(8,128)S(1)}, f32[512,128]{1,0:T(8,128)}, u32[]{:S(2)}) copy-start(f32[512,128]{1,0:T(8,128)} %copy-done.21) | copy-start | bytes 786436
  71.2 20.8 %collective-permute-start.8 = (f32[288,128]{1,0:T(8,128)S(1)}, f32[288,128]{1,0:T(8,128)S(1)}, u32[]{:S(2)}, u32[]{:S(2)}) collective-permute-start(f32[288,128]{1,0:T(8,128)S(1)} %get-tuple-element.105), channel_id=1, source_target_pairs={{0,4},{4,0},{8,12},{12,8},{1,5},{5,1},{9,13},{13,9},{2,6},{6,2},{1... | collective-permute-start | bytes 442376 | tf_op jit(solution)/shard_map/ppermute | solution.py:488
  74.4 17.6 %collective-permute-start.9 = (f32[288,128]{1,0:T(8,128)S(1)}, f32[288,128]{1,0:T(8,128)S(1)}, u32[]{:S(2)}, u32[]{:S(2)}) collective-permute-start(f32[288,128]{1,0:T(8,128)S(1)} %get-tuple-element.106), channel_id=1, source_target_pairs={{4,8},{8,4},{5,9},{9,5},{6,10},{10,6},{7,11},{11,7},{20,24},{24,20... | collective-permute-start | bytes 442376 | tf_op jit(solution)/shard_map/ppermute | solution.py:487
  84.5 14.8 %all-to-all-start.1 = ((f32[8,16,128]{2,1,0:T(8,128)}), f32[8,16,128]{2,1,0:T(8,128)S(1)}, u32[]{:S(2)}, u32[]{:S(2)}) async-start(f32[8,16,128]{2,1,0:T(8,128)} %shard_map.239), calls=%async_computation.1 | async-start | bytes 131072 | tf_op jit(solution)/shard_map/all_to_all | solution.py:504
  99.3 11.3 %collective-permute-start.10 = (f32[288,128]{1,0:T(8,128)S(1)}, f32[288,128]{1,0:T(8,128)S(1)}, u32[]{:S(2)}, u32[]{:S(2)}) collective-permute-start(f32[288,128]{1,0:T(8,128)S(1)} %get-tuple-element.111), channel_id=1, source_target_pairs={{16,32},{32,16},{48,64},{64,48},{80,96},{96,80},{112,128},{128,112... | collective-permute-start | bytes 442376 | tf_op jit(solution)/shard_map/ppermute | solution.py:487
  100.0 10.7 %collective-permute-start.11 = (f32[288,128]{1,0:T(8,128)S(1)}, f32[288,128]{1,0:T(8,128)S(1)}, u32[]{:S(2)}, u32[]{:S(2)}) collective-permute-start(f32[288,128]{1,0:T(8,128)S(1)} %get-tuple-element.112), channel_id=1, source_target_pairs={{0,16},{16,0},{32,48},{48,32},{64,80},{80,64},{96,112},{112,96},{1... | collective-permute-start | bytes 442376 | tf_op jit(solution)/shard_map/ppermute | solution.py:488
  103.9 16.9 %all-to-all-start.2 = ((f32[32,16,128]{2,1,0:T(8,128)}), f32[32,16,128]{2,1,0:T(8,128)}, u32[]{:S(2)}, u32[]{:S(2)}) async-start(f32[32,16,128]{2,1,0:T(8,128)} %shard_map.241), calls=%async_computation.2 | async-start | bytes 524288 | tf_op jit(solution)/shard_map/all_to_all | solution.py:508
  120.8 7.4 %collective-permute-start.12 = (f32[512,128]{1,0:T(8,128)}, f32[512,128]{1,0:T(8,128)S(1)}, u32[]{:S(2)}, u32[]{:S(2)}) collective-permute-start(f32[512,128]{1,0:T(8,128)} %bitcast.7.part_ref), channel_id=1, source_target_pairs={{0,1},{1,0},{2,3},{3,2},{4,5},{5,4},{6,7},{7,6},{8,9},{9,8},{10,11... | collective-permute-start | bytes 786440 | tf_op jit(solution)/shard_map/ppermute | solution.py:577

commit v5 on v4

--- a/solution.py
+++ b/solution.py
@@ -465,7 +465,7 @@
         [(CELLS, HID)],
         operands,
         scratch=[((SLOT, HID), jnp.int32)],
-        flops=1000000000000,
+        flops=5 * 10**9,
     )[0]
 
 
@@ -561,12 +561,12 @@
     part = call(add_kernel, [(CELLS, HID)], [keep, taken])[0]
     part = scatter_half(part)
     second = lax.ppermute(back[2], GZ, swaps(GZ)[1])
-    first, mid, second = regroup((taken, back[1], second), SLOT, 1000000000000)
+    first, mid, second = regroup((taken, back[1], second), SLOT, 10**10)
     part, _ = join((part, mid))
     part = every_term(part)
     first, second = trade(first, second, GY)
     first, mid, second = regroup((first, mid, second), 3 * SLOT, 0)
-    part, first, mid, second = join((part, first, mid, second))
+    part, _ = join((part, mid))
     part = gather_half(part)
     first, second = trade(first, second, GX)
     second, first = join((second, first))

time: 131 us -> 122 us (0.931)
  waiting for transfers between devices: 31.8 us -> 27.8 us
  starting transfers between devices: 74.1 us -> 71.2 us
  Pallas kernels: 20.9 us -> 19 us
    all_to_all x1, waiting for transfers between devices: 7.18 us -> 3.28 us  [every_term(): return lax.all_to_all(sum_spread(terms, 8), 'y', 0, 0)]
    all_to_all x1, starting transfers between devices: 6.71 us -> 4.49 us  [gather_half(): part = lax.all_to_all(sum_spread(terms, 32), ('x', 'zl', 'zh'), 0, 0)]
    pallas_call x13, Pallas kernels: 20.9 us -> 19 us  [call(): pl.pallas_call(body, out_shape=shapes, in_specs=[SMEM] * len(smem) + [VME...]
where the time goes in v5:
time: 122 us; the launch traced here: 121 us
  starting transfers between devices  71.2 us (58%)
  waiting for transfers between devices  27.8 us (23%)
  Pallas kernels  19 us (16%)
  local copies, waits for them, and re-layouts  1.83 us (2%)
    ppermute x5, starting transfers between devices, trade(): return (lax.ppermute(first, axis, near), second)  19.7 us
    pallas_call x13, Pallas kernels, call(): pl.pallas_call(body, out_shape=shapes, in_specs=[SMEM] * len(smem) + [VME...  19 us
    ppermute x5, starting transfers between devices, trade(): second = lax.ppermute(second, axis, far)  13.8 us
    all_to_all x1, starting transfers between devices, scatter_half(): return lax.all_to_all(part.reshape(32, 16, HID), ('x', 'zl', 'zh'), 0, 0)  11 us
    all_to_all x1, waiting for transfers between devices, gather_half(): part = lax.all_to_all(sum_spread(terms, 32), ('x', 'zl', 'zh'), 0, 0)  8.32 us
    all_to_all x1, waiting for transfers between devices, scatter_half(): return lax.all_to_all(part.reshape(32, 16, HID), ('x', 'zl', 'zh'), 0, 0)  7.87 us
    all_to_all x1, starting transfers between devices, every_term(): return lax.all_to_all(sum_spread(terms, 8), 'y', 0, 0)  7.57 us
    ppermute x1, starting transfers between devices, on_device(): second = lax.ppermute(back[2], GZ, swaps(GZ)[1])  7.08 us
  transfers between devices with their start and end apart: 16, of which 8 were waited for; matrix products, arithmetic and copies ran while one was open for 0% of the time, Pallas kernels for 5%

profile of v5, /device:TPU:1, one launch (start us, length us, event | category | flops | bytes accessed | tf_op | source)
XLA Modules:
  0.0 120.9 jit_solution(5348552494308955617)
XLA Ops:
  0.7 1.0 copy-done.3
  1.7 0.7 copy-done.9
  2.5 0.5 shard_map.231
  3.0 0.7 collective-permute-start
  3.7 8.2 %collective-permute-start.1 = (f32[288,128]{1,0:T(8,128)S(1)}, f32[288,128]{1,0:T(8,128)S(1)}, u32[]{:S(2)}, u32[]{:S(2)}) collective-permute-start(f32[288,128]{1,0:T(8,128)S(1)} %get-tuple-element.67), channel_id=1, source_target_pairs={{0,16},{16,0},{32,48},{48,32},{64,80},{80,64},{96,112},{112,96},{1... | collective-permute-start | bytes 442376 | tf_op jit(solution)/shard_map/ppermute | solution.py:488
  12.0 0.0 copy-start.1
  12.0 0.0 copy-start.2
  12.0 0.0 copy-start.15
  12.0 0.0 copy-start.16
  12.0 0.0 copy-start.17
  12.0 2.1 %shard_map.232 = (f32[2048,128]{1,0:T(8,128)S(1)}, f32[512,128]{1,0:T(8,128)S(1)}, s32[2048,128]{1,0:T(8,128)S(1)}, s32[2048,128]{1,0:T(8,128)S(1)}, s32[16,128]...) custom-call(f32[512,128]{1,0:T(8,128)S(1)} %copy-done.4, f32[2048,128]{1,0:T(8,128)S(1)} %copy-done, s32[16,128]{1,0:T(8,128)S(1)} %bitcast.14, ...), custom_call_target="tpu_custom_call" | custom-call | flops 3000000000 | bytes 7562240 | tf_op jit(solution)/shard_map/pallas_call | solution.py:386
  14.1 0.0 collective-permute-done.in2
  14.1 3.9 %collective-permute-done.1.in0 = f32[288,128]{1,0:T(8,128)S(1)} collective-permute-done((f32[288,128]{1,0:T(8,128)S(1)}, f32[288,128]{1,0:T(8,128)S(1)}, u32[]{:S(2)}, u32[]{:S(2)}) %collective-permute-start.1) | collective-permute-done | bytes 147488 | tf_op jit(solution)/shard_map/ppermute | solution.py:488
  18.1 3.1 %collective-permute-start.2 = (f32[288,128]{1,0:T(8,128)S(1)}, f32[288,128]{1,0:T(8,128)S(1)}, u32[]{:S(2)}, u32[]{:S(2)}) collective-permute-start(f32[288,128]{1,0:T(8,128)S(1)} %get-tuple-element.77), channel_id=1, source_target_pairs={{0,4},{4,0},{8,12},{12,8},{1,5},{5,1},{9,13},{13,9},{2,6},{6,2},{1... | collective-permute-start | bytes 442376 | tf_op jit(solution)/shard_map/ppermute | solution.py:488
  21.2 0.7 collective-permute-start.3
  21.8 2.1 %collective-permute-done.2.in0 = f32[288,128]{1,0:T(8,128)S(1)} collective-permute-done((f32[288,128]{1,0:T(8,128)S(1)}, f32[288,128]{1,0:T(8,128)S(1)}, u32[]{:S(2)}, u32[]{:S(2)}) %collective-permute-start.2) | collective-permute-done | bytes 147488 | tf_op jit(solution)/shard_map/ppermute | solution.py:488
  23.9 0.0 collective-permute-done.3.in2
  24.0 11.2 %collective-permute-start.4 = (f32[288,128]{1,0:T(8,128)S(1)}, f32[288,128]{1,0:T(8,128)S(1)}, u32[]{:S(2)}, u32[]{:S(2)}) collective-permute-start(f32[288,128]{1,0:T(8,128)S(1)} %get-tuple-element.80), channel_id=1, source_target_pairs={{1,2},{2,1},{5,6},{6,5},{9,10},{10,9},{13,14},{14,13},{17,18},{18,... | collective-permute-start | bytes 442376 | tf_op jit(solution)/shard_map/ppermute | solution.py:487
  35.1 2.1 %collective-permute-start.5 = (f32[288,128]{1,0:T(8,128)S(1)}, f32[288,128]{1,0:T(8,128)S(1)}, u32[]{:S(2)}, u32[]{:S(2)}) collective-permute-start(f32[288,128]{1,0:T(8,128)S(1)} %get-tuple-element.81), channel_id=1, source_target_pairs={{0,1},{1,0},{2,3},{3,2},{4,5},{5,4},{6,7},{7,6},{8,9},{9,8},{10,11... | collective-permute-start | bytes 442376 | tf_op jit(solution)/shard_map/ppermute | solution.py:488
  37.3 0.8 collective-permute-done.4.halo2_ref
  38.1 0.4 collective-permute-done.5.halo0_ref
  38.4 10.9 %shard_map.235 = (f32[288,128]{1,0:T(8,128)S(1)}, f32[288,128]{1,0:T(8,128)S(1)}, f32[288,128]{1,0:T(8,128)S(1)}, f32[512,128]{1,0:T(8,128)S(1)}, f32[512,128]{1...) custom-call(s32[16]{0:T(128)S(1)} %copy-done.15, ...), custom_call_target="tpu_custom_call" | custom-call | flops 10000000000 | bytes 11912192 | tf_op jit(solution)/shard_map/pallas_call | solution.py:386
  49.4 0.6 shard_map.236
  50.0 2.1 %collective-permute-start.6 = (f32[800,128]{1,0:T(8,128)S(1)}, f32[800,128]{1,0:T(8,128)S(1)}, u32[]{:S(2)}, u32[]{:S(2)}) collective-permute-start(f32[800,128]{1,0:T(8,128)S(1)} %get-tuple-element.99), channel_id=1, source_target_pairs={{0,1},{1,0},{2,3},{3,2},{4,5},{5,4},{6,7},{7,6},{8,9},{9,8},{10,11... | collective-permute-start | bytes 1228808 | tf_op jit(solution)/shard_map/ppermute | solution.py:560
  52.0 7.1 %collective-permute-start.7 = (f32[288,128]{1,0:T(8,128)S(1)}, f32[288,128]{1,0:T(8,128)S(1)}, u32[]{:S(2)}, u32[]{:S(2)}) collective-permute-start(f32[288,128]{1,0:T(8,128)S(1)} %get-tuple-element.93.back2_ref), channel_id=1, source_target_pairs={{1,2},{2,1},{5,6},{6,5},{9,10},{10,9},{13,14},{14,13},{17,18},{18,... | collective-permute-start | bytes 442376 | tf_op jit(solution)/shard_map/ppermute | solution.py:563
  59.1 0.0 collective-permute-done.6.taken_ref.in0
  59.1 0.7 shard_map.237
  59.9 11.0 %all-to-all-start = ((f32[32,16,128]{2,1,0:T(8,128)}), f32[32,16,128]{2,1,0:T(8,128)S(1)}, u32[]{:S(2)}, u32[]{:S(2)}) async-start(f32[32,16,128]{2,1,0:T(8,128)} %bitcast.6), calls=%async_computation | async-start | bytes 524288 | tf_op jit(solution)/shard_map/all_to_all | solution.py:500
  70.8 0.0 collective-permute-done.7.in2
  70.9 0.0 copy-start.10
  70.9 3.1 %collective-permute-start.8 = (f32[288,128]{1,0:T(8,128)S(1)}, f32[288,128]{1,0:T(8,128)S(1)}, u32[]{:S(2)}, u32[]{:S(2)}) collective-permute-start(f32[288,128]{1,0:T(8,128)S(1)} %get-tuple-element.102), channel_id=1, source_target_pairs={{0,4},{4,0},{8,12},{12,8},{1,5},{5,1},{9,13},{13,9},{2,6},{6,2},{1... | collective-permute-start | bytes 442376 | tf_op jit(solution)/shard_map/ppermute | solution.py:488
  74.1 0.7 collective-permute-start.9
  74.7 7.9 %all-to-all-done.terms_ref = f32[32,16,128]{2,1,0:T(8,128)S(1)} async-done(((f32[32,16,128]{2,1,0:T(8,128)}), f32[32,16,128]{2,1,0:T(8,128)S(1)}, u32[]{:S(2)}, u32[]{:S(2)}) %all-to-all-start) | async-done | bytes 262176 | tf_op jit(solution)/shard_map/all_to_all | solution.py:500
  82.6 0.7 shard_map.239
  83.3 7.6 %all-to-all-start.1 = ((f32[8,16,128]{2,1,0:T(8,128)}), f32[8,16,128]{2,1,0:T(8,128)S(1)}, u32[]{:S(2)}, u32[]{:S(2)}) async-start(f32[8,16,128]{2,1,0:T(8,128)} %shard_map.239), calls=%async_computation.1 | async-start | bytes 131072 | tf_op jit(solution)/shard_map/all_to_all | solution.py:504
  90.8 0.0 collective-permute-done.8.in0
  90.8 0.0 collective-permute-done.9.in2
  90.9 0.7 collective-permute-start.10
  91.6 3.2 %collective-permute-start.11 = (f32[288,128]{1,0:T(8,128)S(1)}, f32[288,128]{1,0:T(8,128)S(1)}, u32[]{:S(2)}, u32[]{:S(2)}) collective-permute-start(f32[288,128]{1,0:T(8,128)S(1)} %get-tuple-element.107), channel_id=1, source_target_pairs={{0,16},{16,0},{32,48},{48,32},{64,80},{80,64},{96,112},{112,96},{1... | collective-permute-start | bytes 442376 | tf_op jit(solution)/shard_map/ppermute | solution.py:488
  94.8 3.3 %all-to-all-done.1.terms_ref = f32[8,16,128]{2,1,0:T(8,128)S(1)} async-done(((f32[8,16,128]{2,1,0:T(8,128)}), f32[8,16,128]{2,1,0:T(8,128)S(1)}, u32[]{:S(2)}, u32[]{:S(2)}) %all-to-all-start.1) | async-done | bytes 65568 | tf_op jit(solution)/shard_map/all_to_all | solution.py:504
  98.1 0.7 shard_map.241
  98.8 4.5 %all-to-all-start.2 = ((f32[32,16,128]{2,1,0:T(8,128)}), f32[32,16,128]{2,1,0:T(8,128)S(1)}, u32[]{:S(2)}, u32[]{:S(2)}) async-start(f32[32,16,128]{2,1,0:T(8,128)} %shard_map.241), calls=%async_computation.2 | async-start | bytes 524288 | tf_op jit(solution)/shard_map/all_to_all | solution.py:508
  103.3 0.0 collective-permute-done.10.second_ref
  103.3 1.8 %shard_map.242 = f32[512,128]{1,0:T(8,128)} custom-call(s32[3,3,3,32]{3,2,1,0:T(4,128)S(1)} %copy-done.10, f32[288,128]{1,0:T(8,128)S(1)} %collective-permute-done.11.first_ref, f32[288,128]{1,0:T(8,128)S(1)} %get-tuple-element.104.mid_ref, f32[288,128]{1,0:T(8,128)S(1)} %collective-permute-done.10.second_ref, f32[512,128]{1,0:T(8,128)S(1)} %get-tuple-element.110.base_ref, ...), custom_call_target="tpu_custom_call" | custom-call | flops 5000000000 | bytes 1691008 | tf_op jit(solution)/shard_map/pallas_call | solution.py:386
  105.2 8.3 %all-to-all-done.2 = f32[32,16,128]{2,1,0:T(8,128)S(1)} async-done(((f32[32,16,128]{2,1,0:T(8,128)}), f32[32,16,128]{2,1,0:T(8,128)S(1)}, u32[]{:S(2)}, u32[]{:S(2)}) %all-to-all-start.2) | async-done | bytes 262176 | tf_op jit(solution)/shard_map/all_to_all | solution.py:508
  113.5 5.5 %collective-permute-start.12 = (f32[512,128]{1,0:T(8,128)S(1)}, f32[512,128]{1,0:T(8,128)S(1)}, u32[]{:S(2)}, u32[]{:S(2)}) collective-permute-start(f32[512,128]{1,0:T(8,128)S(1)} %bitcast.12), channel_id=1, source_target_pairs={{0,1},{1,0},{2,3},{3,2},{4,5},{5,4},{6,7},{7,6},{8,9},{9,8},{10,11... | collective-permute-start | bytes 786440 | tf_op jit(solution)/shard_map/ppermute | solution.py:577
  119.0 1.1 collective-permute-done.12.other_ref
  120.1 0.8 shard_map.243
  (33 shorter events, 0.2 us)
Async XLA Ops:
  0.6 11.2 %copy-start = (f32[2048,128]{1,0:T(8,128)S(1)}, f32[2048,128]{1,0:T(8,128)}, u32[]{:S(2)}) copy-start(f32[2048,128]{1,0:T(8,128)} %edge_ref.3) | copy-start | bytes 3145732
  0.7 1.0 copy-start.3
  1.7 0.7 copy-start.9
  2.4 9.5 %copy-start.4 = (f32[512,128]{1,0:T(8,128)S(1)}, f32[512,128]{1,0:T(8,128)}, u32[]{:S(2)}) copy-start(f32[512,128]{1,0:T(8,128)} %node_ref.7) | copy-start | bytes 786436
  2.4 9.5 %copy-start.5 = (f32[384,128]{1,0:T(8,128)S(1)}, f32[384,128]{1,0:T(8,128)}, u32[]{:S(2)}) copy-start(f32[384,128]{1,0:T(8,128)} %weight_ref.1) | copy-start | bytes 589828
  2.4 9.5 %copy-start.6 = (f32[256,128]{1,0:T(8,128)S(1)}, f32[256,128]{1,0:T(8,128)}, u32[]{:S(2)}) copy-start(f32[256,128]{1,0:T(8,128)} %nin_ref.1) | copy-start | bytes 393220
  2.4 9.5 %copy-start.7 = (f32[128,128]{1,0:T(8,128)S(1)}, f32[128,128]{1,0:T(8,128)}, u32[]{:S(2)}) copy-start(f32[128,128]{1,0:T(8,128)} %eout_ref.1) | copy-start | bytes 196612
  2.4 9.5 %copy-start.8 = (f32[128,128]{1,0:T(8,128)S(1)}, f32[128,128]{1,0:T(8,128)}, u32[]{:S(2)}) copy-start(f32[128,128]{1,0:T(8,128)} %nout_ref.1) | copy-start | bytes 196612
  2.4 9.5 %copy-start.11 = (s32[2048]{0:T(1024)S(1)}, s32[2048]{0:T(1024)}, u32[]{:S(2)}) copy-start(s32[2048]{0:T(1024)} %param.20) | copy-start | bytes 24580
  2.4 9.5 %copy-start.12 = (s32[2048]{0:T(1024)S(1)}, s32[2048]{0:T(1024)}, u32[]{:S(2)}) copy-start(s32[2048]{0:T(1024)} %param.21) | copy-start | bytes 24580
  2.5 9.5 %copy-start.13 = (f32[128]{0:T(128)S(1)}, f32[128]{0:T(128)}, u32[]{:S(2)}) copy-start(f32[128]{0:T(128)} %param.25) | copy-start | bytes 1540
  2.5 9.5 %copy-start.14 = (f32[128]{0:T(128)S(1)}, f32[128]{0:T(128)}, u32[]{:S(2)}) copy-start(f32[128]{0:T(128)} %param.29) | copy-start | bytes 1540
  3.0 11.1 %collective-permute-start = (f32[288,128]{1,0:T(8,128)S(1)}, f32[288,128]{1,0:T(8,128)S(1)}, u32[]{:S(2)}, u32[]{:S(2)}) collective-permute-start(f32[288,128]{1,0:T(8,128)S(1)} %get-tuple-element.66), channel_id=1, source_target_pairs={{16,32},{32,16},{48,64},{64,48},{80,96},{96,80},{112,128},{128,112... | collective-permute-start | bytes 442376 | tf_op jit(solution)/shard_map/ppermute | solution.py:487
  3.7 14.3 %collective-permute-start.1 = (f32[288,128]{1,0:T(8,128)S(1)}, f32[288,128]{1,0:T(8,128)S(1)}, u32[]{:S(2)}, u32[]{:S(2)}) collective-permute-start(f32[288,128]{1,0:T(8,128)S(1)} %get-tuple-element.67), channel_id=1, source_target_pairs={{0,16},{16,0},{32,48},{48,32},{64,80},{80,64},{96,112},{112,96},{1... | collective-permute-start | bytes 442376 | tf_op jit(solution)/shard_map/ppermute | solution.py:488
  12.0 26.4 %copy-start.1 = (f32[2048,128]{1,0:T(8,128)S(1)}, f32[2048,128]{1,0:T(8,128)}, u32[]{:S(2)}) copy-start(f32[2048,128]{1,0:T(8,128)} %cot_ref.1) | copy-start | bytes 3145732
  12.0 26.4 %copy-start.2 = (f32[512,128]{1,0:T(8,128)S(1)}, f32[512,128]{1,0:T(8,128)}, u32[]{:S(2)}) copy-start(f32[512,128]{1,0:T(8,128)} %node_cot_ref.1) | copy-start | bytes 786436
  12.0 26.4 %copy-start.15 = (s32[16]{0:T(128)S(1)}, s32[16]{0:T(128)}, u32[]{:S(2)}) copy-start(s32[16]{0:T(128)} %count_ref.1) | copy-start | bytes 196
  12.0 26.4 %copy-start.16 = (f32[128]{0:T(128)S(1)}, f32[128]{0:T(128)}, u32[]{:S(2)}) copy-start(f32[128]{0:T(128)} %param.27) | copy-start | bytes 1540
  12.0 26.4 %copy-start.17 = (f32[128]{0:T(128)S(1)}, f32[128]{0:T(128)}, u32[]{:S(2)}) copy-start(f32[128]{0:T(128)} %param.31) | copy-start | bytes 1540
  18.1 5.9 %collective-permute-start.2 = (f32[288,128]{1,0:T(8,128)S(1)}, f32[288,128]{1,0:T(8,128)S(1)}, u32[]{:S(2)}, u32[]{:S(2)}) collective-permute-start(f32[288,128]{1,0:T(8,128)S(1)} %get-tuple-element.77), channel_id=1, source_target_pairs={{0,4},{4,0},{8,12},{12,8},{1,5},{5,1},{9,13},{13,9},{2,6},{6,2},{1... | collective-permute-start | bytes 442376 | tf_op jit(solution)/shard_map/ppermute | solution.py:488
  21.2 2.8 %collective-permute-start.3 = (f32[288,128]{1,0:T(8,128)S(1)}, f32[288,128]{1,0:T(8,128)S(1)}, u32[]{:S(2)}, u32[]{:S(2)}) collective-permute-start(f32[288,128]{1,0:T(8,128)S(1)} %get-tuple-element.79), channel_id=1, source_target_pairs={{4,8},{8,4},{5,9},{9,5},{6,10},{10,6},{7,11},{11,7},{20,24},{24,20... | collective-permute-start | bytes 442376 | tf_op jit(solution)/shard_map/ppermute | solution.py:487
  24.0 14.1 %collective-permute-start.4 = (f32[288,128]{1,0:T(8,128)S(1)}, f32[288,128]{1,0:T(8,128)S(1)}, u32[]{:S(2)}, u32[]{:S(2)}) collective-permute-start(f32[288,128]{1,0:T(8,128)S(1)} %get-tuple-element.80), channel_id=1, source_target_pairs={{1,2},{2,1},{5,6},{6,5},{9,10},{10,9},{13,14},{14,13},{17,18},{18,... | collective-permute-start | bytes 442376 | tf_op jit(solution)/shard_map/ppermute | solution.py:487
  35.1 3.3 %collective-permute-start.5 = (f32[288,128]{1,0:T(8,128)S(1)}, f32[288,128]{1,0:T(8,128)S(1)}, u32[]{:S(2)}, u32[]{:S(2)}) collective-permute-start(f32[288,128]{1,0:T(8,128)S(1)} %get-tuple-element.81), channel_id=1, source_target_pairs={{0,1},{1,0},{2,3},{3,2},{4,5},{5,4},{6,7},{7,6},{8,9},{9,8},{10,11... | collective-permute-start | bytes 442376 | tf_op jit(solution)/shard_map/ppermute | solution.py:488
  50.0 9.1 %collective-permute-start.6 = (f32[800,128]{1,0:T(8,128)S(1)}, f32[800,128]{1,0:T(8,128)S(1)}, u32[]{:S(2)}, u32[]{:S(2)}) collective-permute-start(f32[800,128]{1,0:T(8,128)S(1)} %get-tuple-element.99), channel_id=1, source_target_pairs={{0,1},{1,0},{2,3},{3,2},{4,5},{5,4},{6,7},{7,6},{8,9},{9,8},{10,11... | collective-permute-start | bytes 1228808 | tf_op jit(solution)/shard_map/ppermute | solution.py:560
  52.0 18.8 %collective-permute-start.7 = (f32[288,128]{1,0:T(8,128)S(1)}, f32[288,128]{1,0:T(8,128)S(1)}, u32[]{:S(2)}, u32[]{:S(2)}) collective-permute-start(f32[288,128]{1,0:T(8,128)S(1)} %get-tuple-element.93.back2_ref), channel_id=1, source_target_pairs={{1,2},{2,1},{5,6},{6,5},{9,10},{10,9},{13,14},{14,13},{17,18},{18,... | collective-permute-start | bytes 442376 | tf_op jit(solution)/shard_map/ppermute | solution.py:563
  59.9 22.7 %all-to-all-start = ((f32[32,16,128]{2,1,0:T(8,128)}), f32[32,16,128]{2,1,0:T(8,128)S(1)}, u32[]{:S(2)}, u32[]{:S(2)}) async-start(f32[32,16,128]{2,1,0:T(8,128)} %bitcast.6), calls=%async_computation | async-start | bytes 524288 | tf_op jit(solution)/shard_map/all_to_all | solution.py:500
  70.9 32.4 %copy-start.10 = (s32[3,3,3,32]{3,2,1,0:T(4,128)S(1)}, s32[3,3,3,32]{3,2,1,0:T(4,128)}, u32[]{:S(2)}) copy-start(s32[3,3,3,32]{3,2,1,0:T(4,128)} %lists_ref.3) | copy-start | bytes 10372
  70.9 19.9 %collective-permute-start.8 = (f32[288,128]{1,0:T(8,128)S(1)}, f32[288,128]{1,0:T(8,128)S(1)}, u32[]{:S(2)}, u32[]{:S(2)}) collective-permute-start(f32[288,128]{1,0:T(8,128)S(1)} %get-tuple-element.102), channel_id=1, source_target_pairs={{0,4},{4,0},{8,12},{12,8},{1,5},{5,1},{9,13},{13,9},{2,6},{6,2},{1... | collective-permute-start | bytes 442376 | tf_op jit(solution)/shard_map/ppermute | solution.py:488
  74.1 16.8 %collective-permute-start.9 = (f32[288,128]{1,0:T(8,128)S(1)}, f32[288,128]{1,0:T(8,128)S(1)}, u32[]{:S(2)}, u32[]{:S(2)}) collective-permute-start(f32[288,128]{1,0:T(8,128)S(1)} %get-tuple-element.103), channel_id=1, source_target_pairs={{4,8},{8,4},{5,9},{9,5},{6,10},{10,6},{7,11},{11,7},{20,24},{24,20... | collective-permute-start | bytes 442376 | tf_op jit(solution)/shard_map/ppermute | solution.py:487
  83.3 14.8 %all-to-all-start.1 = ((f32[8,16,128]{2,1,0:T(8,128)}), f32[8,16,128]{2,1,0:T(8,128)S(1)}, u32[]{:S(2)}, u32[]{:S(2)}) async-start(f32[8,16,128]{2,1,0:T(8,128)} %shard_map.239), calls=%async_computation.1 | async-start | bytes 131072 | tf_op jit(solution)/shard_map/all_to_all | solution.py:504
  90.9 12.4 %collective-permute-start.10 = (f32[288,128]{1,0:T(8,128)S(1)}, f32[288,128]{1,0:T(8,128)S(1)}, u32[]{:S(2)}, u32[]{:S(2)}) collective-permute-start(f32[288,128]{1,0:T(8,128)S(1)} %get-tuple-element.106), channel_id=1, source_target_pairs={{16,32},{32,16},{48,64},{64,48},{80,96},{96,80},{112,128},{128,112... | collective-permute-start | bytes 442376 | tf_op jit(solution)/shard_map/ppermute | solution.py:487
  91.6 11.7 %collective-permute-start.11 = (f32[288,128]{1,0:T(8,128)S(1)}, f32[288,128]{1,0:T(8,128)S(1)}, u32[]{:S(2)}, u32[]{:S(2)}) collective-permute-start(f32[288,128]{1,0:T(8,128)S(1)} %get-tuple-element.107), channel_id=1, source_target_pairs={{0,16},{16,0},{32,48},{48,32},{64,80},{80,64},{96,112},{112,96},{1... | collective-permute-start | bytes 442376 | tf_op jit(solution)/shard_map/ppermute | solution.py:488
  98.8 14.7 %all-to-all-start.2 = ((f32[32,16,128]{2,1,0:T(8,128)}), f32[32,16,128]{2,1,0:T(8,128)S(1)}, u32[]{:S(2)}, u32[]{:S(2)}) async-start(f32[32,16,128]{2,1,0:T(8,128)} %shard_map.241), calls=%async_computation.2 | async-start | bytes 524288 | tf_op jit(solution)/shard_map/all_to_all | solution.py:508
  113.5 6.6 %collective-permute-start.12 = (f32[512,128]{1,0:T(8,128)S(1)}, f32[512,128]{1,0:T(8,128)S(1)}, u32[]{:S(2)}, u32[]{:S(2)}) collective-permute-start(f32[512,128]{1,0:T(8,128)S(1)} %bitcast.12), channel_id=1, source_target_pairs={{0,1},{1,0},{2,3},{3,2},{4,5},{5,4},{6,7},{7,6},{8,9},{9,8},{10,11... | collective-permute-start | bytes 786440 | tf_op jit(solution)/shard_map/ppermute | solution.py:577

commit v6 on v5

--- a/solution.py
+++ b/solution.py
@@ -497,15 +497,15 @@
 
 
 def scatter_half(part):
-    return lax.all_to_all(part.reshape(32, 16, HID), ("x", "zl", "zh"), 0, 0)
+    return lax.all_to_all(part.reshape(32, 16, HID), ("x", "y"), 0, 0)
 
 
 def every_term(terms):
-    return lax.all_to_all(sum_spread(terms, 8), "y", 0, 0)
+    return lax.all_to_all(sum_spread(terms, 8), ("zl", "zh"), 0, 0)
 
 
 def gather_half(terms):
-    part = lax.all_to_all(sum_spread(terms, 32), ("x", "zl", "zh"), 0, 0)
+    part = lax.all_to_all(sum_spread(terms, 32), ("x", "y"), 0, 0)
     return part.reshape(CELLS, HID)
 
 

time: 122 us -> 121 us (level)
  waiting for transfers between devices: 27.8 us -> 22.1 us
  starting transfers between devices: 71.2 us -> 76.1 us
    all_to_all x3, waiting for transfers between devices: 19.5 us -> 13.7 us  [the longest x1 7.82 us: gather_half(): part = lax.all_to_all(sum_spread(terms, 32), ('x', 'y'), 0, 0)]
    ppermute x5, starting transfers between devices: 19.7 us -> 22.2 us  [trade(): return (lax.ppermute(first, axis, near), second)]
    all_to_all x3, starting transfers between devices: 23 us -> 25 us  [the longest x1 14.7 us: scatter_half(): return lax.all_to_all(part.reshape(32, 16, HID), ('x', 'y'), 0, 0)]
where the time goes in v6:
time: 121 us; the launch traced here: 120 us
  starting transfers between devices  76.1 us (63%)
  waiting for transfers between devices  22.1 us (18%)
  Pallas kernels  19 us (16%)
  local copies, waits for them, and re-layouts  1.83 us (2%)
    ppermute x5, starting transfers between devices, trade(): return (lax.ppermute(first, axis, near), second)  22.2 us
    pallas_call x13, Pallas kernels, call(): pl.pallas_call(body, out_shape=shapes, in_specs=[SMEM] * len(smem) + [VME...  19 us
    all_to_all x1, starting transfers between devices, scatter_half(): return lax.all_to_all(part.reshape(32, 16, HID), ('x', 'y'), 0, 0)  14.7 us
    ppermute x5, starting transfers between devices, trade(): second = lax.ppermute(second, axis, far)  13.8 us
    all_to_all x1, waiting for transfers between devices, gather_half(): part = lax.all_to_all(sum_spread(terms, 32), ('x', 'y'), 0, 0)  7.82 us
    ppermute x1, starting transfers between devices, on_device(): second = lax.ppermute(back[2], GZ, swaps(GZ)[1])  7.08 us
    all_to_all x1, starting transfers between devices, gather_half(): part = lax.all_to_all(sum_spread(terms, 32), ('x', 'y'), 0, 0)  6.89 us
    ppermute x5, waiting for transfers between devices, trade(): return (lax.ppermute(first, axis, near), second)  6.36 us
  transfers between devices with their start and end apart: 16, of which 8 were waited for; matrix products, arithmetic and copies ran while one was open for 0% of the time, Pallas kernels for 5%

profile of v6, /device:TPU:1, one launch (start us, length us, event | category | flops | bytes accessed | tf_op | source)
XLA Modules:
  0.0 120.1 jit_solution(1268507052128023282)
XLA Ops:
  0.7 1.0 copy-done.3
  1.7 0.7 copy-done.9
  2.5 0.5 shard_map.231
  3.0 0.7 collective-permute-start
  3.7 8.2 %collective-permute-start.1 = (f32[288,128]{1,0:T(8,128)S(1)}, f32[288,128]{1,0:T(8,128)S(1)}, u32[]{:S(2)}, u32[]{:S(2)}) collective-permute-start(f32[288,128]{1,0:T(8,128)S(1)} %get-tuple-element.67), channel_id=1, source_target_pairs={{0,16},{16,0},{32,48},{48,32},{64,80},{80,64},{96,112},{112,96},{1... | collective-permute-start | bytes 442376 | tf_op jit(solution)/shard_map/ppermute | solution.py:488
  12.0 0.0 copy-start.1
  12.0 0.0 copy-start.2
  12.0 0.0 copy-start.15
  12.0 0.0 copy-start.16
  12.0 0.0 copy-start.17
  12.0 2.1 %shard_map.232 = (f32[2048,128]{1,0:T(8,128)S(1)}, f32[512,128]{1,0:T(8,128)S(1)}, s32[2048,128]{1,0:T(8,128)S(1)}, s32[2048,128]{1,0:T(8,128)S(1)}, s32[16,128]...) custom-call(f32[512,128]{1,0:T(8,128)S(1)} %copy-done.4, f32[2048,128]{1,0:T(8,128)S(1)} %copy-done, s32[16,128]{1,0:T(8,128)S(1)} %bitcast.14, ...), custom_call_target="tpu_custom_call" | custom-call | flops 3000000000 | bytes 7562240 | tf_op jit(solution)/shard_map/pallas_call | solution.py:386
  14.1 0.0 collective-permute-done.in2
  14.1 3.9 %collective-permute-done.1.in0 = f32[288,128]{1,0:T(8,128)S(1)} collective-permute-done((f32[288,128]{1,0:T(8,128)S(1)}, f32[288,128]{1,0:T(8,128)S(1)}, u32[]{:S(2)}, u32[]{:S(2)}) %collective-permute-start.1) | collective-permute-done | bytes 147488 | tf_op jit(solution)/shard_map/ppermute | solution.py:488
  18.1 3.1 %collective-permute-start.2 = (f32[288,128]{1,0:T(8,128)S(1)}, f32[288,128]{1,0:T(8,128)S(1)}, u32[]{:S(2)}, u32[]{:S(2)}) collective-permute-start(f32[288,128]{1,0:T(8,128)S(1)} %get-tuple-element.77), channel_id=1, source_target_pairs={{0,4},{4,0},{8,12},{12,8},{1,5},{5,1},{9,13},{13,9},{2,6},{6,2},{1... | collective-permute-start | bytes 442376 | tf_op jit(solution)/shard_map/ppermute | solution.py:488
  21.2 0.7 collective-permute-start.3
  21.8 2.1 %collective-permute-done.2.in0 = f32[288,128]{1,0:T(8,128)S(1)} collective-permute-done((f32[288,128]{1,0:T(8,128)S(1)}, f32[288,128]{1,0:T(8,128)S(1)}, u32[]{:S(2)}, u32[]{:S(2)}) %collective-permute-start.2) | collective-permute-done | bytes 147488 | tf_op jit(solution)/shard_map/ppermute | solution.py:488
  23.9 0.0 collective-permute-done.3.in2
  24.0 11.2 %collective-permute-start.4 = (f32[288,128]{1,0:T(8,128)S(1)}, f32[288,128]{1,0:T(8,128)S(1)}, u32[]{:S(2)}, u32[]{:S(2)}) collective-permute-start(f32[288,128]{1,0:T(8,128)S(1)} %get-tuple-element.80), channel_id=1, source_target_pairs={{1,2},{2,1},{5,6},{6,5},{9,10},{10,9},{13,14},{14,13},{17,18},{18,... | collective-permute-start | bytes 442376 | tf_op jit(solution)/shard_map/ppermute | solution.py:487
  35.1 2.1 %collective-permute-start.5 = (f32[288,128]{1,0:T(8,128)S(1)}, f32[288,128]{1,0:T(8,128)S(1)}, u32[]{:S(2)}, u32[]{:S(2)}) collective-permute-start(f32[288,128]{1,0:T(8,128)S(1)} %get-tuple-element.81), channel_id=1, source_target_pairs={{0,1},{1,0},{2,3},{3,2},{4,5},{5,4},{6,7},{7,6},{8,9},{9,8},{10,11... | collective-permute-start | bytes 442376 | tf_op jit(solution)/shard_map/ppermute | solution.py:488
  37.3 0.8 collective-permute-done.4.halo2_ref
  38.1 0.4 collective-permute-done.5.halo0_ref
  38.4 10.9 %shard_map.235 = (f32[288,128]{1,0:T(8,128)S(1)}, f32[288,128]{1,0:T(8,128)S(1)}, f32[288,128]{1,0:T(8,128)S(1)}, f32[512,128]{1,0:T(8,128)S(1)}, f32[512,128]{1...) custom-call(s32[16]{0:T(128)S(1)} %copy-done.15, ...), custom_call_target="tpu_custom_call" | custom-call | flops 10000000000 | bytes 11912192 | tf_op jit(solution)/shard_map/pallas_call | solution.py:386
  49.4 0.6 shard_map.236
  50.0 2.1 %collective-permute-start.6 = (f32[800,128]{1,0:T(8,128)S(1)}, f32[800,128]{1,0:T(8,128)S(1)}, u32[]{:S(2)}, u32[]{:S(2)}) collective-permute-start(f32[800,128]{1,0:T(8,128)S(1)} %get-tuple-element.99), channel_id=1, source_target_pairs={{0,1},{1,0},{2,3},{3,2},{4,5},{5,4},{6,7},{7,6},{8,9},{9,8},{10,11... | collective-permute-start | bytes 1228808 | tf_op jit(solution)/shard_map/ppermute | solution.py:560
  52.0 7.1 %collective-permute-start.7 = (f32[288,128]{1,0:T(8,128)S(1)}, f32[288,128]{1,0:T(8,128)S(1)}, u32[]{:S(2)}, u32[]{:S(2)}) collective-permute-start(f32[288,128]{1,0:T(8,128)S(1)} %get-tuple-element.93.back2_ref), channel_id=1, source_target_pairs={{1,2},{2,1},{5,6},{6,5},{9,10},{10,9},{13,14},{14,13},{17,18},{18,... | collective-permute-start | bytes 442376 | tf_op jit(solution)/shard_map/ppermute | solution.py:563
  59.1 0.0 collective-permute-done.6.taken_ref.in0
  59.1 0.7 shard_map.237
  59.9 14.7 %all-to-all-start = ((f32[32,16,128]{2,1,0:T(8,128)}), f32[32,16,128]{2,1,0:T(8,128)S(1)}, u32[]{:S(2)}, u32[]{:S(2)}) async-start(f32[32,16,128]{2,1,0:T(8,128)} %bitcast.6), calls=%async_computation | async-start | bytes 524288 | tf_op jit(solution)/shard_map/all_to_all | solution.py:500
  74.6 0.0 collective-permute-done.7.in2
  74.6 0.0 copy-start.10
  74.7 3.1 %collective-permute-start.8 = (f32[288,128]{1,0:T(8,128)S(1)}, f32[288,128]{1,0:T(8,128)S(1)}, u32[]{:S(2)}, u32[]{:S(2)}) collective-permute-start(f32[288,128]{1,0:T(8,128)S(1)} %get-tuple-element.102), channel_id=1, source_target_pairs={{0,4},{4,0},{8,12},{12,8},{1,5},{5,1},{9,13},{13,9},{2,6},{6,2},{1... | collective-permute-start | bytes 442376 | tf_op jit(solution)/shard_map/ppermute | solution.py:488
  77.8 0.7 collective-permute-start.9
  78.5 5.8 %all-to-all-done.terms_ref = f32[32,16,128]{2,1,0:T(8,128)S(1)} async-done(((f32[32,16,128]{2,1,0:T(8,128)}), f32[32,16,128]{2,1,0:T(8,128)S(1)}, u32[]{:S(2)}, u32[]{:S(2)}) %all-to-all-start) | async-done | bytes 262176 | tf_op jit(solution)/shard_map/all_to_all | solution.py:500
  84.3 0.7 shard_map.239
  85.0 3.4 %all-to-all-start.1 = ((f32[8,16,128]{2,1,0:T(8,128)}), f32[8,16,128]{2,1,0:T(8,128)S(1)}, u32[]{:S(2)}, u32[]{:S(2)}) async-start(f32[8,16,128]{2,1,0:T(8,128)} %shard_map.239), calls=%async_computation.1 | async-start | bytes 131072 | tf_op jit(solution)/shard_map/all_to_all | solution.py:504
  88.4 0.0 collective-permute-done.8.in0
  88.4 0.0 collective-permute-done.9.in2
  88.4 0.7 collective-permute-start.10
  89.1 5.7 %collective-permute-start.11 = (f32[288,128]{1,0:T(8,128)S(1)}, f32[288,128]{1,0:T(8,128)S(1)}, u32[]{:S(2)}, u32[]{:S(2)}) collective-permute-start(f32[288,128]{1,0:T(8,128)S(1)} %get-tuple-element.107), channel_id=1, source_target_pairs={{0,16},{16,0},{32,48},{48,32},{64,80},{80,64},{96,112},{112,96},{1... | collective-permute-start | bytes 442376 | tf_op jit(solution)/shard_map/ppermute | solution.py:488
  94.8 0.1 all-to-all-done.1.terms_ref
  94.9 0.7 shard_map.241
  95.6 6.9 %all-to-all-start.2 = ((f32[32,16,128]{2,1,0:T(8,128)}), f32[32,16,128]{2,1,0:T(8,128)S(1)}, u32[]{:S(2)}, u32[]{:S(2)}) async-start(f32[32,16,128]{2,1,0:T(8,128)} %shard_map.241), calls=%async_computation.2 | async-start | bytes 524288 | tf_op jit(solution)/shard_map/all_to_all | solution.py:508
  102.5 0.0 collective-permute-done.11.first_ref
  102.5 1.8 %shard_map.242 = f32[512,128]{1,0:T(8,128)} custom-call(s32[3,3,3,32]{3,2,1,0:T(4,128)S(1)} %copy-done.10, f32[288,128]{1,0:T(8,128)S(1)} %collective-permute-done.11.first_ref, f32[288,128]{1,0:T(8,128)S(1)} %get-tuple-element.104.mid_ref, f32[288,128]{1,0:T(8,128)S(1)} %collective-permute-done.10.second_ref, f32[512,128]{1,0:T(8,128)S(1)} %get-tuple-element.110.base_ref, ...), custom_call_target="tpu_custom_call" | custom-call | flops 5000000000 | bytes 1691008 | tf_op jit(solution)/shard_map/pallas_call | solution.py:386
  104.4 7.8 %all-to-all-done.2 = f32[32,16,128]{2,1,0:T(8,128)S(1)} async-done(((f32[32,16,128]{2,1,0:T(8,128)}), f32[32,16,128]{2,1,0:T(8,128)S(1)}, u32[]{:S(2)}, u32[]{:S(2)}) %all-to-all-start.2) | async-done | bytes 262176 | tf_op jit(solution)/shard_map/all_to_all | solution.py:508
  112.2 6.0 %collective-permute-start.12 = (f32[512,128]{1,0:T(8,128)S(1)}, f32[512,128]{1,0:T(8,128)S(1)}, u32[]{:S(2)}, u32[]{:S(2)}) collective-permute-start(f32[512,128]{1,0:T(8,128)S(1)} %bitcast.12), channel_id=1, source_target_pairs={{0,1},{1,0},{2,3},{3,2},{4,5},{5,4},{6,7},{7,6},{8,9},{9,8},{10,11... | collective-permute-start | bytes 786440 | tf_op jit(solution)/shard_map/ppermute | solution.py:577
  118.1 1.1 collective-permute-done.12.other_ref
  119.3 0.8 shard_map.243
  (33 shorter events, 0.2 us)
Async XLA Ops:
  0.6 11.2 %copy-start = (f32[2048,128]{1,0:T(8,128)S(1)}, f32[2048,128]{1,0:T(8,128)}, u32[]{:S(2)}) copy-start(f32[2048,128]{1,0:T(8,128)} %edge_ref.3) | copy-start | bytes 3145732
  0.7 1.0 copy-start.3
  1.7 0.7 copy-start.9
  2.4 9.5 %copy-start.4 = (f32[512,128]{1,0:T(8,128)S(1)}, f32[512,128]{1,0:T(8,128)}, u32[]{:S(2)}) copy-start(f32[512,128]{1,0:T(8,128)} %node_ref.7) | copy-start | bytes 786436
  2.4 9.5 %copy-start.5 = (f32[384,128]{1,0:T(8,128)S(1)}, f32[384,128]{1,0:T(8,128)}, u32[]{:S(2)}) copy-start(f32[384,128]{1,0:T(8,128)} %weight_ref.1) | copy-start | bytes 589828
  2.4 9.5 %copy-start.6 = (f32[256,128]{1,0:T(8,128)S(1)}, f32[256,128]{1,0:T(8,128)}, u32[]{:S(2)}) copy-start(f32[256,128]{1,0:T(8,128)} %nin_ref.1) | copy-start | bytes 393220
  2.4 9.5 %copy-start.7 = (f32[128,128]{1,0:T(8,128)S(1)}, f32[128,128]{1,0:T(8,128)}, u32[]{:S(2)}) copy-start(f32[128,128]{1,0:T(8,128)} %eout_ref.1) | copy-start | bytes 196612
  2.4 9.5 %copy-start.8 = (f32[128,128]{1,0:T(8,128)S(1)}, f32[128,128]{1,0:T(8,128)}, u32[]{:S(2)}) copy-start(f32[128,128]{1,0:T(8,128)} %nout_ref.1) | copy-start | bytes 196612
  2.4 9.5 %copy-start.11 = (s32[2048]{0:T(1024)S(1)}, s32[2048]{0:T(1024)}, u32[]{:S(2)}) copy-start(s32[2048]{0:T(1024)} %param.20) | copy-start | bytes 24580
  2.4 9.5 %copy-start.12 = (s32[2048]{0:T(1024)S(1)}, s32[2048]{0:T(1024)}, u32[]{:S(2)}) copy-start(s32[2048]{0:T(1024)} %param.21) | copy-start | bytes 24580
  2.5 9.5 %copy-start.13 = (f32[128]{0:T(128)S(1)}, f32[128]{0:T(128)}, u32[]{:S(2)}) copy-start(f32[128]{0:T(128)} %param.25) | copy-start | bytes 1540
  2.5 9.5 %copy-start.14 = (f32[128]{0:T(128)S(1)}, f32[128]{0:T(128)}, u32[]{:S(2)}) copy-start(f32[128]{0:T(128)} %param.29) | copy-start | bytes 1540
  3.0 11.1 %collective-permute-start = (f32[288,128]{1,0:T(8,128)S(1)}, f32[288,128]{1,0:T(8,128)S(1)}, u32[]{:S(2)}, u32[]{:S(2)}) collective-permute-start(f32[288,128]{1,0:T(8,128)S(1)} %get-tuple-element.66), channel_id=1, source_target_pairs={{16,32},{32,16},{48,64},{64,48},{80,96},{96,80},{112,128},{128,112... | collective-permute-start | bytes 442376 | tf_op jit(solution)/shard_map/ppermute | solution.py:487
  3.7 14.3 %collective-permute-start.1 = (f32[288,128]{1,0:T(8,128)S(1)}, f32[288,128]{1,0:T(8,128)S(1)}, u32[]{:S(2)}, u32[]{:S(2)}) collective-permute-start(f32[288,128]{1,0:T(8,128)S(1)} %get-tuple-element.67), channel_id=1, source_target_pairs={{0,16},{16,0},{32,48},{48,32},{64,80},{80,64},{96,112},{112,96},{1... | collective-permute-start | bytes 442376 | tf_op jit(solution)/shard_map/ppermute | solution.py:488
  12.0 26.4 %copy-start.1 = (f32[2048,128]{1,0:T(8,128)S(1)}, f32[2048,128]{1,0:T(8,128)}, u32[]{:S(2)}) copy-start(f32[2048,128]{1,0:T(8,128)} %cot_ref.1) | copy-start | bytes 3145732
  12.0 26.4 %copy-start.2 = (f32[512,128]{1,0:T(8,128)S(1)}, f32[512,128]{1,0:T(8,128)}, u32[]{:S(2)}) copy-start(f32[512,128]{1,0:T(8,128)} %node_cot_ref.1) | copy-start | bytes 786436
  12.0 26.4 %copy-start.15 = (s32[16]{0:T(128)S(1)}, s32[16]{0:T(128)}, u32[]{:S(2)}) copy-start(s32[16]{0:T(128)} %count_ref.1) | copy-start | bytes 196
  12.0 26.4 %copy-start.16 = (f32[128]{0:T(128)S(1)}, f32[128]{0:T(128)}, u32[]{:S(2)}) copy-start(f32[128]{0:T(128)} %param.27) | copy-start | bytes 1540
  12.0 26.4 %copy-start.17 = (f32[128]{0:T(128)S(1)}, f32[128]{0:T(128)}, u32[]{:S(2)}) copy-start(f32[128]{0:T(128)} %param.31) | copy-start | bytes 1540
  18.1 5.9 %collective-permute-start.2 = (f32[288,128]{1,0:T(8,128)S(1)}, f32[288,128]{1,0:T(8,128)S(1)}, u32[]{:S(2)}, u32[]{:S(2)}) collective-permute-start(f32[288,128]{1,0:T(8,128)S(1)} %get-tuple-element.77), channel_id=1, source_target_pairs={{0,4},{4,0},{8,12},{12,8},{1,5},{5,1},{9,13},{13,9},{2,6},{6,2},{1... | collective-permute-start | bytes 442376 | tf_op jit(solution)/shard_map/ppermute | solution.py:488
  21.2 2.8 %collective-permute-start.3 = (f32[288,128]{1,0:T(8,128)S(1)}, f32[288,128]{1,0:T(8,128)S(1)}, u32[]{:S(2)}, u32[]{:S(2)}) collective-permute-start(f32[288,128]{1,0:T(8,128)S(1)} %get-tuple-element.79), channel_id=1, source_target_pairs={{4,8},{8,4},{5,9},{9,5},{6,10},{10,6},{7,11},{11,7},{20,24},{24,20... | collective-permute-start | bytes 442376 | tf_op jit(solution)/shard_map/ppermute | solution.py:487
  24.0 14.1 %collective-permute-start.4 = (f32[288,128]{1,0:T(8,128)S(1)}, f32[288,128]{1,0:T(8,128)S(1)}, u32[]{:S(2)}, u32[]{:S(2)}) collective-permute-start(f32[288,128]{1,0:T(8,128)S(1)} %get-tuple-element.80), channel_id=1, source_target_pairs={{1,2},{2,1},{5,6},{6,5},{9,10},{10,9},{13,14},{14,13},{17,18},{18,... | collective-permute-start | bytes 442376 | tf_op jit(solution)/shard_map/ppermute | solution.py:487
  35.1 3.3 %collective-permute-start.5 = (f32[288,128]{1,0:T(8,128)S(1)}, f32[288,128]{1,0:T(8,128)S(1)}, u32[]{:S(2)}, u32[]{:S(2)}) collective-permute-start(f32[288,128]{1,0:T(8,128)S(1)} %get-tuple-element.81), channel_id=1, source_target_pairs={{0,1},{1,0},{2,3},{3,2},{4,5},{5,4},{6,7},{7,6},{8,9},{9,8},{10,11... | collective-permute-start | bytes 442376 | tf_op jit(solution)/shard_map/ppermute | solution.py:488
  50.0 9.1 %collective-permute-start.6 = (f32[800,128]{1,0:T(8,128)S(1)}, f32[800,128]{1,0:T(8,128)S(1)}, u32[]{:S(2)}, u32[]{:S(2)}) collective-permute-start(f32[800,128]{1,0:T(8,128)S(1)} %get-tuple-element.99), channel_id=1, source_target_pairs={{0,1},{1,0},{2,3},{3,2},{4,5},{5,4},{6,7},{7,6},{8,9},{9,8},{10,11... | collective-permute-start | bytes 1228808 | tf_op jit(solution)/shard_map/ppermute | solution.py:560
  52.0 22.6 %collective-permute-start.7 = (f32[288,128]{1,0:T(8,128)S(1)}, f32[288,128]{1,0:T(8,128)S(1)}, u32[]{:S(2)}, u32[]{:S(2)}) collective-permute-start(f32[288,128]{1,0:T(8,128)S(1)} %get-tuple-element.93.back2_ref), channel_id=1, source_target_pairs={{1,2},{2,1},{5,6},{6,5},{9,10},{10,9},{13,14},{14,13},{17,18},{18,... | collective-permute-start | bytes 442376 | tf_op jit(solution)/shard_map/ppermute | solution.py:563
  59.9 24.5 %all-to-all-start = ((f32[32,16,128]{2,1,0:T(8,128)}), f32[32,16,128]{2,1,0:T(8,128)S(1)}, u32[]{:S(2)}, u32[]{:S(2)}) async-start(f32[32,16,128]{2,1,0:T(8,128)} %bitcast.6), calls=%async_computation | async-start | bytes 524288 | tf_op jit(solution)/shard_map/all_to_all | solution.py:500
  74.6 27.9 %copy-start.10 = (s32[3,3,3,32]{3,2,1,0:T(4,128)S(1)}, s32[3,3,3,32]{3,2,1,0:T(4,128)}, u32[]{:S(2)}) copy-start(s32[3,3,3,32]{3,2,1,0:T(4,128)} %lists_ref.3) | copy-start | bytes 10372
  74.7 13.7 %collective-permute-start.8 = (f32[288,128]{1,0:T(8,128)S(1)}, f32[288,128]{1,0:T(8,128)S(1)}, u32[]{:S(2)}, u32[]{:S(2)}) collective-permute-start(f32[288,128]{1,0:T(8,128)S(1)} %get-tuple-element.102), channel_id=1, source_target_pairs={{0,4},{4,0},{8,12},{12,8},{1,5},{5,1},{9,13},{13,9},{2,6},{6,2},{1... | collective-permute-start | bytes 442376 | tf_op jit(solution)/shard_map/ppermute | solution.py:488
  77.8 10.6 %collective-permute-start.9 = (f32[288,128]{1,0:T(8,128)S(1)}, f32[288,128]{1,0:T(8,128)S(1)}, u32[]{:S(2)}, u32[]{:S(2)}) collective-permute-start(f32[288,128]{1,0:T(8,128)S(1)} %get-tuple-element.103), channel_id=1, source_target_pairs={{4,8},{8,4},{5,9},{9,5},{6,10},{10,6},{7,11},{11,7},{20,24},{24,20... | collective-permute-start | bytes 442376 | tf_op jit(solution)/shard_map/ppermute | solution.py:487
  85.0 9.9 %all-to-all-start.1 = ((f32[8,16,128]{2,1,0:T(8,128)}), f32[8,16,128]{2,1,0:T(8,128)S(1)}, u32[]{:S(2)}, u32[]{:S(2)}) async-start(f32[8,16,128]{2,1,0:T(8,128)} %shard_map.239), calls=%async_computation.1 | async-start | bytes 131072 | tf_op jit(solution)/shard_map/all_to_all | solution.py:504
  88.4 14.1 %collective-permute-start.10 = (f32[288,128]{1,0:T(8,128)S(1)}, f32[288,128]{1,0:T(8,128)S(1)}, u32[]{:S(2)}, u32[]{:S(2)}) collective-permute-start(f32[288,128]{1,0:T(8,128)S(1)} %get-tuple-element.106), channel_id=1, source_target_pairs={{16,32},{32,16},{48,64},{64,48},{80,96},{96,80},{112,128},{128,112... | collective-permute-start | bytes 442376 | tf_op jit(solution)/shard_map/ppermute | solution.py:487
  89.1 13.4 %collective-permute-start.11 = (f32[288,128]{1,0:T(8,128)S(1)}, f32[288,128]{1,0:T(8,128)S(1)}, u32[]{:S(2)}, u32[]{:S(2)}) collective-permute-start(f32[288,128]{1,0:T(8,128)S(1)} %get-tuple-element.107), channel_id=1, source_target_pairs={{0,16},{16,0},{32,48},{48,32},{64,80},{80,64},{96,112},{112,96},{1... | collective-permute-start | bytes 442376 | tf_op jit(solution)/shard_map/ppermute | solution.py:488
  95.6 16.6 %all-to-all-start.2 = ((f32[32,16,128]{2,1,0:T(8,128)}), f32[32,16,128]{2,1,0:T(8,128)S(1)}, u32[]{:S(2)}, u32[]{:S(2)}) async-start(f32[32,16,128]{2,1,0:T(8,128)} %shard_map.241), calls=%async_computation.2 | async-start | bytes 524288 | tf_op jit(solution)/shard_map/all_to_all | solution.py:508
  112.2 7.1 %collective-permute-start.12 = (f32[512,128]{1,0:T(8,128)S(1)}, f32[512,128]{1,0:T(8,128)S(1)}, u32[]{:S(2)}, u32[]{:S(2)}) collective-permute-start(f32[512,128]{1,0:T(8,128)S(1)} %bitcast.12), channel_id=1, source_target_pairs={{0,1},{1,0},{2,3},{3,2},{4,5},{5,4},{6,7},{7,6},{8,9},{9,8},{10,11... | collective-permute-start | bytes 786440 | tf_op jit(solution)/shard_map/ppermute | solution.py:577
